TPU v7x, 32 devices: a whole 2x2x4 slice. The times are simulated.
32 devices in a mesh: seg: 8 (over z, y), blk: 4 (over x, core).
Axes of the slice: x: 2, y: 2, z: 4, core: 2. Of those that a mesh axis runs over, the one named last changes fastest.
Arguments:
- queries: float32 [4096, 1024], P(('seg', 'blk')), may hold values from -5 to 5
- keys: float32 [4096, 256], P(('seg', 'blk')), may hold values from -5 to 5
- values: float32 [4096, 256], P(('seg', 'blk')), may hold values from -6 to 6
- gate_logit: float32 [8], replicated, may hold values from -3 to 3
- memory_gain: float32 [1024], replicated, may hold values from 0.5 to 2
Outputs:
- mixed: float32 [4096, 1024], P(('seg', 'blk'))
All inputs are finite; a program needn't handle non-finite values.
Results may differ from a plain program's by a relative error of at most 0.0003.
Values sent between devices are 32-bit elements; how exact they have to be, the bound alone decides.
No kernel may reach another device: no remote copies, remote signals or barrier semaphores. Data moves between devices by JAX's collectives and lax.ppermute only.
A program may use at most 64 MiB of HBM per device.

v0:
```python
import jax
import jax.numpy as jnp
from jax import lax
from jax.sharding import PartitionSpec as P

QH = 8
KVH = 2
GROUP = 4
HD = 128


HIGH = lax.Precision.HIGHEST


def prefix_2(part, axis, combine, identity):
    place = lax.axis_index(axis)
    gathered = lax.all_gather(part, axis)
    state = jnp.zeros_like(part) + jnp.asarray(identity, part.dtype)

    def one(lap, state):
        return combine(state, lax.dynamic_index_in_dim(gathered, lap, 0, False))

    return lax.fori_loop(0, place, one, state)


def sigma_map(x):
    return jnp.where(x > 0, x + 1.0, jnp.exp(jnp.minimum(x, 0.0)))


def add_terms(earlier, later):
    return earlier + later


def on_device(queries, keys, values, gate_logit, memory_gain):
    rows = queries.shape[0]
    index = lax.axis_index("blk")
    q_heads = queries.reshape(rows, KVH, GROUP, HD)
    qpos = index * rows + jnp.arange(rows, dtype=jnp.int32)
    scale = 1.0 / jnp.sqrt(jnp.float32(HD))

    def update(carry, pieces):
        top, total, accum = carry
        k_piece, v_piece = pieces
        count = k_piece.shape[0]
        k_h = k_piece.reshape(count, KVH, HD)
        v_h = v_piece.reshape(count, KVH, HD)
        scores = jnp.einsum("rkgd,nkd->kgrn", q_heads, k_h, precision=HIGH) * scale
        kpos = jnp.arange(count, dtype=jnp.int32)
        allowed = (kpos[None, :] <= qpos[:, None])[None, None]
        row_top = jnp.max(jnp.where(allowed, scores, -1e30), axis=-1)
        new_top = jnp.maximum(top, row_top)
        weights = jnp.where(allowed, jnp.exp(scores - new_top[..., None]), 0.0)
        total = jnp.sum(weights, axis=-1)
        accum = jnp.einsum("kgrn,nkd->kgrd", weights, v_h, precision=HIGH)
        return (new_top, total, accum)

    start_state = (
        jnp.full((KVH, GROUP, rows), -1e30, jnp.float32),
        jnp.zeros((KVH, GROUP, rows), jnp.float32),
        jnp.zeros((KVH, GROUP, rows, HD), jnp.float32),
    )
    pieces = (
        lax.all_gather(keys, "blk", axis=0, tiled=True),
        lax.all_gather(values, "blk", axis=0, tiled=True),
    )
    top, total, accum = lax.cond(
        jnp.int32(0) <= qpos[rows - 1], lambda c: update(c, pieces), lambda c: c, start_state
    )
    attention = accum / total[..., None]
    sig_keys = sigma_map(keys.reshape(rows, KVH, HD))
    partial_value = jnp.einsum(
        "rkd,rke->kde", sig_keys, values.reshape(rows, KVH, HD), precision=HIGH
    ).reshape(KVH * HD, HD)
    shard = lax.psum_scatter(partial_value, "blk", scatter_dimension=0, tiled=True)
    prefix = prefix_2(shard, "seg", add_terms, jnp.zeros_like(shard))
    memory = lax.all_gather(prefix, "blk", axis=0, tiled=True)
    retrieval = jnp.einsum(
        "rkgd,kde->kgre", sigma_map(q_heads), memory.reshape(KVH, HD, HD), precision=HIGH
    )
    rms = jnp.sqrt(jnp.mean(retrieval * retrieval, axis=-1, keepdims=True) + 1e-06)
    normed = retrieval / rms * memory_gain.reshape(KVH, GROUP, 1, HD)
    gate = jax.nn.sigmoid(gate_logit).reshape(KVH, GROUP, 1, 1)
    mixed = gate * normed + (1.0 - gate) * attention
    return jnp.transpose(mixed, (2, 0, 1, 3)).reshape(rows, QH * HD)


def solution(mesh):
    return jax.shard_map(
        on_device,
        mesh=mesh,
        in_specs=(
            P(("seg", "blk"), None),
            P(("seg", "blk"), None),
            P(("seg", "blk"), None),
            P(),
            P(),
        ),
        out_specs=P(("seg", "blk"), None),
        check_vma=False,
    )
```

profile of v0, /device:TPU:0, one launch (start us, length us, event | category | flops | bytes accessed | tf_op | source)
XLA Modules:
  0.0 82.2 jit_solution(3702383600021202158)
XLA Ops:
  6.5 0.0 reduce-scatter.2.cloned.1.call-start
  6.5 1.0 %exponential_select_fusion = f32[128,256]{1,0:T(8,128)S(1)} fusion(f32[128,256]{1,0:T(8,128)} %param.10), kind=kLoop, calls=%fused_computation.32 | loop fusion | flops 131072 | bytes 262144 | tf_op jit(solution)/shard_map/jit(_where)/select_n | solution.py:27
  7.5 0.1 copy.34
  7.6 1.8 %fusion.22 = f32[2,128,128]{2,1,0:T(8,128)} fusion(f32[128,2,128]{0,2,1:T(8,128)S(1)} %bitcast.51, f32[128,256]{1,0:T(8,128)} %param.11), kind=kOutput, calls=%fused_computation.29 | convolution fusion | flops 50331648 | bytes 393216 | tf_op jit(solution)/shard_map/rkd,rke->kde/dot_general | solution.py:71
  9.5 0.0 reduce-scatter.2.cloned.1.call-update
  9.5 8.8 %all_gather.18 = f32[512,256]{1,0:T(8,128)S(1)} all-gather(f32[128,256]{1,0:T(8,128)} %param.10), channel_id=1, replica_groups=mesh['seg'=8,'blk'=4] {'blk'}, dimensions={0}, use_global_device_ids=true | all-gather | bytes 655360 | tf_op jit(solution)/shard_map/all_gather | solution.py:63
  18.3 8.8 %all_gather.19 = f32[512,256]{1,0:T(8,128)} all-gather(f32[128,256]{1,0:T(8,128)} %param.11), channel_id=1, replica_groups=mesh['seg'=8,'blk'=4] {'blk'}, dimensions={0}, use_global_device_ids=true | all-gather | bytes 655360 | tf_op jit(solution)/shard_map/all_gather | solution.py:64
  27.2 0.0 copy-done.2
  27.2 0.2 copy.18
  27.4 0.6 slice.3
  28.6 0.1 mul.40
  28.7 6.7 %conditional.1 = (f32[2,4,128]{2,1,0:T(4,128)S(1)}, f32[2,4,128,128]{2,3,1,0:T(8,128)}) conditional(s32[]{:T(128)} %bitcast.12, () %tuple.18, (s32[128]{0:T(128)S(1)}, f32[512,256]{1,0:T(8,128)S(1)}, f32[128,2,4,128]{0,3,2,1:T(8,128)S(1)}, f32[512,256]{1,0:T(8,128)}) %tuple.40), branch_computations={%region_4.5_spmd, %region_5.8_spmd} | conditional | flops 1615920128 | bytes 10773008 | solution.py:66
  28.8 0.3 reshape.68
  29.0 2.0 %fusion = (f32[2,4,128]{2,1,0:T(4,128)S(1)}, f32[2,512,128,4]{2,1,3,0:T(8,128)S(1)}) fusion(pred[128,512]{0,1:T(8,128)(4,1)S(1)} %iota_compare_fusion, f32[128,2,4,128]{0,3,2,1:T(8,128)S(1)} %get-tuple-element.47, f32[512,2,128,1]{2,1,0,3:T(2,128)S(1)} %bitcast.46), kind=kOutput, calls=%fused_computation.3 | convolution fusion | flops 806878208 | bytes 3215360 | tf_op jit(solution)/shard_map/cond/branch_1_fun/rkgd,nkd->kgrn/dot_general | solution.py:47
  31.0 1.3 %reshape.69 = f32[512,2,128]{2,1,0:T(2,128)S(1)} reshape(f32[512,256]{1,0:T(8,128)} %get-tuple-element.38) | data formatting | bytes 1048576 | tf_op jit(solution)/shard_map/cond/branch_1_fun/reshape | solution.py:46
  32.3 2.6 %fusion.3 = f32[2,4,128,128]{2,3,1,0:T(8,128)} fusion(f32[2,512,128,4]{2,1,3,0:T(8,128)S(1)} %get-tuple-element.59, f32[2,4,128]{2,1,0:T(4,128)S(1)} %broadcast_maximum_fusion, pred[128,512]{0,1:T(8,128)(4,1)S(1)} %iota_compare_fusion, f32[512,2,128,1]{2,1,0,3:T(2,128)S(1)} %bitcast.52), kind=kOutput, calls=%fused_computation.6 | convolution fusion | flops 806879232 | bytes 3215360 | tf_op jit(solution)/shard_map/cond | solution.py:66
  34.9 0.4 fusion.5
  35.4 0.0 copy-start.1
  35.4 0.0 reduce-scatter.2.cloned.1.call-done
  35.4 31.5 %all-gather = f32[512,128]{1,0:T(8,128)S(1)} all-gather(f32[64,128]{1,0:T(8,128)} %reduce-scatter.2.cloned.1.call-done), channel_id=2, replica_groups=mesh['seg'=8,'blk'=4] {'seg'}, dimensions={0}, use_global_device_ids=true | all-gather | bytes 294912 | tf_op jit(solution)/shard_map/all_gather | solution.py:17
  66.9 5.4 %all_gather.17 = f32[256,128]{1,0:T(8,128)S(1)} all-gather(f32[64,128]{1,0:T(8,128)S(1)} %get-tuple-element.42), channel_id=1, replica_groups=mesh['seg'=8,'blk'=4] {'blk'}, dimensions={0}, use_global_device_ids=true | all-gather | bytes 163840 | tf_op jit(solution)/shard_map/all_gather | solution.py:76
  72.3 0.7 multiply_reduce_fusion
  73.0 1.3 %multiply_add_fusion = f32[2,4,128,128]{2,3,1,0:T(8,128)S(1)} fusion(f32[2,4,128,128]{2,3,1,0:T(8,128)} %get-tuple-element.49, f32[2,4,128,128]{2,3,1,0:T(8,128)S(1)} %get-tuple-element.61, f32[2,4,128]{2,1,0:T(4,128)S(1)} %get-tuple-element.44, f32[2,4]{1,0:T(2,128)S(1)} %broadcast_subtract_fusion, f32[2,4,128]{2,1,0:T(4,128)S(1)} %bitcast.53, ...), kind=kLoop, calls=%fused_computation.20 | loop fusion | flops 786432 | bytes 1585216 | tf_op jit(solution)/shard_map/add | solution.py:83
  74.3 1.0 %copy.23 = f32[128,1024]{1,0:T(8,128)} copy(f32[128,1024]{0,1:T(8,128)S(1)} %bitcast.47) | data formatting | bytes 1048576 | tf_op jit(solution)/shard_map/reshape | solution.py:84
  (12 shorter events, 0.1 us)
Async XLA Ops:
  6.5 20.6 %copy-start.2 = (f32[8]{0:T(128)S(1)}, f32[8]{0:T(128)}, u32[]{:S(2)}) copy-start(f32[8]{0:T(128)} %param.12) | copy-start | bytes 100
  6.5 20.6 %copy-start = (f32[128,1024]{1,0:T(8,128)S(1)}, f32[128,1024]{1,0:T(8,128)}, u32[]{:S(2)}) copy-start(f32[128,1024]{1,0:T(8,128)} %param.9) | copy-start | bytes 1572868
  6.5 28.9 %reduce-scatter.2.cloned.1.call-start = ((), (), s32[]{:S(2)}) async-start(), calls=%async_computation.1 | async-start | bytes 163840 | tf_op jit(solution)/shard_map/reduce_scatter | solution.py:74
  35.4 37.7 %copy-start.1 = (f32[1024]{0:T(1024)S(1)}, f32[1024]{0:T(1024)}, u32[]{:S(2)}) copy-start(f32[1024]{0:T(1024)} %param.13) | copy-start | bytes 12292
Sparse Core Ops, SparseCore 0:
  9.8 22.2 reduce-scatter.1
where the time goes:
time: 82.5 us; the launch traced here: 82.2 us
  blocking collectives  54.6 us (66%)
  between operations  14.1 us (17%)
  matrix products  7.09 us (9%)
  local copies, waits for them, and re-layouts  3.53 us (4%)
  other arithmetic  2.79 us (3%)
    all_gather x1, blocking collectives, prefix_2(): gathered = lax.all_gather(part, axis)  31.5 us
    all_gather x1, blocking collectives, on_device(): lax.all_gather(values, 'blk', axis=0, tiled=True)  8.84 us
    all_gather x1, blocking collectives, on_device(): lax.all_gather(keys, 'blk', axis=0, tiled=True)  8.83 us
    all_gather x1, blocking collectives, on_device(): memory = lax.all_gather(prefix, 'blk', axis=0, tiled=True)  5.42 us
    cond x1, matrix products, on_device(): lax.cond(jnp.int32(0) <= qpos[rows - 1], lambda c: update(c, pieces), lam...  2.61 us
    dot_general x1, matrix products, update(): scores = jnp.einsum('rkgd,nkd->kgrn', q_heads, k_h, precision=HIGH) * scale  1.96 us
    dot_general x1, matrix products, on_device(): jnp.einsum('rkd,rke->kde', sig_keys, values.reshape(rows, KVH, HD), preci...  1.83 us
  transfers between devices with their start and end apart: 1, of which 0 were waited for; matrix products, arithmetic and copies ran while one was open for 9% of the time, Pallas kernels for 0%

commit v1 on v0

v1 whole, which is shorter than its diff:
```python
import jax
import jax.numpy as jnp
from jax import lax
from jax.experimental import pallas as pl
from jax.experimental.pallas import tpu as pltpu
from jax.sharding import PartitionSpec as P

HD = 128
EPS = 1e-6
NEG = -1e30


def sigma_map(x):
    return jnp.where(x > 0, x + 1.0, jnp.exp(jnp.minimum(x, 0.0)))


def split(x):
    high = x.astype(jnp.bfloat16)
    low = (x - high.astype(jnp.float32)).astype(jnp.bfloat16)
    return high, low


def dot(a, b, dims):
    return lax.dot_general(a, b, (dims, ((), ())), preferred_element_type=jnp.float32)


def partial_kernel(k_ref, v_ref, kc_ref, vc_ref, p_ref):
    head = lax.axis_index("blk") & 1
    cols = pl.ds(pl.multiple_of(head * HD, HD), HD)
    s_hi, s_lo = split(sigma_map(jnp.concatenate([k_ref[:, cols], kc_ref[:, cols]], 0)))
    v_hi, v_lo = split(jnp.concatenate([v_ref[:, cols], vc_ref[:, cols]], 0))
    left = jnp.concatenate([s_hi, s_lo, s_hi], 0)
    right = jnp.concatenate([v_hi, v_hi, v_lo], 0)
    p_ref[...] = dot(left, right, ((0,), (0,)))


def attention_kernel(group, chunks, *refs):
    q_ref = refs[0]
    k_refs = refs[1 : 1 + chunks]
    v_refs = refs[1 + chunks : 1 + 2 * chunks]
    gate_ref, gain_ref = refs[1 + 2 * chunks : 3 + 2 * chunks]
    att_ref, sh_ref, sl_ref, mult_ref = refs[3 + 2 * chunks :]
    rows = q_ref.shape[0]
    kv_heads = k_refs[0].shape[1] // HD
    place = lax.axis_index("blk")
    gates = 1.0 / (1.0 + jnp.exp(-gate_ref[...]))
    causal = lax.broadcasted_iota(jnp.int32, (rows, rows), 1) <= lax.broadcasted_iota(
        jnp.int32, (rows, rows), 0
    )
    causal = jnp.concatenate([causal] * group, 0)
    scale = 1.0 / jnp.sqrt(jnp.float32(HD))
    for head in range(kv_heads):
        kv = slice(head * HD, (head + 1) * HD)
        spans = [
            slice((head * group + g) * HD, (head * group + g + 1) * HD) for g in range(group)
        ]
        q = jnp.concatenate([q_ref[:, s] for s in spans], 0)
        f_hi, f_lo = split(sigma_map(q))
        for g, s in enumerate(spans):
            sh_ref[:, s] = f_hi[g * rows : (g + 1) * rows]
            sl_ref[:, s] = f_lo[g * rows : (g + 1) * rows]
        q_hi, q_lo = split(q * scale)
        left = jnp.concatenate([q_hi, q_lo], 1)
        scores = []
        for m in range(chunks):
            k_hi, k_lo = split(k_refs[m][:, kv])
            piece = dot(left, jnp.concatenate([k_hi, k_hi], 1), ((1,), (1,)))
            piece = piece + dot(q_hi, k_lo, ((1,), (1,)))
            if m == 0:
                piece = jnp.where(causal, piece, NEG)
            else:
                piece = jnp.where((place ^ m) < place, piece, NEG)
            scores.append(piece)
        top = scores[0]
        for piece in scores[1:]:
            top = jnp.maximum(top, piece)
        top = jnp.max(top, axis=1, keepdims=True)
        accum = None
        summed = None
        for m in range(chunks):
            w = jnp.exp(scores[m] - top)
            v_hi, v_lo = split(v_refs[m][:, kv])
            w_hi, w_lo = split(w)
            both = dot(w_hi, jnp.concatenate([v_hi, v_lo], 1), ((1,), (0,)))
            part = both[:, :HD] + both[:, HD:] + dot(w_lo, v_hi, ((1,), (0,)))
            accum = part if accum is None else accum + part
            summed = w if summed is None else summed + w
        att = accum / jnp.sum(summed, axis=1, keepdims=True)
        for g, s in enumerate(spans):
            h = head * group + g
            gate = gates[:, h : h + 1]
            att_ref[:, s] = (1.0 - gate) * att[g * rows : (g + 1) * rows]
            mult_ref[:, s] = gate * gain_ref[:, s]


def final_kernel(group, att_ref, sh_ref, sl_ref, mult_ref, mine_ref, other_ref, out_ref):
    rows = att_ref.shape[0]
    kv_heads = att_ref.shape[1] // (group * HD)
    own = lax.axis_index("blk") & 1
    for head in range(kv_heads):
        memory = jnp.where(own == head, mine_ref[...], other_ref[...])
        m_hi, m_lo = split(memory)
        right = jnp.concatenate([m_hi, m_hi], 0)
        spans = [
            slice((head * group + g) * HD, (head * group + g + 1) * HD) for g in range(group)
        ]
        f_hi = jnp.concatenate([sh_ref[:, s] for s in spans], 0)
        f_lo = jnp.concatenate([sl_ref[:, s] for s in spans], 0)
        r = dot(jnp.concatenate([f_hi, f_lo], 1), right, ((1,), (0,)))
        r = r + dot(f_hi, m_lo, ((1,), (0,)))
        inv = lax.rsqrt(jnp.mean(r * r, axis=1, keepdims=True) + EPS)
        r = r * inv
        for g, s in enumerate(spans):
            out_ref[:, s] = att_ref[:, s] + r[g * rows : (g + 1) * rows] * mult_ref[:, s]


def solution(mesh):
    n_seg, n_blk = mesh.shape["seg"], mesh.shape["blk"]
    both = ("seg", "blk")

    def swap(x, seg_bits, blk_bits):
        pairs = [
            (s * n_blk + b, (s ^ seg_bits) * n_blk + (b ^ blk_bits))
            for s in range(n_seg)
            for b in range(n_blk)
        ]
        return lax.ppermute(x, both, pairs)

    bits = [(1 << i, 0) for i in reversed(range(n_seg.bit_length() - 1))]
    bits += [(0, 1 << i) for i in reversed(range(1, n_blk.bit_length() - 1))]
    stages = [bits[i : i + 2] for i in range(0, len(bits), 2)]

    def on_device(queries, keys, values, gate_logit, memory_gain):
        rows, width = queries.shape
        kv_width = keys.shape[1]
        group = width // kv_width
        seg = lax.axis_index("seg")

        k_held, v_held = [keys], [values]
        k_held.append(swap(keys, 0, 1))
        v_held.append(swap(values, 0, 1))
        part = pl.pallas_call(
            partial_kernel, out_shape=jax.ShapeDtypeStruct((HD, HD), jnp.float32)
        )(k_held[0], v_held[0], k_held[1], v_held[1])

        step = 2
        while step < n_blk:
            fresh_k = [swap(k_held[m], 0, step) for m in range(0, step, 2)]
            fresh_v = [swap(v_held[m], 0, step) for m in range(0, step, 2)]
            for k_new, v_new in zip(fresh_k, fresh_v, strict=True):
                k_held += [k_new, swap(k_new, 0, 1)]
                v_held += [v_new, swap(v_new, 0, 1)]
            step *= 2

        carried = None
        for stage in stages:
            masks = [(0, 0)]
            for s, b in stage:
                masks += [(s ^ p, b ^ q) for p, q in masks]
            total = carried
            for s, b in masks[1:]:
                if s:
                    sent = part if carried is None else carried + jnp.where((seg ^ s) > seg, part, 0.0)
                else:
                    sent = carried if carried is not None else jnp.zeros_like(part)
                got = swap(sent, s, b)
                if carried is None:
                    got = jnp.where((seg ^ s) < seg, got, 0.0)
                total = got if total is None else total + got
            carried = total
        mine = carried
        other = swap(mine, 0, 1)

        att, f_hi, f_lo, mult = pl.pallas_call(
            lambda *refs: attention_kernel(group, n_blk, *refs),
            out_shape=(
                jax.ShapeDtypeStruct((rows, width), jnp.float32),
                jax.ShapeDtypeStruct((rows, width), jnp.bfloat16),
                jax.ShapeDtypeStruct((rows, width), jnp.bfloat16),
                jax.ShapeDtypeStruct((1, width), jnp.float32),
            ),
            compiler_params=pltpu.CompilerParams(vmem_limit_bytes=48 * 1024 * 1024),
        )(
            queries,
            *k_held,
            *v_held,
            gate_logit.reshape(1, -1),
            memory_gain.reshape(1, -1),
        )
        return pl.pallas_call(
            lambda *refs: final_kernel(group, *refs),
            out_shape=jax.ShapeDtypeStruct((rows, width), jnp.float32),
            compiler_params=pltpu.CompilerParams(vmem_limit_bytes=48 * 1024 * 1024),
        )(att, f_hi, f_lo, mult, mine, other)

    return jax.shard_map(
        on_device,
        mesh=mesh,
        in_specs=(P(both, None), P(both, None), P(both, None), P(), P()),
        out_specs=P(both, None),
        check_vma=False,
    )
```

time: 82.5 us -> 28.9 us (0.35)
  blocking collectives: 54.6 us -> 0 us
  between operations: 14.1 us -> 0.09 us
  starting transfers between devices: 0.01 us -> 12.2 us
  waiting for transfers between devices: 0.04 us -> 7.38 us
  matrix products: 7.09 us -> 0 us
  Pallas kernels: 0 us -> 5.6 us
  other arithmetic: 2.79 us -> 0.88 us
  local copies, waits for them, and re-layouts: 3.53 us -> 2.49 us
    all_gather x4 -> x0, blocking collectives: 54.6 us -> none  [the longest x1 31.5 us: prefix_2(): gathered = lax.all_gather(part, axis)]
    ppermute x0 -> x13, starting transfers between devices: none -> 12.2 us  [swap(): return lax.ppermute(x, both, pairs)]
    ppermute x0 -> x13, waiting for transfers between devices: none -> 7.38 us  [swap(): return lax.ppermute(x, both, pairs)]
    pallas_call x0 -> x3, Pallas kernels: none -> 5.6 us  [the longest x1 2.36 us: on_device(): pl.pallas_call(lambda *refs: attention_kernel(group, n_blk, *refs), out_s...]
    dot_general x3 -> x0, matrix products: 4.48 us -> none  [the longest x1 1.96 us: update(): scores = jnp.einsum('rkgd,nkd->kgrn', q_heads, k_h, precision=HIGH) * scale]
    cond x1 -> x0, matrix products: 2.61 us -> none  [on_device(): lax.cond(jnp.int32(0) <= qpos[rows - 1], lambda c: update(c, pieces), lam...]
    reshape x3 -> x0, local copies, waits for them, and re-layouts: 2.57 us -> none  [the longest x1 1.3 us: update(): v_h = v_piece.reshape(count, KVH, HD)]
    unnamed x7 -> x18, local copies, waits for them, and re-layouts: 0.2 us -> 2.49 us
  transfers between devices with their start and end apart: 1 -> 13, of which waited for: 0 -> 8; matrix products, arithmetic and copies ran while one was open for 9% -> 3% of each run, Pallas kernels for 0% -> 8%
where the time goes in v1:
time: 28.9 us; the launch traced here: 28.6 us
  starting transfers between devices  12.2 us (42%)
  waiting for transfers between devices  7.38 us (26%)
  Pallas kernels  5.6 us (19%)
  local copies, waits for them, and re-layouts  2.49 us (9%)
  other arithmetic  0.88 us (3%)
    ppermute x13, starting transfers between devices, swap(): return lax.ppermute(x, both, pairs)  12.2 us
    ppermute x13, waiting for transfers between devices, swap(): return lax.ppermute(x, both, pairs)  7.38 us
    unnamed x18, local copies, waits for them, and re-layouts  2.49 us
    pallas_call x1, Pallas kernels, on_device(): pl.pallas_call(lambda *refs: attention_kernel(group, n_blk, *refs), out_s...  2.36 us
    pallas_call x1, Pallas kernels, on_device(): pl.pallas_call(partial_kernel, out_shape=jax.ShapeDtypeStruct((HD, HD), j...  1.98 us
    pallas_call x1, Pallas kernels, on_device(): pl.pallas_call(lambda *refs: final_kernel(group, *refs), out_shape=jax.Sh...  1.26 us
    add x1, other arithmetic, on_device(): carried + jnp.where(seg ^ s > seg, part, 0.0)  0.86 us
  transfers between devices with their start and end apart: 13, of which 8 were waited for; matrix products, arithmetic and copies ran while one was open for 3% of the time, Pallas kernels for 8%

profile of v1, /device:TPU:0, one launch (start us, length us, event | category | flops | bytes accessed | tf_op | source)
XLA Modules:
  0.0 28.6 jit_solution(16581782791655486211)
XLA Ops:
  0.0 0.5 %collective-permute-start = (f32[128,256]{1,0:T(8,128)}, f32[128,256]{1,0:T(8,128)S(1)}, u32[]{:S(2)}, u32[]{:S(2)}) collective-permute-start(f32[128,256]{1,0:T(8,128)} %k_ref.1), channel_id=1, source_target_pairs={{0,1},{1,0},{2,3},{3,2},{4,5},{5,4},{6,7},{7,6},{8,9},{9,8},{10,11... | collective-permute-start | bytes 393224 | tf_op jit(solution)/shard_map/ppermute | solution.py:127
  0.5 1.1 %collective-permute-done.refs_2_.kc_ref = f32[128,256]{1,0:T(8,128)S(1)} collective-permute-done((f32[128,256]{1,0:T(8,128)}, f32[128,256]{1,0:T(8,128)S(1)}, u32[]{:S(2)}, u32[]{:S(2)}) %collective-permute-start) | collective-permute-done | bytes 131104 | tf_op jit(solution)/shard_map/ppermute | solution.py:127
  1.7 0.4 %collective-permute-done.3.refs_6_.vc_ref = f32[128,256]{1,0:T(8,128)S(1)} collective-permute-done((f32[128,256]{1,0:T(8,128)}, f32[128,256]{1,0:T(8,128)S(1)}, u32[]{:S(2)}, u32[]{:S(2)}) %collective-permute-start.3) | collective-permute-done | bytes 131104 | tf_op jit(solution)/shard_map/ppermute | solution.py:127
  2.3 0.6 %copy-done.5 = f32[128,256]{1,0:T(8,128)} copy-done((f32[128,256]{1,0:T(8,128)}, f32[128,256]{1,0:T(8,128)S(1)}, u32[]{:S(2)}) %copy-start.5) | copy-done | bytes 131096
  3.0 2.0 %shard_map.56 = f32[128,128]{1,0:T(8,128)} custom-call(f32[128,256]{1,0:T(8,128)} %k_ref.1, f32[128,256]{1,0:T(8,128)} %v_ref.1, f32[128,256]{1,0:T(8,128)} %copy-done.3, f32[128,256]{1,0:T(8,128)} %copy-done.5), custom_call_target="tpu_custom_call" | custom-call | tf_op jit(solution)/shard_map/pallas_call | solution.py:142
  4.9 5.0 %collective-permute-start.8 = (f32[128,128]{1,0:T(8,128)}, f32[128,128]{1,0:T(8,128)S(1)}, u32[]{:S(2)}, u32[]{:S(2)}) collective-permute-start(f32[128,128]{1,0:T(8,128)} %shard_map.56), channel_id=1, source_target_pairs={{0,24},{1,25},{2,26},{3,27},{4,28},{5,29},{6,30},{7,31},{8,16},{9,... | collective-permute-start | bytes 196616 | tf_op jit(solution)/shard_map/ppermute | solution.py:127
  9.9 0.6 %collective-permute-start.6 = (f32[128,128]{1,0:T(8,128)}, f32[128,128]{1,0:T(8,128)S(1)}, u32[]{:S(2)}, u32[]{:S(2)}) collective-permute-start(f32[128,128]{1,0:T(8,128)} %shard_map.56), channel_id=1, source_target_pairs={{0,16},{1,17},{2,18},{3,19},{4,20},{5,21},{6,22},{7,23},{8,24},{9,... | collective-permute-start | bytes 196616 | tf_op jit(solution)/shard_map/ppermute | solution.py:127
  10.5 1.7 %collective-permute-start.1 = (f32[128,256]{1,0:T(8,128)S(1)}, f32[128,256]{1,0:T(8,128)S(1)}, u32[]{:S(2)}, u32[]{:S(2)}) collective-permute-start(f32[128,256]{1,0:T(8,128)S(1)} %copy-done.1), channel_id=1, source_target_pairs={{0,2},{1,3},{2,0},{3,1},{4,6},{5,7},{6,4},{7,5},{8,10},{9,11},{10,... | collective-permute-start | bytes 393224 | tf_op jit(solution)/shard_map/ppermute | solution.py:127
  12.2 0.3 %collective-permute-start.4 = (f32[128,256]{1,0:T(8,128)S(1)}, f32[128,256]{1,0:T(8,128)S(1)}, u32[]{:S(2)}, u32[]{:S(2)}) collective-permute-start(f32[128,256]{1,0:T(8,128)S(1)} %copy-done.2), channel_id=1, source_target_pairs={{0,2},{1,3},{2,0},{3,1},{4,6},{5,7},{6,4},{7,5},{8,10},{9,11},{10,... | collective-permute-start | bytes 393224 | tf_op jit(solution)/shard_map/ppermute | solution.py:127
  12.5 0.5 %collective-permute-done.8 = f32[128,128]{1,0:T(8,128)S(1)} collective-permute-done((f32[128,128]{1,0:T(8,128)}, f32[128,128]{1,0:T(8,128)S(1)}, u32[]{:S(2)}, u32[]{:S(2)}) %collective-permute-start.8) | collective-permute-done | bytes 65568 | tf_op jit(solution)/shard_map/ppermute | solution.py:127
  13.0 2.1 %collective-permute-done.7 = f32[128,128]{1,0:T(8,128)S(1)} collective-permute-done((f32[128,128]{1,0:T(8,128)}, f32[128,128]{1,0:T(8,128)S(1)}, u32[]{:S(2)}, u32[]{:S(2)}) %collective-permute-start.7) | collective-permute-done | bytes 65568 | tf_op jit(solution)/shard_map/ppermute | solution.py:127
  15.1 0.9 %collective-permute-done.6 = f32[128,128]{1,0:T(8,128)S(1)} collective-permute-done((f32[128,128]{1,0:T(8,128)}, f32[128,128]{1,0:T(8,128)S(1)}, u32[]{:S(2)}, u32[]{:S(2)}) %collective-permute-start.6) | collective-permute-done | bytes 65568 | tf_op jit(solution)/shard_map/ppermute | solution.py:127
  16.0 0.9 %select_add_fusion = (f32[128,128]{1,0:T(8,128)S(1)}, f32[128,128]{1,0:T(8,128)S(1)}) fusion(f32[128,128]{1,0:T(8,128)} %shard_map.56, pred[]{:T(512)S(6)} %gt.4, f32[128,128]{1,0:T(8,128)S(1)} %collective-permute-done.8, pred[]{:T(512)S(6)} %lt.11, f32[128,128]{1,0:T(8,128)S(1)} %collective-permute-done.7, pred[]{:T(512)S(6)} %lt.10, ...), kind=kLoop, calls=%fused_computation.1 | loop fusion | flops 114688 | bytes 393220 | tf_op jit(solution)/shard_map/add | solution.py:163
  16.8 1.7 %collective-permute-start.11 = (f32[128,128]{1,0:T(8,128)S(1)}, f32[128,128]{1,0:T(8,128)S(1)}, u32[]{:S(2)}, u32[]{:S(2)}) collective-permute-start(f32[128,128]{1,0:T(8,128)S(1)} %get-tuple-element.13), channel_id=1, source_target_pairs={{0,6},{1,7},{2,4},{3,5},{4,2},{5,3},{6,0},{7,1},{8,14},{9,15},{10,... | collective-permute-start | bytes 196616 | tf_op jit(solution)/shard_map/ppermute | solution.py:127
  18.5 0.5 %collective-permute-start.10 = (f32[128,128]{1,0:T(8,128)S(1)}, f32[128,128]{1,0:T(8,128)S(1)}, u32[]{:S(2)}, u32[]{:S(2)}) collective-permute-start(f32[128,128]{1,0:T(8,128)S(1)} %get-tuple-element.14), channel_id=1, source_target_pairs={{0,2},{1,3},{2,0},{3,1},{4,6},{5,7},{6,4},{7,5},{8,10},{9,11},{10,... | collective-permute-start | bytes 196616 | tf_op jit(solution)/shard_map/ppermute | solution.py:127
  19.1 1.3 %collective-permute-start.9 = (f32[128,128]{1,0:T(8,128)S(1)}, f32[128,128]{1,0:T(8,128)S(1)}, u32[]{:S(2)}, u32[]{:S(2)}) collective-permute-start(f32[128,128]{1,0:T(8,128)S(1)} %get-tuple-element.13), channel_id=1, source_target_pairs={{0,4},{1,5},{2,6},{3,7},{4,0},{5,1},{6,2},{7,3},{8,12},{9,13},{10,... | collective-permute-start | bytes 196616 | tf_op jit(solution)/shard_map/ppermute | solution.py:127
  20.4 0.5 %collective-permute-start.5 = (f32[128,256]{1,0:T(8,128)S(1)}, f32[128,256]{1,0:T(8,128)S(1)}, u32[]{:S(2)}, u32[]{:S(2)}) collective-permute-start(f32[128,256]{1,0:T(8,128)S(1)} %collective-permute-done.4.refs_7_), channel_id=1, source_target_pairs={{0,1},{1,0},{2,3},{3,2},{4,5},{5,4},{6,7},{7,6},{8,9},{9,8},{10,11... | collective-permute-start | bytes 393224 | tf_op jit(solution)/shard_map/ppermute | solution.py:127
  20.9 1.2 %collective-permute-done.11 = f32[128,128]{1,0:T(8,128)S(1)} collective-permute-done((f32[128,128]{1,0:T(8,128)S(1)}, f32[128,128]{1,0:T(8,128)S(1)}, u32[]{:S(2)}, u32[]{:S(2)}) %collective-permute-start.11) | collective-permute-done | bytes 65568 | tf_op jit(solution)/shard_map/ppermute | solution.py:127
  22.1 0.7 %collective-permute-done.10 = f32[128,128]{1,0:T(8,128)S(1)} collective-permute-done((f32[128,128]{1,0:T(8,128)S(1)}, f32[128,128]{1,0:T(8,128)S(1)}, u32[]{:S(2)}, u32[]{:S(2)}) %collective-permute-start.10) | collective-permute-done | bytes 65568 | tf_op jit(solution)/shard_map/ppermute | solution.py:127
  22.8 0.5 %collective-permute-done.9 = f32[128,128]{1,0:T(8,128)S(1)} collective-permute-done((f32[128,128]{1,0:T(8,128)S(1)}, f32[128,128]{1,0:T(8,128)S(1)}, u32[]{:S(2)}, u32[]{:S(2)}) %collective-permute-start.9) | collective-permute-done | bytes 65568 | tf_op jit(solution)/shard_map/ppermute | solution.py:127
  23.5 0.5 %copy-done.7 = f32[1024]{0:T(1024)S(1)} copy-done((f32[1024]{0:T(1024)S(1)}, f32[1024]{0:T(1024)}, u32[]{:S(2)}) %copy-start.7) | copy-done | bytes 4120
  24.1 0.9 %copy-done.6 = f32[128,256]{1,0:T(8,128)S(1)} copy-done((f32[128,256]{1,0:T(8,128)S(1)}, f32[128,256]{1,0:T(8,128)}, u32[]{:S(2)}) %copy-start.6) | copy-done | bytes 131096
  25.0 2.4 %shard_map.55 = (f32[128,1024]{1,0:T(8,128)S(1)}, bf16[128,1024]{1,0:T(8,128)(2,1)S(1)}, bf16[128,1024]{1,0:T(8,128)(2,1)S(1)}, f32[1,1024]{1,0:T(1,128)S(1)}) custom-call(f32[128,1024]{1,0:T(8,128)S(1)} %copy-done, f32[128,256]{1,0:T(8,128)S(1)} %copy-done.1, f32[128,256]{1,0:T(8,128)S(1)} %copy-done.4, f32[128,256]{1,0:T(8,128)S(1)} %collective-permute-done.1.refs_3_, ...), custom_call_target="tpu_custom_call" | custom-call | tf_op jit(solution)/shard_map/pallas_call | solution.py:174
  27.4 1.3 %shard_map.57 = f32[128,1024]{1,0:T(8,128)} custom-call(f32[128,1024]{1,0:T(8,128)S(1)} %get-tuple-element.9.refs_0_, bf16[128,1024]{1,0:T(8,128)(2,1)S(1)} %get-tuple-element.10.refs_1_, bf16[128,1024]{1,0:T(8,128)(2,1)S(1)} %get-tuple-element.11.refs_2_, f32[1,1024]{1,0:T(1,128)S(1)} %get-tuple-element.12.refs_3_, f32[128,128]{1,0:T(8,128)S(1)} %add_add_fusion.refs_4_, ...), custom_call_target="tpu_custom_call" | custom-call | tf_op jit(solution)/shard_map/pallas_call | solution.py:190
  (25 shorter events, 0.6 us)
Async XLA Ops:
  0.0 10.5 %copy-start.1 = (f32[128,256]{1,0:T(8,128)S(1)}, f32[128,256]{1,0:T(8,128)}, u32[]{:S(2)}) copy-start(f32[128,256]{1,0:T(8,128)} %k_ref.1) | copy-start | bytes 393220
  0.0 12.2 %copy-start.2 = (f32[128,256]{1,0:T(8,128)S(1)}, f32[128,256]{1,0:T(8,128)}, u32[]{:S(2)}) copy-start(f32[128,256]{1,0:T(8,128)} %v_ref.1) | copy-start | bytes 393220
  0.0 1.6 %collective-permute-start = (f32[128,256]{1,0:T(8,128)}, f32[128,256]{1,0:T(8,128)S(1)}, u32[]{:S(2)}, u32[]{:S(2)}) collective-permute-start(f32[128,256]{1,0:T(8,128)} %k_ref.1), channel_id=1, source_target_pairs={{0,1},{1,0},{2,3},{3,2},{4,5},{5,4},{6,7},{7,6},{8,9},{9,8},{10,11... | collective-permute-start | bytes 393224 | tf_op jit(solution)/shard_map/ppermute | solution.py:127
  0.5 1.6 %collective-permute-start.3 = (f32[128,256]{1,0:T(8,128)}, f32[128,256]{1,0:T(8,128)S(1)}, u32[]{:S(2)}, u32[]{:S(2)}) collective-permute-start(f32[128,256]{1,0:T(8,128)} %v_ref.1), channel_id=1, source_target_pairs={{0,1},{1,0},{2,3},{3,2},{4,5},{5,4},{6,7},{7,6},{8,9},{9,8},{10,11... | collective-permute-start | bytes 393224 | tf_op jit(solution)/shard_map/ppermute | solution.py:127
  1.7 0.7 %copy-start.3 = (f32[128,256]{1,0:T(8,128)}, f32[128,256]{1,0:T(8,128)S(1)}, u32[]{:S(2)}) copy-start(f32[128,256]{1,0:T(8,128)S(1)} %collective-permute-done.refs_2_.kc_ref) | copy-start | bytes 393220
  2.3 0.7 %copy-start.5 = (f32[128,256]{1,0:T(8,128)}, f32[128,256]{1,0:T(8,128)S(1)}, u32[]{:S(2)}) copy-start(f32[128,256]{1,0:T(8,128)S(1)} %collective-permute-done.3.refs_6_.vc_ref) | copy-start | bytes 393220
  4.9 18.5 %copy-start = (f32[128,1024]{1,0:T(8,128)S(1)}, f32[128,1024]{1,0:T(8,128)}, u32[]{:S(2)}) copy-start(f32[128,1024]{1,0:T(8,128)} %refs_0_.1) | copy-start | bytes 1572868
  4.9 8.1 %collective-permute-start.8 = (f32[128,128]{1,0:T(8,128)}, f32[128,128]{1,0:T(8,128)S(1)}, u32[]{:S(2)}, u32[]{:S(2)}) collective-permute-start(f32[128,128]{1,0:T(8,128)} %shard_map.56), channel_id=1, source_target_pairs={{0,24},{1,25},{2,26},{3,27},{4,28},{5,29},{6,30},{7,31},{8,16},{9,... | collective-permute-start | bytes 196616 | tf_op jit(solution)/shard_map/ppermute | solution.py:127
  9.9 5.2 %collective-permute-start.7 = (f32[128,128]{1,0:T(8,128)}, f32[128,128]{1,0:T(8,128)S(1)}, u32[]{:S(2)}, u32[]{:S(2)}) collective-permute-start(f32[128,128]{1,0:T(8,128)} %shard_map.56), channel_id=1, source_target_pairs={{0,8},{1,9},{2,10},{3,11},{4,12},{5,13},{6,14},{7,15},{8,0},{9,1},... | collective-permute-start | bytes 196616 | tf_op jit(solution)/shard_map/ppermute | solution.py:127
  9.9 6.1 %collective-permute-start.6 = (f32[128,128]{1,0:T(8,128)}, f32[128,128]{1,0:T(8,128)S(1)}, u32[]{:S(2)}, u32[]{:S(2)}) collective-permute-start(f32[128,128]{1,0:T(8,128)} %shard_map.56), channel_id=1, source_target_pairs={{0,16},{1,17},{2,18},{3,19},{4,20},{5,21},{6,22},{7,23},{8,24},{9,... | collective-permute-start | bytes 196616 | tf_op jit(solution)/shard_map/ppermute | solution.py:127
  10.5 9.9 %collective-permute-start.1 = (f32[128,256]{1,0:T(8,128)S(1)}, f32[128,256]{1,0:T(8,128)S(1)}, u32[]{:S(2)}, u32[]{:S(2)}) collective-permute-start(f32[128,256]{1,0:T(8,128)S(1)} %copy-done.1), channel_id=1, source_target_pairs={{0,2},{1,3},{2,0},{3,1},{4,6},{5,7},{6,4},{7,5},{8,10},{9,11},{10,... | collective-permute-start | bytes 393224 | tf_op jit(solution)/shard_map/ppermute | solution.py:127
  12.2 8.2 %collective-permute-start.4 = (f32[128,256]{1,0:T(8,128)S(1)}, f32[128,256]{1,0:T(8,128)S(1)}, u32[]{:S(2)}, u32[]{:S(2)}) collective-permute-start(f32[128,256]{1,0:T(8,128)S(1)} %copy-done.2), channel_id=1, source_target_pairs={{0,2},{1,3},{2,0},{3,1},{4,6},{5,7},{6,4},{7,5},{8,10},{9,11},{10,... | collective-permute-start | bytes 393224 | tf_op jit(solution)/shard_map/ppermute | solution.py:127
  16.8 5.2 %collective-permute-start.11 = (f32[128,128]{1,0:T(8,128)S(1)}, f32[128,128]{1,0:T(8,128)S(1)}, u32[]{:S(2)}, u32[]{:S(2)}) collective-permute-start(f32[128,128]{1,0:T(8,128)S(1)} %get-tuple-element.13), channel_id=1, source_target_pairs={{0,6},{1,7},{2,4},{3,5},{4,2},{5,3},{6,0},{7,1},{8,14},{9,15},{10,... | collective-permute-start | bytes 196616 | tf_op jit(solution)/shard_map/ppermute | solution.py:127
  18.5 4.9 %copy-start.4 = (f32[128,256]{1,0:T(8,128)S(1)}, f32[128,256]{1,0:T(8,128)}, u32[]{:S(2)}) copy-start(f32[128,256]{1,0:T(8,128)} %copy-done.3) | copy-start | bytes 393220
  18.5 4.3 %collective-permute-start.10 = (f32[128,128]{1,0:T(8,128)S(1)}, f32[128,128]{1,0:T(8,128)S(1)}, u32[]{:S(2)}, u32[]{:S(2)}) collective-permute-start(f32[128,128]{1,0:T(8,128)S(1)} %get-tuple-element.14), channel_id=1, source_target_pairs={{0,2},{1,3},{2,0},{3,1},{4,6},{5,7},{6,4},{7,5},{8,10},{9,11},{10,... | collective-permute-start | bytes 196616 | tf_op jit(solution)/shard_map/ppermute | solution.py:127
  19.1 4.3 %collective-permute-start.9 = (f32[128,128]{1,0:T(8,128)S(1)}, f32[128,128]{1,0:T(8,128)S(1)}, u32[]{:S(2)}, u32[]{:S(2)}) collective-permute-start(f32[128,128]{1,0:T(8,128)S(1)} %get-tuple-element.13), channel_id=1, source_target_pairs={{0,4},{1,5},{2,6},{3,7},{4,0},{5,1},{6,2},{7,3},{8,12},{9,13},{10,... | collective-permute-start | bytes 196616 | tf_op jit(solution)/shard_map/ppermute | solution.py:127
  20.4 3.0 %collective-permute-start.2 = (f32[128,256]{1,0:T(8,128)S(1)}, f32[128,256]{1,0:T(8,128)S(1)}, u32[]{:S(2)}, u32[]{:S(2)}) collective-permute-start(f32[128,256]{1,0:T(8,128)S(1)} %collective-permute-done.1.refs_3_), channel_id=1, source_target_pairs={{0,1},{1,0},{2,3},{3,2},{4,5},{5,4},{6,7},{7,6},{8,9},{9,8},{10,11... | collective-permute-start | bytes 393224 | tf_op jit(solution)/shard_map/ppermute | solution.py:127
  20.4 3.0 %collective-permute-start.5 = (f32[128,256]{1,0:T(8,128)S(1)}, f32[128,256]{1,0:T(8,128)S(1)}, u32[]{:S(2)}, u32[]{:S(2)}) collective-permute-start(f32[128,256]{1,0:T(8,128)S(1)} %collective-permute-done.4.refs_7_), channel_id=1, source_target_pairs={{0,1},{1,0},{2,3},{3,2},{4,5},{5,4},{6,7},{7,6},{8,9},{9,8},{10,11... | collective-permute-start | bytes 393224 | tf_op jit(solution)/shard_map/ppermute | solution.py:127
  23.3 0.7 %copy-start.7 = (f32[1024]{0:T(1024)S(1)}, f32[1024]{0:T(1024)}, u32[]{:S(2)}) copy-start(f32[1024]{0:T(1024)} %param.9) | copy-start | bytes 12292
  23.3 4.0 %collective-permute-start.12 = (f32[128,128]{1,0:T(8,128)S(1)}, f32[128,128]{1,0:T(8,128)S(1)}, u32[]{:S(2)}, u32[]{:S(2)}) collective-permute-start(f32[128,128]{1,0:T(8,128)S(1)} %add_add_fusion.refs_4_), channel_id=1, source_target_pairs={{0,1},{1,0},{2,3},{3,2},{4,5},{5,4},{6,7},{7,6},{8,9},{9,8},{10,11... | collective-permute-start | bytes 196616 | tf_op jit(solution)/shard_map/ppermute | solution.py:127
  23.4 0.7 %copy-start.8 = (f32[8]{0:T(128)S(1)}, f32[8]{0:T(128)}, u32[]{:S(2)}) copy-start(f32[8]{0:T(128)} %param.8) | copy-start | bytes 100
  24.1 0.9 %copy-start.6 = (f32[128,256]{1,0:T(8,128)S(1)}, f32[128,256]{1,0:T(8,128)}, u32[]{:S(2)}) copy-start(f32[128,256]{1,0:T(8,128)} %copy-done.5) | copy-start | bytes 393220

commit v2 on v1

v2 whole, which is shorter than its diff:
```python
import functools

import jax
import jax.numpy as jnp
from jax import lax
from jax.experimental import pallas as pl
from jax.experimental.pallas import tpu as pltpu
from jax.sharding import PartitionSpec as P

HD = 128
EPS = 1e-6
NEG = -1e30


def sigma_map(x):
    return jnp.where(x > 0, x + 1.0, jnp.exp(jnp.minimum(x, 0.0)))


def split(x):
    high = x.astype(jnp.bfloat16)
    low = (x - high.astype(jnp.float32)).astype(jnp.bfloat16)
    return high, low


def dot(a, b, dims):
    return lax.dot_general(a, b, (dims, ((), ())), preferred_element_type=jnp.float32)


def carried_head(lines):
    head = lax.axis_index("blk") & 1
    for axis, bit in lines:
        head = head ^ ((lax.axis_index(axis) >> bit) & 1)
    return head


def partial_kernel(lines, has_part, passed, *refs):
    k_ref, v_ref = refs[:2]
    out_ref = refs[2 + has_part + passed]
    head = carried_head(lines)
    cols = pl.ds(pl.multiple_of(head * HD, HD), HD)
    s_hi, s_lo = split(sigma_map(k_ref[:, cols]))
    v_hi, v_lo = split(v_ref[:, cols])
    left = jnp.concatenate([s_hi, s_lo, s_hi], 0)
    right = jnp.concatenate([v_hi, v_hi, v_lo], 0)
    part = dot(left, right, ((0,), (0,)))
    if has_part:
        out_ref[...] = refs[2][...] + part
    else:
        out_ref[...] = part
        refs[-2][...] = k_ref[...]
        refs[-1][...] = v_ref[...]


def combine_kernel(masks, nexts, carries, loose, *refs):
    count = len(masks)
    part_ref = refs[0]
    got_refs = refs[1 : 1 + count]
    outs = refs[1 + count + carries + loose :]
    seg = lax.axis_index("seg")
    total = refs[1 + count][...] if carries else None
    for (s, _), got_ref in zip(masks, got_refs, strict=True):
        got = got_ref[...]
        if not carries:
            got = jnp.where((seg ^ s) < seg, got, 0.0)
        total = got if total is None else total + got
    outs[0][...] = total
    for s, out_ref in zip(nexts, outs[1 : 1 + len(nexts)], strict=True):
        out_ref[...] = total + jnp.where((seg ^ s) > seg, part_ref[...], 0.0)


def attend(q_hi, q_lo, pieces, causal):
    left = jnp.concatenate([q_hi, q_lo], 1)
    scores = []
    for k, _ in pieces:
        k_hi, k_lo = split(k)
        piece = dot(left, jnp.concatenate([k_hi, k_hi], 1), ((1,), (1,)))
        scores.append(piece + dot(q_hi, k_lo, ((1,), (1,))))
    if causal is not None:
        scores[0] = jnp.where(causal, scores[0], NEG)
    top = functools.reduce(jnp.maximum, scores)
    top = jnp.max(top, axis=1, keepdims=True)
    accum, summed = [], []
    for piece, (_, v) in zip(scores, pieces, strict=True):
        w = jnp.exp(piece - top)
        v_hi, v_lo = split(v)
        w_hi, w_lo = split(w)
        both = dot(w_hi, jnp.concatenate([v_hi, v_lo], 1), ((1,), (0,)))
        accum.append(both[:, :HD] + both[:, HD:] + dot(w_lo, v_hi, ((1,), (0,))))
        summed.append(w)
    total = jnp.sum(functools.reduce(jnp.add, summed), axis=1, keepdims=True)
    return top, total, functools.reduce(jnp.add, accum)


def load_queries(q_ref, group, head):
    spans = [slice((head * group + g) * HD, (head * group + g + 1) * HD) for g in range(group)]
    return spans, jnp.concatenate([q_ref[:, s] for s in spans], 0)


def local_kernel(group, *refs):
    q_ref, k_ref, kc_ref, v_ref, vc_ref, gate_ref, gain_ref = refs[:7]
    acc_ref, top_ref, total_ref, sh_ref, sl_ref, mult_ref = refs[7:]
    rows = q_ref.shape[0]
    kv_heads = k_ref.shape[1] // HD
    second = (lax.axis_index("blk") & 1) == 1
    gates = 1.0 / (1.0 + jnp.exp(-gate_ref[...]))
    causal = lax.broadcasted_iota(jnp.int32, (rows, rows), 1) <= lax.broadcasted_iota(
        jnp.int32, (rows, rows), 0
    )
    causal = jnp.concatenate([causal] * group, 0)
    scale = 1.0 / jnp.sqrt(jnp.float32(HD))

    def work(with_other):
        for head in range(kv_heads):
            kv = slice(head * HD, (head + 1) * HD)
            spans, q = load_queries(q_ref, group, head)
            f_hi, f_lo = split(sigma_map(q))
            pieces = [(k_ref[:, kv], v_ref[:, kv])]
            if with_other:
                pieces.append((kc_ref[:, kv], vc_ref[:, kv]))
            top, total, accum = attend(*split(q * scale), pieces, causal)
            for g, s in enumerate(spans):
                h = head * group + g
                part = slice(g * rows, (g + 1) * rows)
                sh_ref[:, s] = f_hi[part]
                sl_ref[:, s] = f_lo[part]
                acc_ref[:, s] = accum[part]
                top_ref[:, h : h + 1] = top[part]
                total_ref[:, h : h + 1] = total[part]
                mult_ref[:, s] = gates[:, h : h + 1] * gain_ref[:, s]

    pl.when(second)(lambda: work(True))
    pl.when(jnp.logical_not(second))(lambda: work(False))


def remote_kernel(group, chunks, *refs):
    q_ref = refs[0]
    k_refs, v_refs = refs[1 : 1 + chunks], refs[1 + chunks : 1 + 2 * chunks]
    acc_ref, top_ref, total_ref, gate_ref = refs[1 + 2 * chunks : 5 + 2 * chunks]
    att_ref, top_out, total_out, done_ref = refs[5 + 2 * chunks :]
    rows = q_ref.shape[0]
    kv_heads = k_refs[0].shape[1] // HD
    place = lax.axis_index("blk")
    scale = 1.0 / jnp.sqrt(jnp.float32(HD))
    top_out[...] = top_ref[...]
    total_out[...] = total_ref[...]
    att_ref[...] = acc_ref[...]

    def add_chunks(first, last):
        for head in range(kv_heads):
            kv = slice(head * HD, (head + 1) * HD)
            spans, q = load_queries(q_ref, group, head)
            pieces = [(k_refs[m][:, kv], v_refs[m][:, kv]) for m in range(first, last)]
            top, total, accum = attend(*split(q * scale), pieces, None)
            for g, s in enumerate(spans):
                h = head * group + g
                part = slice(g * rows, (g + 1) * rows)
                old = top_out[:, h : h + 1]
                peak = jnp.maximum(old, top[part])
                before, after = jnp.exp(old - peak), jnp.exp(top[part] - peak)
                total_out[:, h : h + 1] = total_out[:, h : h + 1] * before + total[part] * after
                att_ref[:, s] = att_ref[:, s] * before + accum[part] * after
                top_out[:, h : h + 1] = peak

    bit = 1
    while (1 << bit) < chunks + 2:
        first = (1 << bit) - 2
        pl.when(((place >> bit) & 1) == 1)(
            functools.partial(add_chunks, first, first + (1 << bit))
        )
        bit += 1
    gates = 1.0 / (1.0 + jnp.exp(-gate_ref[...]))
    for h in range(kv_heads * group):
        s = slice(h * HD, (h + 1) * HD)
        weight = (1.0 - gates[:, h : h + 1]) / total_out[:, h : h + 1]
        att_ref[:, s] = att_ref[:, s] * weight
    done_ref[...] = jnp.zeros_like(done_ref)


def final_kernel(group, lines, att_ref, sh_ref, sl_ref, mult_ref, mine_ref, other_ref, out_ref):
    rows = att_ref.shape[0]
    kv_heads = att_ref.shape[1] // (group * HD)
    own = carried_head(lines)
    for head in range(kv_heads):
        memory = jnp.where(own == head, mine_ref[...], other_ref[...])
        m_hi, m_lo = split(memory)
        right = jnp.concatenate([m_hi, m_hi], 0)
        spans = [
            slice((head * group + g) * HD, (head * group + g + 1) * HD) for g in range(group)
        ]
        f_hi = jnp.concatenate([sh_ref[:, s] for s in spans], 0)
        f_lo = jnp.concatenate([sl_ref[:, s] for s in spans], 0)
        r = dot(jnp.concatenate([f_hi, f_lo], 1), right, ((1,), (0,)))
        r = r + dot(f_hi, m_lo, ((1,), (0,)))
        inv = lax.rsqrt(jnp.mean(r * r, axis=1, keepdims=True) + EPS)
        r = r * inv
        for g, s in enumerate(spans):
            out_ref[:, s] = att_ref[:, s] + r[g * rows : (g + 1) * rows] * mult_ref[:, s]


def solution(mesh):
    n_seg, n_blk = mesh.shape["seg"], mesh.shape["blk"]
    both = ("seg", "blk")

    def swap(x, seg_bits, blk_bits):
        pairs = [
            (s * n_blk + b, (s ^ seg_bits) * n_blk + (b ^ blk_bits))
            for s in range(n_seg)
            for b in range(n_blk)
        ]
        return lax.ppermute(x, both, pairs)

    bits = [("seg", i) for i in reversed(range(n_seg.bit_length() - 1))]
    bits += [("blk", i) for i in reversed(range(1, n_blk.bit_length() - 1))]
    groups = [bits[i : i + 2] for i in range(0, len(bits), 2)]
    lines = groups[-1]

    def masks_of(number):
        found = [(0, 0)]
        for axis, bit in reversed(groups[number]):
            flip = int(number == len(groups) - 1)
            step = (1 << bit, flip) if axis == "seg" else (0, (1 << bit) ^ flip)
            found += [(s ^ step[0], b ^ step[1]) for s, b in found]
        return [found[i] for i in ((1, 3, 2) if number == 0 and len(found) > 3 else range(1, len(found)))]

    def on_device(queries, keys, values, gate_logit, memory_gain):
        rows, width = queries.shape
        group = width // keys.shape[1]
        square = jax.ShapeDtypeStruct((HD, HD), jnp.float32)

        def pass_on(kernel, inputs, loose, passed, outs, flops):
            anywhere = pl.BlockSpec(memory_space=pl.ANY)
            count, n_out = len(inputs) + len(loose), len(outs)
            return pl.pallas_call(
                kernel,
                in_specs=[pl.BlockSpec()] * len(inputs) + [anywhere] * (len(loose) + len(passed)),
                out_specs=[pl.BlockSpec()] * n_out + [anywhere] * len(passed),
                out_shape=outs
                + [jax.ShapeDtypeStruct(x.shape, x.dtype) for x in passed],
                input_output_aliases={count + i: n_out + i for i in range(len(passed))},
                compiler_params=pltpu.CompilerParams(vmem_limit_bytes=8 * 1024 * 1024),
                cost_estimate=pl.CostEstimate(
                    flops=flops, bytes_accessed=500_000, transcendentals=20_000
                ),
            )(*inputs, *loose, *passed)

        k_core, v_core = swap(keys, 0, 1), swap(values, 0, 1)
        tall = jax.ShapeDtypeStruct(keys.shape, jnp.float32)
        part, k_own, v_own = pass_on(
            functools.partial(partial_kernel, lines, 0, 0),
            [keys, values],
            [],
            [],
            [square, tall, tall],
            500_000_000,
        )
        part, k_own, v_own = pass_on(
            functools.partial(partial_kernel, lines, 1, 2),
            [k_core, v_core, part],
            [],
            [k_own, v_own],
            [square],
            500_000_000,
        )
        gate, gain = gate_logit.reshape(1, -1), memory_gain.reshape(1, -1)
        wide = jax.ShapeDtypeStruct((rows, width), jnp.float32)
        wide_half = jax.ShapeDtypeStruct((rows, width), jnp.bfloat16)
        per_head = jax.ShapeDtypeStruct((rows, width // HD), jnp.float32)
        line = jax.ShapeDtypeStruct((1, width), jnp.float32)
        large = pltpu.CompilerParams(vmem_limit_bytes=24 * 1024 * 1024)
        cost = pl.CostEstimate(flops=1_000_000_000, bytes_accessed=2_000_000, transcendentals=400_000)
        accum, top, total, f_hi, f_lo, mult = pl.pallas_call(
            functools.partial(local_kernel, group),
            out_shape=(wide, per_head, per_head, wide_half, wide_half, line),
            compiler_params=large,
            cost_estimate=cost,
        )(queries, k_own, k_core, v_own, v_core, gate, gain)

        k_held, v_held = [k_own, k_core], [v_own, v_core]
        fresh = [swap(k_own, 0, 2), swap(v_own, 0, 2)] if n_blk > 2 else []

        att = None
        carried = None
        sends = {s: part for s, _ in masks_of(0)}
        for number in range(len(groups)):
            masks = masks_of(number)
            got = [swap(sends[s], s, b) for s, b in masks]
            last = number == len(groups) - 1
            nexts = [] if last else sorted({s for s, _ in masks_of(number + 1) if s})
            some = [] if carried is None else [carried]
            loose = [mult] if number == 0 else [done] if last else []
            passed = fresh if number == 0 else []
            carried, *extra = pass_on(
                functools.partial(combine_kernel, masks, nexts, len(some), len(loose) + len(passed)),
                [part, *got, *some],
                loose,
                passed,
                [square] * (1 + len(nexts)),
                100_000,
            )
            sends = {0: carried, **dict(zip(nexts, extra[: len(nexts)], strict=True))}
            if number == 0:
                fresh = extra[len(nexts) :]
                step = 2
                while step < n_blk:
                    if step == 2:
                        fresh_k, fresh_v = fresh[:1], fresh[1:]
                    else:
                        fresh_k = [swap(k_held[m], 0, step) for m in range(0, step, 2)]
                        fresh_v = [swap(v_held[m], 0, step) for m in range(0, step, 2)]
                    for k_new, v_new in zip(fresh_k, fresh_v, strict=True):
                        k_held += [k_new, swap(k_new, 0, 1)]
                        v_held += [v_new, swap(v_new, 0, 1)]
                    step *= 2
                att, _, _, done = pl.pallas_call(
                    functools.partial(remote_kernel, group, n_blk - 2),
                    out_shape=(wide, per_head, per_head, jax.ShapeDtypeStruct((8, HD), jnp.float32)),
                    compiler_params=large,
                    cost_estimate=cost,
                )(queries, *k_held[2:], *v_held[2:], accum, top, total, gate)
        other = swap(carried, 0, 1)

        return pl.pallas_call(
            functools.partial(final_kernel, group, lines),
            out_shape=jax.ShapeDtypeStruct((rows, width), jnp.float32),
            compiler_params=pltpu.CompilerParams(vmem_limit_bytes=16 * 1024 * 1024),
        )(att, f_hi, f_lo, mult, carried, other)

    return jax.shard_map(
        on_device,
        mesh=mesh,
        in_specs=(P(both, None), P(both, None), P(both, None), P(), P()),
        out_specs=P(both, None),
        check_vma=False,
    )
```

time: 28.9 us -> 26.6 us (0.920)
  Pallas kernels: 5.6 us -> 3.48 us
  waiting for transfers between devices: 7.38 us -> 8.46 us
  other arithmetic: 0.88 us -> 0 us
    pallas_call x3 -> x7, Pallas kernels: 5.6 us -> 3.48 us  [the longest x1 1.26 us: on_device(): pl.pallas_call(functools.partial(final_kernel, group, lines), out_shape=j...]
    ppermute x13, waiting for transfers between devices: 7.38 us -> 8.46 us  [swap(): return lax.ppermute(x, both, pairs)]
    add x2 -> x0, other arithmetic: 0.88 us -> none  [the longest x1 0.86 us: on_device(): carried + jnp.where(seg ^ s > seg, part, 0.0)]
    unnamed x18 -> x10, local copies, waits for them, and re-layouts: 2.49 us -> 2.47 us
  transfers between devices with their start and end apart: 13 -> 13, of which waited for: 8 -> 6; matrix products, arithmetic and copies ran while one was open for 3% -> 0% of each run, Pallas kernels for 8% -> 7%
where the time goes in v2:
time: 26.6 us; the launch traced here: 26.4 us
  starting transfers between devices  12 us (45%)
  waiting for transfers between devices  8.46 us (32%)
  Pallas kernels  3.48 us (13%)
  local copies, waits for them, and re-layouts  2.47 us (9%)
    ppermute x13, starting transfers between devices, swap(): return lax.ppermute(x, both, pairs)  12 us
    ppermute x13, waiting for transfers between devices, swap(): return lax.ppermute(x, both, pairs)  8.46 us
    unnamed x10, local copies, waits for them, and re-layouts  2.47 us
    pallas_call x1, Pallas kernels, on_device(): pl.pallas_call(functools.partial(final_kernel, group, lines), out_shape=j...  1.26 us
    pallas_call x1, Pallas kernels, on_device(): pl.pallas_call(functools.partial(local_kernel, group), out_shape=(wide, p...  1.02 us
    pallas_call x1, Pallas kernels, on_device(): pl.pallas_call(functools.partial(remote_kernel, group, n_blk - 2), out_sh...  0.69 us
  transfers between devices with their start and end apart: 13, of which 6 were waited for; matrix products, arithmetic and copies ran while one was open for 0% of the time, Pallas kernels for 7%

profile of v2, /device:TPU:0, one launch (start us, length us, event | category | flops | bytes accessed | tf_op | source)
XLA Modules:
  0.0 26.4 jit_solution(17502683852970836854)
XLA Ops:
  0.0 0.5 %collective-permute-start = (f32[128,256]{1,0:T(8,128)}, f32[128,256]{1,0:T(8,128)S(1)}, u32[]{:S(2)}, u32[]{:S(2)}) collective-permute-start(f32[128,256]{1,0:T(8,128)} %refs_0_.3), channel_id=1, source_target_pairs={{0,1},{1,0},{2,3},{3,2},{4,5},{5,4},{6,7},{7,6},{8,9},{9,8},{10,11... | collective-permute-start | bytes 393224 | tf_op jit(solution)/shard_map/ppermute | solution.py:210
  0.5 0.9 %copy-done.1 = f32[128,256]{1,0:T(8,128)S(1)} copy-done((f32[128,256]{1,0:T(8,128)S(1)}, f32[128,256]{1,0:T(8,128)}, u32[]{:S(2)}) %copy-start.1) | copy-done | bytes 131096
  1.4 0.9 %copy-done.2 = f32[128,256]{1,0:T(8,128)S(1)} copy-done((f32[128,256]{1,0:T(8,128)S(1)}, f32[128,256]{1,0:T(8,128)}, u32[]{:S(2)}) %copy-start.2) | copy-done | bytes 131096
  2.3 0.2 shard_map.55
  2.6 0.2 shard_map.56
  2.9 3.0 %collective-permute-start.5 = (f32[128,256]{1,0:T(8,128)S(1)}, f32[128,256]{1,0:T(8,128)S(1)}, u32[]{:S(2)}, u32[]{:S(2)}) collective-permute-start(f32[128,256]{1,0:T(8,128)S(1)} %get-tuple-element.27.refs_1_), channel_id=1, source_target_pairs={{0,2},{1,3},{2,0},{3,1},{4,6},{5,7},{6,4},{7,5},{8,10},{9,11},{10,... | collective-permute-start | bytes 393224 | tf_op jit(solution)/shard_map/ppermute | solution.py:210
  5.9 2.0 %collective-permute-start.2 = (f32[128,128]{1,0:T(8,128)S(1)}, f32[128,128]{1,0:T(8,128)S(1)}, u32[]{:S(2)}, u32[]{:S(2)}) collective-permute-start(f32[128,128]{1,0:T(8,128)S(1)} %get-tuple-element.26.refs_0_), channel_id=1, source_target_pairs={{0,8},{1,9},{2,10},{3,11},{4,12},{5,13},{6,14},{7,15},{8,0},{9,1},... | collective-permute-start | bytes 196616 | tf_op jit(solution)/shard_map/ppermute | solution.py:210
  8.0 2.5 %collective-permute-start.3 = (f32[128,128]{1,0:T(8,128)S(1)}, f32[128,128]{1,0:T(8,128)S(1)}, u32[]{:S(2)}, u32[]{:S(2)}) collective-permute-start(f32[128,128]{1,0:T(8,128)S(1)} %get-tuple-element.26.refs_0_), channel_id=1, source_target_pairs={{0,24},{1,25},{2,26},{3,27},{4,28},{5,29},{6,30},{7,31},{8,16},{9,... | collective-permute-start | bytes 196616 | tf_op jit(solution)/shard_map/ppermute | solution.py:210
  10.4 0.1 collective-permute-start.4
  10.6 0.6 %copy-done.4 = f32[8]{0:T(128)S(1)} copy-done((f32[8]{0:T(128)S(1)}, f32[8]{0:T(128)}, u32[]{:S(2)}) %copy-start.4) | copy-done | bytes 56
  11.2 1.0 %shard_map.57 = (f32[128,1024]{1,0:T(8,128)S(1)}, f32[128,8]{1,0:T(8,128)S(1)}, f32[128,8]{1,0:T(8,128)S(1)}, bf16[128,1024]{1,0:T(8,128)(2,1)S(1)}, bf16[128,10...) custom-call(f32[128,1024]{1,0:T(8,128)S(1)} %copy-done, f32[128,256]{1,0:T(8,128)S(1)} %get-tuple-element.27.refs_1_, ...), custom_call_target="tpu_custom_call" | custom-call | flops 1000000000 | bytes 2000000 | tf_op jit(solution)/shard_map/pallas_call | solution.py:271
  12.2 2.2 %collective-permute-done.3.refs_2_ = f32[128,128]{1,0:T(8,128)S(1)} collective-permute-done((f32[128,128]{1,0:T(8,128)S(1)}, f32[128,128]{1,0:T(8,128)S(1)}, u32[]{:S(2)}, u32[]{:S(2)}) %collective-permute-start.3) | collective-permute-done | bytes 65568 | tf_op jit(solution)/shard_map/ppermute | solution.py:210
  14.4 2.1 %collective-permute-done.4.refs_3_ = f32[128,128]{1,0:T(8,128)S(1)} collective-permute-done((f32[128,128]{1,0:T(8,128)S(1)}, f32[128,128]{1,0:T(8,128)S(1)}, u32[]{:S(2)}, u32[]{:S(2)}) %collective-permute-start.4) | collective-permute-done | bytes 65568 | tf_op jit(solution)/shard_map/ppermute | solution.py:210
  16.7 0.5 %collective-permute-start.8 = (f32[128,256]{1,0:T(8,128)S(1)}, f32[128,256]{1,0:T(8,128)S(1)}, u32[]{:S(2)}, u32[]{:S(2)}) collective-permute-start(f32[128,256]{1,0:T(8,128)S(1)} %get-tuple-element.31.refs_3_), channel_id=1, source_target_pairs={{0,1},{1,0},{2,3},{3,2},{4,5},{5,4},{6,7},{7,6},{8,9},{9,8},{10,11... | collective-permute-start | bytes 393224 | tf_op jit(solution)/shard_map/ppermute | solution.py:210
  17.1 1.2 %collective-permute-start.10 = (f32[128,128]{1,0:T(8,128)S(1)}, f32[128,128]{1,0:T(8,128)S(1)}, u32[]{:S(2)}, u32[]{:S(2)}) collective-permute-start(f32[128,128]{1,0:T(8,128)S(1)} %get-tuple-element.39), channel_id=1, source_target_pairs={{0,5},{1,4},{2,7},{3,6},{4,1},{5,0},{6,3},{7,2},{8,13},{9,12},{10,... | collective-permute-start | bytes 196616 | tf_op jit(solution)/shard_map/ppermute | solution.py:210
  18.4 1.4 %collective-permute-start.11 = (f32[128,128]{1,0:T(8,128)S(1)}, f32[128,128]{1,0:T(8,128)S(1)}, u32[]{:S(2)}, u32[]{:S(2)}) collective-permute-start(f32[128,128]{1,0:T(8,128)S(1)} %get-tuple-element.39), channel_id=1, source_target_pairs={{0,6},{1,7},{2,4},{3,5},{4,2},{5,3},{6,0},{7,1},{8,14},{9,15},{10,... | collective-permute-start | bytes 196616 | tf_op jit(solution)/shard_map/ppermute | solution.py:210
  19.8 0.3 %collective-permute-start.9 = (f32[128,128]{1,0:T(8,128)S(1)}, f32[128,128]{1,0:T(8,128)S(1)}, u32[]{:S(2)}, u32[]{:S(2)}) collective-permute-start(f32[128,128]{1,0:T(8,128)S(1)} %get-tuple-element.38.refs_4_), channel_id=1, source_target_pairs={{0,3},{1,2},{2,1},{3,0},{4,7},{5,6},{6,5},{7,4},{8,11},{9,10},{10,... | collective-permute-start | bytes 196616 | tf_op jit(solution)/shard_map/ppermute | solution.py:210
  20.1 0.7 %shard_map.59 = (f32[128,1024]{1,0:T(8,128)S(1)}, f32[128,8]{1,0:T(8,128)}, f32[128,8]{1,0:T(8,128)}, f32[8,128]{1,0:T(8,128)S(1)}) custom-call(f32[128,1024]{1,0:T(8,128)S(1)} %copy-done, f32[128,256]{1,0:T(8,128)S(1)} %get-tuple-element.30.refs_1_, f32[128,256]{1,0:T(8,128)S(1)} %collective-permute-done.7.refs_2_, ...), custom_call_target="tpu_custom_call" | custom-call | flops 1000000000 | bytes 2000000 | tf_op jit(solution)/shard_map/pallas_call | solution.py:314
  20.8 0.5 %collective-permute-done.10.refs_2_ = f32[128,128]{1,0:T(8,128)S(1)} collective-permute-done((f32[128,128]{1,0:T(8,128)S(1)}, f32[128,128]{1,0:T(8,128)S(1)}, u32[]{:S(2)}, u32[]{:S(2)}) %collective-permute-start.10) | collective-permute-done | bytes 65568 | tf_op jit(solution)/shard_map/ppermute | solution.py:210
  21.3 2.4 %collective-permute-done.11.refs_3_ = f32[128,128]{1,0:T(8,128)S(1)} collective-permute-done((f32[128,128]{1,0:T(8,128)S(1)}, f32[128,128]{1,0:T(8,128)S(1)}, u32[]{:S(2)}, u32[]{:S(2)}) %collective-permute-start.11) | collective-permute-done | bytes 65568 | tf_op jit(solution)/shard_map/ppermute | solution.py:210
  23.7 0.2 collective-permute-done.9.refs_1_
  23.9 0.2 collective-permute-start.12
  24.1 1.1 %collective-permute-done.12.other_ref = f32[128,128]{1,0:T(8,128)S(1)} collective-permute-done((f32[128,128]{1,0:T(8,128)S(1)}, f32[128,128]{1,0:T(8,128)S(1)}, u32[]{:S(2)}, u32[]{:S(2)}) %collective-permute-start.12) | collective-permute-done | bytes 65568 | tf_op jit(solution)/shard_map/ppermute | solution.py:210
  25.2 1.3 %shard_map.61 = f32[128,1024]{1,0:T(8,128)} custom-call(f32[128,1024]{1,0:T(8,128)S(1)} %get-tuple-element.35.att_ref, bf16[128,1024]{1,0:T(8,128)(2,1)S(1)} %get-tuple-element.36.sh_ref, bf16[128,1024]{1,0:T(8,128)(2,1)S(1)} %get-tuple-element.37.sl_ref, f32[1,1024]{1,0:T(1,128)S(1)} %get-tuple-element.29.refs_4_.mult_ref, ...), custom_call_target="tpu_custom_call" | custom-call | tf_op jit(solution)/shard_map/pallas_call | solution.py:322
  (19 shorter events, 0.3 us)
Async XLA Ops:
  0.0 2.6 %collective-permute-start = (f32[128,256]{1,0:T(8,128)}, f32[128,256]{1,0:T(8,128)S(1)}, u32[]{:S(2)}, u32[]{:S(2)}) collective-permute-start(f32[128,256]{1,0:T(8,128)} %refs_0_.3), channel_id=1, source_target_pairs={{0,1},{1,0},{2,3},{3,2},{4,5},{5,4},{6,7},{7,6},{8,9},{9,8},{10,11... | collective-permute-start | bytes 393224 | tf_op jit(solution)/shard_map/ppermute | solution.py:210
  0.5 2.1 %collective-permute-start.1 = (f32[128,256]{1,0:T(8,128)}, f32[128,256]{1,0:T(8,128)S(1)}, u32[]{:S(2)}, u32[]{:S(2)}) collective-permute-start(f32[128,256]{1,0:T(8,128)} %refs_1_.1), channel_id=1, source_target_pairs={{0,1},{1,0},{2,3},{3,2},{4,5},{5,4},{6,7},{7,6},{8,9},{9,8},{10,11... | collective-permute-start | bytes 393224 | tf_op jit(solution)/shard_map/ppermute | solution.py:210
  0.5 0.9 %copy-start.1 = (f32[128,256]{1,0:T(8,128)S(1)}, f32[128,256]{1,0:T(8,128)}, u32[]{:S(2)}) copy-start(f32[128,256]{1,0:T(8,128)} %refs_0_.3) | copy-start | bytes 393220
  1.4 0.9 %copy-start.2 = (f32[128,256]{1,0:T(8,128)S(1)}, f32[128,256]{1,0:T(8,128)}, u32[]{:S(2)}) copy-start(f32[128,256]{1,0:T(8,128)} %refs_1_.1) | copy-start | bytes 393220
  2.6 8.0 %copy-start = (f32[128,1024]{1,0:T(8,128)S(1)}, f32[128,1024]{1,0:T(8,128)}, u32[]{:S(2)}) copy-start(f32[128,1024]{1,0:T(8,128)} %refs_0_.5) | copy-start | bytes 1572868
  2.8 7.7 %copy-start.3 = (f32[1024]{0:T(1024)S(1)}, f32[1024]{0:T(1024)}, u32[]{:S(2)}) copy-start(f32[1024]{0:T(1024)} %param.9) | copy-start | bytes 12292
  2.9 13.7 %collective-permute-start.5 = (f32[128,256]{1,0:T(8,128)S(1)}, f32[128,256]{1,0:T(8,128)S(1)}, u32[]{:S(2)}, u32[]{:S(2)}) collective-permute-start(f32[128,256]{1,0:T(8,128)S(1)} %get-tuple-element.27.refs_1_), channel_id=1, source_target_pairs={{0,2},{1,3},{2,0},{3,1},{4,6},{5,7},{6,4},{7,5},{8,10},{9,11},{10,... | collective-permute-start | bytes 393224 | tf_op jit(solution)/shard_map/ppermute | solution.py:210
  5.9 10.7 %collective-permute-start.6 = (f32[128,256]{1,0:T(8,128)S(1)}, f32[128,256]{1,0:T(8,128)S(1)}, u32[]{:S(2)}, u32[]{:S(2)}) collective-permute-start(f32[128,256]{1,0:T(8,128)S(1)} %get-tuple-element.28.refs_3_), channel_id=1, source_target_pairs={{0,2},{1,3},{2,0},{3,1},{4,6},{5,7},{6,4},{7,5},{8,10},{9,11},{10,... | collective-permute-start | bytes 393224 | tf_op jit(solution)/shard_map/ppermute | solution.py:210
  5.9 6.3 %collective-permute-start.2 = (f32[128,128]{1,0:T(8,128)S(1)}, f32[128,128]{1,0:T(8,128)S(1)}, u32[]{:S(2)}, u32[]{:S(2)}) collective-permute-start(f32[128,128]{1,0:T(8,128)S(1)} %get-tuple-element.26.refs_0_), channel_id=1, source_target_pairs={{0,8},{1,9},{2,10},{3,11},{4,12},{5,13},{6,14},{7,15},{8,0},{9,1},... | collective-permute-start | bytes 196616 | tf_op jit(solution)/shard_map/ppermute | solution.py:210
  8.0 6.5 %collective-permute-start.3 = (f32[128,128]{1,0:T(8,128)S(1)}, f32[128,128]{1,0:T(8,128)S(1)}, u32[]{:S(2)}, u32[]{:S(2)}) collective-permute-start(f32[128,128]{1,0:T(8,128)S(1)} %get-tuple-element.26.refs_0_), channel_id=1, source_target_pairs={{0,24},{1,25},{2,26},{3,27},{4,28},{5,29},{6,30},{7,31},{8,16},{9,... | collective-permute-start | bytes 196616 | tf_op jit(solution)/shard_map/ppermute | solution.py:210
  10.4 6.1 %collective-permute-start.4 = (f32[128,128]{1,0:T(8,128)S(1)}, f32[128,128]{1,0:T(8,128)S(1)}, u32[]{:S(2)}, u32[]{:S(2)}) collective-permute-start(f32[128,128]{1,0:T(8,128)S(1)} %get-tuple-element.26.refs_0_), channel_id=1, source_target_pairs={{0,16},{1,17},{2,18},{3,19},{4,20},{5,21},{6,22},{7,23},{8,24},{9,... | collective-permute-start | bytes 196616 | tf_op jit(solution)/shard_map/ppermute | solution.py:210
  10.6 0.7 %copy-start.4 = (f32[8]{0:T(128)S(1)}, f32[8]{0:T(128)}, u32[]{:S(2)}) copy-start(f32[8]{0:T(128)} %param.8) | copy-start | bytes 100
  16.6 3.5 %collective-permute-start.7 = (f32[128,256]{1,0:T(8,128)S(1)}, f32[128,256]{1,0:T(8,128)S(1)}, u32[]{:S(2)}, u32[]{:S(2)}) collective-permute-start(f32[128,256]{1,0:T(8,128)S(1)} %get-tuple-element.30.refs_1_), channel_id=1, source_target_pairs={{0,1},{1,0},{2,3},{3,2},{4,5},{5,4},{6,7},{7,6},{8,9},{9,8},{10,11... | collective-permute-start | bytes 393224 | tf_op jit(solution)/shard_map/ppermute | solution.py:210
  16.7 3.4 %collective-permute-start.8 = (f32[128,256]{1,0:T(8,128)S(1)}, f32[128,256]{1,0:T(8,128)S(1)}, u32[]{:S(2)}, u32[]{:S(2)}) collective-permute-start(f32[128,256]{1,0:T(8,128)S(1)} %get-tuple-element.31.refs_3_), channel_id=1, source_target_pairs={{0,1},{1,0},{2,3},{3,2},{4,5},{5,4},{6,7},{7,6},{8,9},{9,8},{10,11... | collective-permute-start | bytes 393224 | tf_op jit(solution)/shard_map/ppermute | solution.py:210
  17.1 4.1 %collective-permute-start.10 = (f32[128,128]{1,0:T(8,128)S(1)}, f32[128,128]{1,0:T(8,128)S(1)}, u32[]{:S(2)}, u32[]{:S(2)}) collective-permute-start(f32[128,128]{1,0:T(8,128)S(1)} %get-tuple-element.39), channel_id=1, source_target_pairs={{0,5},{1,4},{2,7},{3,6},{4,1},{5,0},{6,3},{7,2},{8,13},{9,12},{10,... | collective-permute-start | bytes 196616 | tf_op jit(solution)/shard_map/ppermute | solution.py:210
  18.4 5.3 %collective-permute-start.11 = (f32[128,128]{1,0:T(8,128)S(1)}, f32[128,128]{1,0:T(8,128)S(1)}, u32[]{:S(2)}, u32[]{:S(2)}) collective-permute-start(f32[128,128]{1,0:T(8,128)S(1)} %get-tuple-element.39), channel_id=1, source_target_pairs={{0,6},{1,7},{2,4},{3,5},{4,2},{5,3},{6,0},{7,1},{8,14},{9,15},{10,... | collective-permute-start | bytes 196616 | tf_op jit(solution)/shard_map/ppermute | solution.py:210
  19.8 4.1 %collective-permute-start.9 = (f32[128,128]{1,0:T(8,128)S(1)}, f32[128,128]{1,0:T(8,128)S(1)}, u32[]{:S(2)}, u32[]{:S(2)}) collective-permute-start(f32[128,128]{1,0:T(8,128)S(1)} %get-tuple-element.38.refs_4_), channel_id=1, source_target_pairs={{0,3},{1,2},{2,1},{3,0},{4,7},{5,6},{6,5},{7,4},{8,11},{9,10},{10,... | collective-permute-start | bytes 196616 | tf_op jit(solution)/shard_map/ppermute | solution.py:210
  23.9 1.3 %collective-permute-start.12 = (f32[128,128]{1,0:T(8,128)S(1)}, f32[128,128]{1,0:T(8,128)S(1)}, u32[]{:S(2)}, u32[]{:S(2)}) collective-permute-start(f32[128,128]{1,0:T(8,128)S(1)} %shard_map.60.mine_ref), channel_id=1, source_target_pairs={{0,1},{1,0},{2,3},{3,2},{4,5},{5,4},{6,7},{7,6},{8,9},{9,8},{10,11... | collective-permute-start | bytes 196616 | tf_op jit(solution)/shard_map/ppermute | solution.py:210

commit v3 on v2

v3 whole, which is shorter than its diff:
```python
import functools

import jax
import jax.numpy as jnp
from jax import lax
from jax.experimental import pallas as pl
from jax.experimental.pallas import tpu as pltpu
from jax.sharding import PartitionSpec as P

HD = 128
EPS = 1e-6
NEG = -1e30


def sigma_map(x):
    return jnp.where(x > 0, x + 1.0, jnp.exp(jnp.minimum(x, 0.0)))


def split(x):
    high = x.astype(jnp.bfloat16)
    low = (x - high.astype(jnp.float32)).astype(jnp.bfloat16)
    return high, low


def dot(a, b, dims):
    return lax.dot_general(a, b, (dims, ((), ())), preferred_element_type=jnp.float32)


def carried_head(lines):
    head = lax.axis_index("blk") & 1
    for axis, bit in lines:
        head = head ^ ((lax.axis_index(axis) >> bit) & 1)
    return head


def add_partial(head, k_ref, v_ref):
    cols = pl.ds(pl.multiple_of(head * HD, HD), HD)
    s_hi, s_lo = split(sigma_map(k_ref[:, cols]))
    v_hi, v_lo = split(v_ref[:, cols])
    left = jnp.concatenate([s_hi, s_lo, s_hi], 0)
    right = jnp.concatenate([v_hi, v_hi, v_lo], 0)
    return dot(left, right, ((0,), (0,)))


def chip_kernel(lines, kv_ref, kc_ref, vc_ref, part_ref):
    half = kc_ref.shape[1]
    head = carried_head(lines)
    own = add_partial(head, kv_ref.at[:, :half], kv_ref.at[:, half:])
    part_ref[...] = own + add_partial(head, kc_ref, vc_ref)


def hold_kernel(*refs):
    pass


def combine_kernel(masks, nexts, carries, loose, *refs):
    count = len(masks)
    part_ref = refs[0]
    got_refs = refs[1 : 1 + count]
    outs = refs[1 + count + carries + loose :]
    seg = lax.axis_index("seg")
    total = refs[1 + count][...] if carries else None
    for (s, _), got_ref in zip(masks, got_refs, strict=True):
        got = got_ref[...]
        if not carries:
            got = jnp.where((seg ^ s) < seg, got, 0.0)
        total = got if total is None else total + got
    outs[0][...] = total
    for s, out_ref in zip(nexts, outs[1 : 1 + len(nexts)], strict=True):
        out_ref[...] = total + jnp.where((seg ^ s) > seg, part_ref[...], 0.0)


def attend(q_hi, q_lo, keys, values, mask):
    k_hi, k_lo = split(jnp.concatenate(keys, 0))
    v_hi, v_lo = split(jnp.concatenate(values, 0))
    left = jnp.concatenate([q_hi, q_lo], 1)
    scores = dot(left, jnp.concatenate([k_hi, k_hi], 1), ((1,), (1,)))
    scores = scores + dot(q_hi, k_lo, ((1,), (1,)))
    scores = mask(scores)
    top = jnp.max(scores, axis=1, keepdims=True)
    w = jnp.exp(scores - top)
    total = jnp.sum(w, axis=1, keepdims=True)
    w_hi, w_lo = split(w)
    both = dot(w_hi, jnp.concatenate([v_hi, v_lo], 1), ((1,), (0,)))
    return top, total, both[:, :HD] + both[:, HD:] + dot(w_lo, v_hi, ((1,), (0,)))


def prepare_kernel(group, *refs):
    q_ref, gate_ref, gain_ref = refs[:3]
    qh_ref, ql_ref, sh_ref, sl_ref, mult_ref, keep_ref = refs[3:]
    scale = 1.0 / jnp.sqrt(jnp.float32(HD))
    gates = 1.0 / (1.0 + jnp.exp(-gate_ref[...]))
    for h in range(q_ref.shape[1] // HD):
        s = slice(h * HD, (h + 1) * HD)
        q = q_ref[:, s]
        qh_ref[:, s], ql_ref[:, s] = split(q * scale)
        sh_ref[:, s], sl_ref[:, s] = split(sigma_map(q))
        gate = jnp.broadcast_to(gates[:, h : h + 1], (1, HD))
        mult_ref[:, s] = gate * gain_ref[:, s]
        keep_ref[:, s] = 1.0 - gate


def attention_kernel(group, chunks, *refs):
    qh_ref, ql_ref = refs[:2]
    half = refs[2].shape[1]
    k_refs = [ref.at[:, :half] for ref in refs[4 : 3 + chunks]]
    v_refs = [ref.at[:, half:] for ref in refs[4 : 3 + chunks]]
    k_refs.insert(1, refs[2])
    v_refs.insert(1, refs[3])
    keep_ref, att_ref, done_ref = refs[3 + chunks :]
    rows = qh_ref.shape[0]
    kv_heads = half // HD
    place = lax.axis_index("blk")
    causal = lax.broadcasted_iota(jnp.int32, (rows, rows), 1) <= lax.broadcasted_iota(
        jnp.int32, (rows, rows), 0
    )
    causal = jnp.concatenate([causal] * group, 0)

    def work(count):
        def mask(scores):
            pieces = [jnp.where(causal, scores[:, :rows], NEG)]
            for m in range(1, count // 2):
                piece = scores[:, m * rows : (m + 1) * rows]
                pieces.append(jnp.where((place ^ m) < place, piece, NEG))
            if count > 1:
                pieces.append(scores[:, max(count // 2, 1) * rows :])
            return jnp.concatenate(pieces, 1) if count > 1 else pieces[0]

        for head in range(kv_heads):
            kv = slice(head * HD, (head + 1) * HD)
            spans = [
                slice((head * group + g) * HD, (head * group + g + 1) * HD) for g in range(group)
            ]
            q_hi = jnp.concatenate([qh_ref[:, s] for s in spans], 0)
            q_lo = jnp.concatenate([ql_ref[:, s] for s in spans], 0)
            keys = [k_refs[m][:, kv] for m in range(count)]
            values = [v_refs[m][:, kv] for m in range(count)]
            _, total, accum = attend(q_hi, q_lo, keys, values, mask)
            accum = accum / total
            for g, s in enumerate(spans):
                att_ref[:, s] = accum[g * rows : (g + 1) * rows] * keep_ref[:, s]

    count = 1
    while count <= chunks:
        low, high = count // 2, count
        pl.when((place >= low) & (place < high))(functools.partial(work, count))
        count *= 2
    done_ref[...] = jnp.zeros_like(done_ref)


def final_kernel(group, lines, att_ref, sh_ref, sl_ref, mult_ref, mine_ref, other_ref, out_ref):
    rows = att_ref.shape[0]
    kv_heads = att_ref.shape[1] // (group * HD)
    own = carried_head(lines)
    for head in range(kv_heads):
        memory = jnp.where(own == head, mine_ref[...], other_ref[...])
        m_hi, m_lo = split(memory)
        right = jnp.concatenate([m_hi, m_hi], 0)
        spans = [
            slice((head * group + g) * HD, (head * group + g + 1) * HD) for g in range(group)
        ]
        f_hi = jnp.concatenate([sh_ref[:, s] for s in spans], 0)
        f_lo = jnp.concatenate([sl_ref[:, s] for s in spans], 0)
        r = dot(jnp.concatenate([f_hi, f_lo], 1), right, ((1,), (0,)))
        r = r + dot(f_hi, m_lo, ((1,), (0,)))
        inv = lax.rsqrt(jnp.mean(r * r, axis=1, keepdims=True) + EPS)
        r = r * inv
        for g, s in enumerate(spans):
            out_ref[:, s] = att_ref[:, s] + r[g * rows : (g + 1) * rows] * mult_ref[:, s]


def solution(mesh):
    n_seg, n_blk = mesh.shape["seg"], mesh.shape["blk"]
    both = ("seg", "blk")

    def swap(x, seg_bits, blk_bits):
        pairs = [
            (s * n_blk + b, (s ^ seg_bits) * n_blk + (b ^ blk_bits))
            for s in range(n_seg)
            for b in range(n_blk)
        ]
        return lax.ppermute(x, both, pairs)

    bits = [("seg", i) for i in reversed(range(n_seg.bit_length() - 1))]
    bits += [("blk", i) for i in reversed(range(1, n_blk.bit_length() - 1))]
    groups = [bits[i : i + 2] for i in range(0, len(bits), 2)]
    lines = groups[-1]

    def masks_of(number):
        found = [(0, 0)]
        for axis, bit in reversed(groups[number]):
            flip = int(number == len(groups) - 1)
            step = (1 << bit, flip) if axis == "seg" else (0, (1 << bit) ^ flip)
            found += [(s ^ step[0], b ^ step[1]) for s, b in found]
        return [found[i] for i in ((1, 3, 2) if number == 0 and len(found) > 3 else range(1, len(found)))]

    def on_device(queries, keys, values, gate_logit, memory_gain):
        rows, width = queries.shape
        group = width // keys.shape[1]
        square = jax.ShapeDtypeStruct((HD, HD), jnp.float32)

        def pass_on(kernel, inputs, loose, passed, outs, flops):
            anywhere = pl.BlockSpec(memory_space=pl.ANY)
            count, n_out = len(inputs) + len(loose), len(outs)
            return pl.pallas_call(
                kernel,
                in_specs=[pl.BlockSpec()] * len(inputs) + [anywhere] * (len(loose) + len(passed)),
                out_specs=[pl.BlockSpec()] * n_out + [anywhere] * len(passed),
                out_shape=outs
                + [jax.ShapeDtypeStruct(x.shape, x.dtype) for x in passed],
                input_output_aliases={count + i: n_out + i for i in range(len(passed))},
                compiler_params=pltpu.CompilerParams(vmem_limit_bytes=8 * 1024 * 1024),
                cost_estimate=pl.CostEstimate(
                    flops=flops, bytes_accessed=500_000, transcendentals=20_000
                ),
            )(*inputs, *loose, *passed)

        k_core, v_core = swap(keys, 0, 1), swap(values, 0, 1)
        own = jnp.concatenate([keys, values], 1)
        (part,) = pass_on(
            functools.partial(chip_kernel, lines), [own, k_core, v_core], [], [], [square], 500_000_000
        )
        gate, gain = gate_logit.reshape(1, -1), memory_gain.reshape(1, -1)
        wide = jax.ShapeDtypeStruct((rows, width), jnp.float32)
        half = jax.ShapeDtypeStruct((rows, width), jnp.bfloat16)
        line = jax.ShapeDtypeStruct((1, width), jnp.float32)
        large = pltpu.CompilerParams(vmem_limit_bytes=24 * 1024 * 1024)
        q_hi, q_lo, f_hi, f_lo, mult, keep = pl.pallas_call(
            functools.partial(prepare_kernel, group),
            out_shape=(half, half, half, half, line, line),
            compiler_params=large,
            cost_estimate=pl.CostEstimate(
                flops=1_000_000, bytes_accessed=100_000, transcendentals=0
            ),
        )(queries, gate, gain)

        held = [own, None]
        fresh = [swap(own, 0, 2)] if n_blk > 2 else []

        carried = None
        sends = {s: part for s, _ in masks_of(0)}
        for number in range(len(groups)):
            masks = masks_of(number)
            got = [swap(sends[s], s, b) for s, b in masks]
            last = number == len(groups) - 1
            nexts = [] if last else sorted({s for s, _ in masks_of(number + 1) if s})
            some = [] if carried is None else [carried]
            loose = [mult] if number == 0 else [done] if last else []
            carried, *extra = pass_on(
                functools.partial(combine_kernel, masks, nexts, len(some), len(loose)),
                [part, *got, *some],
                loose,
                [],
                [square] * (1 + len(nexts)),
                10_000_000_000 if number == 0 else 100_000,
            )
            sends = {0: carried, **dict(zip(nexts, extra, strict=True))}
            if number == 0:
                step = 2
                while step < n_blk:
                    if step == 2:
                        news = pass_on(hold_kernel, [], [carried], fresh, [], 0)
                    else:
                        news = [swap(held[m], 0, step) for m in range(0, step, 2)]
                    for new in news:
                        held += [new, swap(new, 0, 1)]
                    step *= 2
                att, done = pl.pallas_call(
                    functools.partial(attention_kernel, group, n_blk),
                    out_shape=(wide, jax.ShapeDtypeStruct((8, HD), jnp.float32)),
                    compiler_params=large,
                    cost_estimate=pl.CostEstimate(
                        flops=1_000_000, bytes_accessed=100_000, transcendentals=0
                    ),
                )(q_hi, q_lo, k_core, v_core, own, *held[2:], keep)
        other = swap(carried, 0, 1)

        return pl.pallas_call(
            functools.partial(final_kernel, group, lines),
            out_shape=jax.ShapeDtypeStruct((rows, width), jnp.float32),
            compiler_params=pltpu.CompilerParams(vmem_limit_bytes=16 * 1024 * 1024),
        )(att, f_hi, f_lo, mult, carried, other)

    return jax.shard_map(
        on_device,
        mesh=mesh,
        in_specs=(P(both, None), P(both, None), P(both, None), P(), P()),
        out_specs=P(both, None),
        check_vma=False,
    )
```

time: 26.6 us -> 26.5 us (level)
  waiting for transfers between devices: 8.46 us -> 11.2 us
  starting transfers between devices: 12 us -> 10.7 us
  local copies, waits for them, and re-layouts: 2.47 us -> 1.59 us
  Pallas kernels: 3.48 us -> 2.84 us
    ppermute x13 -> x11, waiting for transfers between devices: 8.46 us -> 11.2 us  [swap(): return lax.ppermute(x, both, pairs)]
    ppermute x13 -> x11, starting transfers between devices: 12 us -> 10.7 us  [swap(): return lax.ppermute(x, both, pairs)]
    unnamed x10 -> x9, local copies, waits for them, and re-layouts: 2.47 us -> 1.58 us
    pallas_call x2, Pallas kernels: 1.72 us -> 1.29 us  [the longest x1 0.9 us: on_device(): pl.pallas_call(functools.partial(attention_kernel, group, n_blk), out_sha...]
  transfers between devices with their start and end apart: 13 -> 11, of which waited for: 6 -> 8; matrix products, arithmetic and copies ran while one was open for 0% -> 4% of each run, Pallas kernels for 7% -> 5%
where the time goes in v3:
time: 26.5 us; the launch traced here: 26.4 us
  waiting for transfers between devices  11.2 us (42%)
  starting transfers between devices  10.7 us (40%)
  Pallas kernels  2.84 us (11%)
  local copies, waits for them, and re-layouts  1.59 us (6%)
    ppermute x11, waiting for transfers between devices, swap(): return lax.ppermute(x, both, pairs)  11.2 us
    ppermute x11, starting transfers between devices, swap(): return lax.ppermute(x, both, pairs)  10.7 us
    unnamed x9, local copies, waits for them, and re-layouts  1.58 us
    pallas_call x1, Pallas kernels, on_device(): pl.pallas_call(functools.partial(final_kernel, group, lines), out_shape=j...  1.26 us
    pallas_call x1, Pallas kernels, on_device(): pl.pallas_call(functools.partial(attention_kernel, group, n_blk), out_sha...  0.9 us
  transfers between devices with their start and end apart: 11, of which 8 were waited for; matrix products, arithmetic and copies ran while one was open for 4% of the time, Pallas kernels for 5%

profile of v3, /device:TPU:0, one launch (start us, length us, event | category | flops | bytes accessed | tf_op | source)
XLA Modules:
  0.0 26.4 jit_solution(3893654101164739915)
XLA Ops:
  0.0 0.5 %collective-permute-start = (f32[128,256]{1,0:T(8,128)}, f32[128,256]{1,0:T(8,128)S(1)}, u32[]{:S(2)}, u32[]{:S(2)}) collective-permute-start(f32[128,256]{1,0:T(8,128)} %param.6), channel_id=1, source_target_pairs={{0,1},{1,0},{2,3},{3,2},{4,5},{5,4},{6,7},{7,6},{8,9},{9,8},{10,11... | collective-permute-start | bytes 393224 | tf_op jit(solution)/shard_map/ppermute | solution.py:182
  0.5 0.1 collective-permute-start.1
  0.5 0.9 %constant_dynamic-update-slice_fusion.1 = f32[128,512]{1,0:T(8,128)S(1)} fusion(f32[128,256]{1,0:T(8,128)} %param.6), kind=kLoop, calls=%fused_computation.1 | loop fusion | bytes 262144
  1.5 0.2 collective-permute-done.kc_ref.refs_2_
  1.7 0.4 %collective-permute-done.1.vc_ref.refs_3_ = f32[128,256]{1,0:T(8,128)S(1)} collective-permute-done((f32[128,256]{1,0:T(8,128)}, f32[128,256]{1,0:T(8,128)S(1)}, u32[]{:S(2)}, u32[]{:S(2)}) %collective-permute-start.1) | collective-permute-done | bytes 131104 | tf_op jit(solution)/shard_map/ppermute | solution.py:182
  2.0 0.3 shard_map.56.refs_0_
  2.3 2.8 %collective-permute-start.2 = (f32[128,128]{1,0:T(8,128)S(1)}, f32[128,128]{1,0:T(8,128)S(1)}, u32[]{:S(2)}, u32[]{:S(2)}) collective-permute-start(f32[128,128]{1,0:T(8,128)S(1)} %shard_map.56.refs_0_), channel_id=1, source_target_pairs={{0,8},{1,9},{2,10},{3,11},{4,12},{5,13},{6,14},{7,15},{8,0},{9,1},... | collective-permute-start | bytes 196616 | tf_op jit(solution)/shard_map/ppermute | solution.py:182
  5.1 2.5 %collective-permute-start.3 = (f32[128,128]{1,0:T(8,128)S(1)}, f32[128,128]{1,0:T(8,128)S(1)}, u32[]{:S(2)}, u32[]{:S(2)}) collective-permute-start(f32[128,128]{1,0:T(8,128)S(1)} %shard_map.56.refs_0_), channel_id=1, source_target_pairs={{0,24},{1,25},{2,26},{3,27},{4,28},{5,29},{6,30},{7,31},{8,16},{9,... | collective-permute-start | bytes 196616 | tf_op jit(solution)/shard_map/ppermute | solution.py:182
  7.6 0.1 collective-permute-start.4
  7.7 1.5 %collective-permute-start.5 = (f32[128,512]{1,0:T(8,128)S(1)}, f32[128,512]{1,0:T(8,128)S(1)}, u32[]{:S(2)}, u32[]{:S(2)}) collective-permute-start(f32[128,512]{1,0:T(8,128)S(1)} %constant_dynamic-update-slice_fusion.kv_ref.refs_4_), channel_id=1, source_target_pairs={{0,2},{1,3},{2,0},{3,1},{4,6},{5,7},{6,4},{7,5},{8,10},{9,11},{10,... | collective-permute-start | bytes 786440 | tf_op jit(solution)/shard_map/ppermute | solution.py:182
  9.2 0.6 %copy-done.2 = f32[8]{0:T(128)S(1)} copy-done((f32[8]{0:T(128)S(1)}, f32[8]{0:T(128)}, u32[]{:S(2)}) %copy-start.2) | copy-done | bytes 56
  9.8 0.4 %shard_map.55 = (bf16[128,1024]{1,0:T(8,128)(2,1)S(1)}, bf16[128,1024]{1,0:T(8,128)(2,1)S(1)}, bf16[128,1024]{1,0:T(8,128)(2,1)S(1)}, bf16[128,1024]{1,0:T(8,128...) custom-call(f32[128,1024]{1,0:T(8,128)S(1)} %copy-done, f32[1,8]{1,0:T(1,128)S(1)} %bitcast.3, f32[1,1024]{1,0:T(1,128)S(1)} %bitcast.2), custom_call_target="tpu_custom_call" | custom-call | flops 1000000 | bytes 100000 | tf_op jit(solution)/shard_map/pallas_call | solution.py:228
  10.2 1.5 %collective-permute-done.3.refs_2_ = f32[128,128]{1,0:T(8,128)S(1)} collective-permute-done((f32[128,128]{1,0:T(8,128)S(1)}, f32[128,128]{1,0:T(8,128)S(1)}, u32[]{:S(2)}, u32[]{:S(2)}) %collective-permute-start.3) | collective-permute-done | bytes 65568 | tf_op jit(solution)/shard_map/ppermute | solution.py:182
  11.7 2.5 %collective-permute-done.4.refs_3_ = f32[128,128]{1,0:T(8,128)S(1)} collective-permute-done((f32[128,128]{1,0:T(8,128)S(1)}, f32[128,128]{1,0:T(8,128)S(1)}, u32[]{:S(2)}, u32[]{:S(2)}) %collective-permute-start.4) | collective-permute-done | bytes 65568 | tf_op jit(solution)/shard_map/ppermute | solution.py:182
  14.2 1.4 %collective-permute-done.5.refs_1_ = f32[128,512]{1,0:T(8,128)S(1)} collective-permute-done((f32[128,512]{1,0:T(8,128)S(1)}, f32[128,512]{1,0:T(8,128)S(1)}, u32[]{:S(2)}, u32[]{:S(2)}) %collective-permute-start.5) | collective-permute-done | bytes 262176 | tf_op jit(solution)/shard_map/ppermute | solution.py:182
  15.7 1.6 %collective-permute-start.7 = (f32[128,128]{1,0:T(8,128)S(1)}, f32[128,128]{1,0:T(8,128)S(1)}, u32[]{:S(2)}, u32[]{:S(2)}) collective-permute-start(f32[128,128]{1,0:T(8,128)S(1)} %get-tuple-element.18.refs_0_.refs_4_), channel_id=1, source_target_pairs={{0,3},{1,2},{2,1},{3,0},{4,7},{5,6},{6,5},{7,4},{8,11},{9,10},{10,... | collective-permute-start | bytes 196616 | tf_op jit(solution)/shard_map/ppermute | solution.py:182
  17.3 1.1 %collective-permute-start.8 = (f32[128,128]{1,0:T(8,128)S(1)}, f32[128,128]{1,0:T(8,128)S(1)}, u32[]{:S(2)}, u32[]{:S(2)}) collective-permute-start(f32[128,128]{1,0:T(8,128)S(1)} %get-tuple-element.23), channel_id=1, source_target_pairs={{0,5},{1,4},{2,7},{3,6},{4,1},{5,0},{6,3},{7,2},{8,13},{9,12},{10,... | collective-permute-start | bytes 196616 | tf_op jit(solution)/shard_map/ppermute | solution.py:182
  18.4 0.5 %collective-permute-start.9 = (f32[128,128]{1,0:T(8,128)S(1)}, f32[128,128]{1,0:T(8,128)S(1)}, u32[]{:S(2)}, u32[]{:S(2)}) collective-permute-start(f32[128,128]{1,0:T(8,128)S(1)} %get-tuple-element.23), channel_id=1, source_target_pairs={{0,6},{1,7},{2,4},{3,5},{4,2},{5,3},{6,0},{7,1},{8,14},{9,15},{10,... | collective-permute-start | bytes 196616 | tf_op jit(solution)/shard_map/ppermute | solution.py:182
  18.9 0.9 %shard_map.59 = (f32[128,1024]{1,0:T(8,128)S(1)}, f32[8,128]{1,0:T(8,128)S(1)}) custom-call(bf16[128,1024]{1,0:T(8,128)(2,1)S(1)} %get-tuple-element.15.refs_0_, bf16[128,1024]{1,0:T(8,128)(2,1)S(1)} %get-tuple-element.16.refs_1_, f32[128,256]{1,0:T(8,128)S(1)} %collective-permute-done.kc_ref.refs_2_, f32[128,256]{1,0:T(8,128)S(1)} %collective-permute-done.1.vc_ref.refs_3_, ...), custom_call_target="tpu_custom_call" | custom-call | flops 1000000 | bytes 100000 | tf_op jit(solution)/shard_map/pallas_call | solution.py:268
  19.8 1.7 %collective-permute-done.8.refs_2_ = f32[128,128]{1,0:T(8,128)S(1)} collective-permute-done((f32[128,128]{1,0:T(8,128)S(1)}, f32[128,128]{1,0:T(8,128)S(1)}, u32[]{:S(2)}, u32[]{:S(2)}) %collective-permute-start.8) | collective-permute-done | bytes 65568 | tf_op jit(solution)/shard_map/ppermute | solution.py:182
  21.5 2.3 %collective-permute-done.9.refs_3_ = f32[128,128]{1,0:T(8,128)S(1)} collective-permute-done((f32[128,128]{1,0:T(8,128)S(1)}, f32[128,128]{1,0:T(8,128)S(1)}, u32[]{:S(2)}, u32[]{:S(2)}) %collective-permute-start.9) | collective-permute-done | bytes 65568 | tf_op jit(solution)/shard_map/ppermute | solution.py:182
  23.8 0.1 collective-permute-start.10
  23.9 1.2 %collective-permute-done.10.other_ref = f32[128,128]{1,0:T(8,128)S(1)} collective-permute-done((f32[128,128]{1,0:T(8,128)S(1)}, f32[128,128]{1,0:T(8,128)S(1)}, u32[]{:S(2)}, u32[]{:S(2)}) %collective-permute-start.10) | collective-permute-done | bytes 65568 | tf_op jit(solution)/shard_map/ppermute | solution.py:182
  25.1 1.3 %shard_map.61 = f32[128,1024]{1,0:T(8,128)} custom-call(f32[128,1024]{1,0:T(8,128)S(1)} %get-tuple-element.20.att_ref, bf16[128,1024]{1,0:T(8,128)(2,1)S(1)} %get-tuple-element.21.sh_ref, bf16[128,1024]{1,0:T(8,128)(2,1)S(1)} %get-tuple-element.22.sl_ref, f32[1,1024]{1,0:T(1,128)S(1)} %get-tuple-element.17.refs_4_.mult_ref, ...), custom_call_target="tpu_custom_call" | custom-call | tf_op jit(solution)/shard_map/pallas_call | solution.py:278
  (15 shorter events, 0.1 us)
Async XLA Ops:
  0.0 1.4 %copy-start.3 = (f32[128,256]{1,0:T(8,128)S(1)}, f32[128,256]{1,0:T(8,128)}, u32[]{:S(2)}) copy-start(f32[128,256]{1,0:T(8,128)} %param.7) | copy-start | bytes 393220
  0.0 1.6 %collective-permute-start = (f32[128,256]{1,0:T(8,128)}, f32[128,256]{1,0:T(8,128)S(1)}, u32[]{:S(2)}, u32[]{:S(2)}) collective-permute-start(f32[128,256]{1,0:T(8,128)} %param.6), channel_id=1, source_target_pairs={{0,1},{1,0},{2,3},{3,2},{4,5},{5,4},{6,7},{7,6},{8,9},{9,8},{10,11... | collective-permute-start | bytes 393224 | tf_op jit(solution)/shard_map/ppermute | solution.py:182
  0.5 1.6 %collective-permute-start.1 = (f32[128,256]{1,0:T(8,128)}, f32[128,256]{1,0:T(8,128)S(1)}, u32[]{:S(2)}, u32[]{:S(2)}) collective-permute-start(f32[128,256]{1,0:T(8,128)} %param.7), channel_id=1, source_target_pairs={{0,1},{1,0},{2,3},{3,2},{4,5},{5,4},{6,7},{7,6},{8,9},{9,8},{10,11... | collective-permute-start | bytes 393224 | tf_op jit(solution)/shard_map/ppermute | solution.py:182
  1.5 7.7 %copy-start = (f32[128,1024]{1,0:T(8,128)S(1)}, f32[128,1024]{1,0:T(8,128)}, u32[]{:S(2)}) copy-start(f32[128,1024]{1,0:T(8,128)} %refs_0_.1) | copy-start | bytes 1572868
  2.0 7.2 %copy-start.1 = (f32[1024]{0:T(1024)S(1)}, f32[1024]{0:T(1024)}, u32[]{:S(2)}) copy-start(f32[1024]{0:T(1024)} %param.9) | copy-start | bytes 12292
  2.3 8.0 %collective-permute-start.2 = (f32[128,128]{1,0:T(8,128)S(1)}, f32[128,128]{1,0:T(8,128)S(1)}, u32[]{:S(2)}, u32[]{:S(2)}) collective-permute-start(f32[128,128]{1,0:T(8,128)S(1)} %shard_map.56.refs_0_), channel_id=1, source_target_pairs={{0,8},{1,9},{2,10},{3,11},{4,12},{5,13},{6,14},{7,15},{8,0},{9,1},... | collective-permute-start | bytes 196616 | tf_op jit(solution)/shard_map/ppermute | solution.py:182
  5.1 6.6 %collective-permute-start.3 = (f32[128,128]{1,0:T(8,128)S(1)}, f32[128,128]{1,0:T(8,128)S(1)}, u32[]{:S(2)}, u32[]{:S(2)}) collective-permute-start(f32[128,128]{1,0:T(8,128)S(1)} %shard_map.56.refs_0_), channel_id=1, source_target_pairs={{0,24},{1,25},{2,26},{3,27},{4,28},{5,29},{6,30},{7,31},{8,16},{9,... | collective-permute-start | bytes 196616 | tf_op jit(solution)/shard_map/ppermute | solution.py:182
  7.6 6.6 %collective-permute-start.4 = (f32[128,128]{1,0:T(8,128)S(1)}, f32[128,128]{1,0:T(8,128)S(1)}, u32[]{:S(2)}, u32[]{:S(2)}) collective-permute-start(f32[128,128]{1,0:T(8,128)S(1)} %shard_map.56.refs_0_), channel_id=1, source_target_pairs={{0,16},{1,17},{2,18},{3,19},{4,20},{5,21},{6,22},{7,23},{8,24},{9,... | collective-permute-start | bytes 196616 | tf_op jit(solution)/shard_map/ppermute | solution.py:182
  7.7 8.0 %collective-permute-start.5 = (f32[128,512]{1,0:T(8,128)S(1)}, f32[128,512]{1,0:T(8,128)S(1)}, u32[]{:S(2)}, u32[]{:S(2)}) collective-permute-start(f32[128,512]{1,0:T(8,128)S(1)} %constant_dynamic-update-slice_fusion.kv_ref.refs_4_), channel_id=1, source_target_pairs={{0,2},{1,3},{2,0},{3,1},{4,6},{5,7},{6,4},{7,5},{8,10},{9,11},{10,... | collective-permute-start | bytes 786440 | tf_op jit(solution)/shard_map/ppermute | solution.py:182
  9.2 0.7 %copy-start.2 = (f32[8]{0:T(128)S(1)}, f32[8]{0:T(128)}, u32[]{:S(2)}) copy-start(f32[8]{0:T(128)} %param.8) | copy-start | bytes 100
  15.7 3.2 %collective-permute-start.6 = (f32[128,512]{1,0:T(8,128)S(1)}, f32[128,512]{1,0:T(8,128)S(1)}, u32[]{:S(2)}, u32[]{:S(2)}) collective-permute-start(f32[128,512]{1,0:T(8,128)S(1)} %shard_map.58.refs_5_), channel_id=1, source_target_pairs={{0,1},{1,0},{2,3},{3,2},{4,5},{5,4},{6,7},{7,6},{8,9},{9,8},{10,11... | collective-permute-start | bytes 786440 | tf_op jit(solution)/shard_map/ppermute | solution.py:182
  15.7 4.1 %collective-permute-start.7 = (f32[128,128]{1,0:T(8,128)S(1)}, f32[128,128]{1,0:T(8,128)S(1)}, u32[]{:S(2)}, u32[]{:S(2)}) collective-permute-start(f32[128,128]{1,0:T(8,128)S(1)} %get-tuple-element.18.refs_0_.refs_4_), channel_id=1, source_target_pairs={{0,3},{1,2},{2,1},{3,0},{4,7},{5,6},{6,5},{7,4},{8,11},{9,10},{10,... | collective-permute-start | bytes 196616 | tf_op jit(solution)/shard_map/ppermute | solution.py:182
  17.3 4.2 %collective-permute-start.8 = (f32[128,128]{1,0:T(8,128)S(1)}, f32[128,128]{1,0:T(8,128)S(1)}, u32[]{:S(2)}, u32[]{:S(2)}) collective-permute-start(f32[128,128]{1,0:T(8,128)S(1)} %get-tuple-element.23), channel_id=1, source_target_pairs={{0,5},{1,4},{2,7},{3,6},{4,1},{5,0},{6,3},{7,2},{8,13},{9,12},{10,... | collective-permute-start | bytes 196616 | tf_op jit(solution)/shard_map/ppermute | solution.py:182
  18.4 5.4 %collective-permute-start.9 = (f32[128,128]{1,0:T(8,128)S(1)}, f32[128,128]{1,0:T(8,128)S(1)}, u32[]{:S(2)}, u32[]{:S(2)}) collective-permute-start(f32[128,128]{1,0:T(8,128)S(1)} %get-tuple-element.23), channel_id=1, source_target_pairs={{0,6},{1,7},{2,4},{3,5},{4,2},{5,3},{6,0},{7,1},{8,14},{9,15},{10,... | collective-permute-start | bytes 196616 | tf_op jit(solution)/shard_map/ppermute | solution.py:182
  23.8 1.3 %collective-permute-start.10 = (f32[128,128]{1,0:T(8,128)S(1)}, f32[128,128]{1,0:T(8,128)S(1)}, u32[]{:S(2)}, u32[]{:S(2)}) collective-permute-start(f32[128,128]{1,0:T(8,128)S(1)} %shard_map.60.mine_ref), channel_id=1, source_target_pairs={{0,1},{1,0},{2,3},{3,2},{4,5},{5,4},{6,7},{7,6},{8,9},{9,8},{10,11... | collective-permute-start | bytes 196616 | tf_op jit(solution)/shard_map/ppermute | solution.py:182

commit v4 on v3

--- a/solution.py
+++ b/solution.py
@@ -42,15 +42,11 @@
     return dot(left, right, ((0,), (0,)))
 
 
-def chip_kernel(lines, kv_ref, kc_ref, vc_ref, part_ref):
+def chip_kernel(lines, kc_ref, vc_ref, kv_ref, part_ref, _):
     half = kc_ref.shape[1]
     head = carried_head(lines)
     own = add_partial(head, kv_ref.at[:, :half], kv_ref.at[:, half:])
     part_ref[...] = own + add_partial(head, kc_ref, vc_ref)
-
-
-def hold_kernel(*refs):
-    pass
 
 
 def combine_kernel(masks, nexts, carries, loose, *refs):
@@ -192,20 +188,20 @@
             flip = int(number == len(groups) - 1)
             step = (1 << bit, flip) if axis == "seg" else (0, (1 << bit) ^ flip)
             found += [(s ^ step[0], b ^ step[1]) for s, b in found]
-        return [found[i] for i in ((1, 3, 2) if number == 0 and len(found) > 3 else range(1, len(found)))]
+        return [found[i] for i in ((2, 3, 1) if number == 0 and len(found) > 3 else range(1, len(found)))]
 
     def on_device(queries, keys, values, gate_logit, memory_gain):
         rows, width = queries.shape
         group = width // keys.shape[1]
         square = jax.ShapeDtypeStruct((HD, HD), jnp.float32)
 
-        def pass_on(kernel, inputs, loose, passed, outs, flops):
+        def pass_on(kernel, inputs, loose, passed, outs, flops, passing=pl.BlockSpec(memory_space=pl.ANY)):
             anywhere = pl.BlockSpec(memory_space=pl.ANY)
             count, n_out = len(inputs) + len(loose), len(outs)
             return pl.pallas_call(
                 kernel,
-                in_specs=[pl.BlockSpec()] * len(inputs) + [anywhere] * (len(loose) + len(passed)),
-                out_specs=[pl.BlockSpec()] * n_out + [anywhere] * len(passed),
+                in_specs=[pl.BlockSpec()] * len(inputs) + [anywhere] * len(loose) + [passing] * len(passed),
+                out_specs=[pl.BlockSpec()] * n_out + [passing] * len(passed),
                 out_shape=outs
                 + [jax.ShapeDtypeStruct(x.shape, x.dtype) for x in passed],
                 input_output_aliases={count + i: n_out + i for i in range(len(passed))},
@@ -217,8 +213,8 @@
 
         k_core, v_core = swap(keys, 0, 1), swap(values, 0, 1)
         own = jnp.concatenate([keys, values], 1)
-        (part,) = pass_on(
-            functools.partial(chip_kernel, lines), [own, k_core, v_core], [], [], [square], 500_000_000
+        part, own = pass_on(
+            functools.partial(chip_kernel, lines), [k_core, v_core], [], [own], [square], 500_000_000, pl.BlockSpec()
         )
         gate, gain = gate_logit.reshape(1, -1), memory_gain.reshape(1, -1)
         wide = jax.ShapeDtypeStruct((rows, width), jnp.float32)
@@ -258,10 +254,7 @@
             if number == 0:
                 step = 2
                 while step < n_blk:
-                    if step == 2:
-                        news = pass_on(hold_kernel, [], [carried], fresh, [], 0)
-                    else:
-                        news = [swap(held[m], 0, step) for m in range(0, step, 2)]
+                    news = fresh if step == 2 else [swap(held[m], 0, step) for m in range(0, step, 2)]
                     for new in news:
                         held += [new, swap(new, 0, 1)]
                     step *= 2

time: 26.5 us -> 24 us (0.906)
  waiting for transfers between devices: 11.2 us -> 8.53 us
  other arithmetic: 0 us -> 0.99 us
  local copies, waits for them, and re-layouts: 1.59 us -> 0.66 us
    ppermute x11, waiting for transfers between devices: 11.2 us -> 8.53 us  [swap(): return lax.ppermute(x, both, pairs)]
    concatenate x0 -> x1, other arithmetic: none -> 0.99 us  [on_device(): own = jnp.concatenate([keys, values], 1)]
    unnamed x9 -> x6, local copies, waits for them, and re-layouts: 1.58 us -> 0.66 us
  transfers between devices with their start and end apart: 11 -> 11, of which waited for: 8 -> 9; matrix products, arithmetic and copies ran while one was open for 4% -> 4% of each run, Pallas kernels for 5% -> 5%
where the time goes in v4:
time: 24 us; the launch traced here: 23.9 us
  starting transfers between devices  10.8 us (45%)
  waiting for transfers between devices  8.53 us (36%)
  Pallas kernels  2.85 us (12%)
  other arithmetic  0.99 us (4%)
  local copies, waits for them, and re-layouts  0.66 us (3%)
    ppermute x11, starting transfers between devices, swap(): return lax.ppermute(x, both, pairs)  10.8 us
    ppermute x11, waiting for transfers between devices, swap(): return lax.ppermute(x, both, pairs)  8.53 us
    pallas_call x1, Pallas kernels, on_device(): pl.pallas_call(functools.partial(final_kernel, group, lines), out_shape=j...  1.26 us
    concatenate x1, other arithmetic, on_device(): own = jnp.concatenate([keys, values], 1)  0.99 us
    pallas_call x1, Pallas kernels, on_device(): pl.pallas_call(functools.partial(attention_kernel, group, n_blk), out_sha...  0.9 us
    unnamed x6, local copies, waits for them, and re-layouts  0.66 us
  transfers between devices with their start and end apart: 11, of which 9 were waited for; matrix products, arithmetic and copies ran while one was open for 4% of the time, Pallas kernels for 5%

profile of v4, /device:TPU:0, one launch (start us, length us, event | category | flops | bytes accessed | tf_op | source)
XLA Modules:
  0.0 23.9 jit_solution(4281437357086774036)
XLA Ops:
  0.0 0.5 %collective-permute-start = (f32[128,256]{1,0:T(8,128)}, f32[128,256]{1,0:T(8,128)S(1)}, u32[]{:S(2)}, u32[]{:S(2)}) collective-permute-start(f32[128,256]{1,0:T(8,128)} %param.6), channel_id=1, source_target_pairs={{0,1},{1,0},{2,3},{3,2},{4,5},{5,4},{6,7},{7,6},{8,9},{9,8},{10,11... | collective-permute-start | bytes 393224 | tf_op jit(solution)/shard_map/ppermute | solution.py:178
  0.5 1.0 %pad_maximum_fusion.kv_ref = f32[128,512]{1,0:T(8,128)S(1)} fusion(f32[128,256]{1,0:T(8,128)} %param.7, f32[128,256]{1,0:T(8,128)} %param.6), kind=kLoop, calls=%fused_computation | loop fusion | flops 65536 | bytes 524288 | tf_op jit(solution)/shard_map/concatenate | solution.py:215
  1.5 0.1 collective-permute-done.kc_ref.refs_2_
  1.7 0.4 %collective-permute-done.1.vc_ref.refs_3_ = f32[128,256]{1,0:T(8,128)S(1)} collective-permute-done((f32[128,256]{1,0:T(8,128)}, f32[128,256]{1,0:T(8,128)S(1)}, u32[]{:S(2)}, u32[]{:S(2)}) %collective-permute-start.1) | collective-permute-done | bytes 131104 | tf_op jit(solution)/shard_map/ppermute | solution.py:178
  2.0 0.3 %shard_map.56 = (f32[128,128]{1,0:T(8,128)S(1)}, f32[128,512]{1,0:T(8,128)S(1)}) custom-call(f32[128,256]{1,0:T(8,128)S(1)} %collective-permute-done.kc_ref.refs_2_, f32[128,256]{1,0:T(8,128)S(1)} %collective-permute-done.1.vc_ref.refs_3_, f32[128,512]{1,0:T(8,128)S(1)} %pad_maximum_fusion.kv_ref), custom_call_target="tpu_custom_call", output_to_operand_aliasing={{1}: (2, {})} | custom-call | flops 500000000 | bytes 500000 | tf_op jit(solution)/shard_map/pallas_call | solution.py:201
  2.3 2.7 %collective-permute-start.2 = (f32[128,512]{1,0:T(8,128)S(1)}, f32[128,512]{1,0:T(8,128)S(1)}, u32[]{:S(2)}, u32[]{:S(2)}) collective-permute-start(f32[128,512]{1,0:T(8,128)S(1)} %get-tuple-element.19.refs_4_), channel_id=1, source_target_pairs={{0,2},{1,3},{2,0},{3,1},{4,6},{5,7},{6,4},{7,5},{8,10},{9,11},{10,... | collective-permute-start | bytes 786440 | tf_op jit(solution)/shard_map/ppermute | solution.py:178
  5.0 2.6 %collective-permute-start.4 = (f32[128,128]{1,0:T(8,128)S(1)}, f32[128,128]{1,0:T(8,128)S(1)}, u32[]{:S(2)}, u32[]{:S(2)}) collective-permute-start(f32[128,128]{1,0:T(8,128)S(1)} %get-tuple-element.25.refs_0_), channel_id=1, source_target_pairs={{0,16},{1,17},{2,18},{3,19},{4,20},{5,21},{6,22},{7,23},{8,24},{9,... | collective-permute-start | bytes 196616 | tf_op jit(solution)/shard_map/ppermute | solution.py:178
  7.6 1.3 %collective-permute-start.5 = (f32[128,128]{1,0:T(8,128)S(1)}, f32[128,128]{1,0:T(8,128)S(1)}, u32[]{:S(2)}, u32[]{:S(2)}) collective-permute-start(f32[128,128]{1,0:T(8,128)S(1)} %get-tuple-element.25.refs_0_), channel_id=1, source_target_pairs={{0,24},{1,25},{2,26},{3,27},{4,28},{5,29},{6,30},{7,31},{8,16},{9,... | collective-permute-start | bytes 196616 | tf_op jit(solution)/shard_map/ppermute | solution.py:178
  9.0 0.2 collective-permute-start.6
  9.2 0.6 %copy-done.2 = f32[8]{0:T(128)S(1)} copy-done((f32[8]{0:T(128)S(1)}, f32[8]{0:T(128)}, u32[]{:S(2)}) %copy-start.2) | copy-done | bytes 56
  9.9 0.4 %shard_map.55 = (bf16[128,1024]{1,0:T(8,128)(2,1)S(1)}, bf16[128,1024]{1,0:T(8,128)(2,1)S(1)}, bf16[128,1024]{1,0:T(8,128)(2,1)S(1)}, bf16[128,1024]{1,0:T(8,128...) custom-call(f32[128,1024]{1,0:T(8,128)S(1)} %copy-done, f32[1,8]{1,0:T(1,128)S(1)} %bitcast.3, f32[1,1024]{1,0:T(1,128)S(1)} %bitcast.2), custom_call_target="tpu_custom_call" | custom-call | flops 1000000 | bytes 100000 | tf_op jit(solution)/shard_map/pallas_call | solution.py:224
  10.2 1.6 %collective-permute-done.2.refs_5_ = f32[128,512]{1,0:T(8,128)S(1)} collective-permute-done((f32[128,512]{1,0:T(8,128)S(1)}, f32[128,512]{1,0:T(8,128)S(1)}, u32[]{:S(2)}, u32[]{:S(2)}) %collective-permute-start.2) | collective-permute-done | bytes 262176 | tf_op jit(solution)/shard_map/ppermute | solution.py:178
  11.8 0.9 %collective-permute-done.4.refs_1_ = f32[128,128]{1,0:T(8,128)S(1)} collective-permute-done((f32[128,128]{1,0:T(8,128)S(1)}, f32[128,128]{1,0:T(8,128)S(1)}, u32[]{:S(2)}, u32[]{:S(2)}) %collective-permute-start.4) | collective-permute-done | bytes 65568 | tf_op jit(solution)/shard_map/ppermute | solution.py:178
  12.7 1.2 %collective-permute-done.5.refs_2_ = f32[128,128]{1,0:T(8,128)S(1)} collective-permute-done((f32[128,128]{1,0:T(8,128)S(1)}, f32[128,128]{1,0:T(8,128)S(1)}, u32[]{:S(2)}, u32[]{:S(2)}) %collective-permute-start.5) | collective-permute-done | bytes 65568 | tf_op jit(solution)/shard_map/ppermute | solution.py:178
  13.9 0.3 %collective-permute-done.6.refs_3_ = f32[128,128]{1,0:T(8,128)S(1)} collective-permute-done((f32[128,128]{1,0:T(8,128)S(1)}, f32[128,128]{1,0:T(8,128)S(1)}, u32[]{:S(2)}, u32[]{:S(2)}) %collective-permute-start.6) | collective-permute-done | bytes 65568 | tf_op jit(solution)/shard_map/ppermute | solution.py:178
  14.3 0.1 collective-permute-start.7
  14.3 1.8 %collective-permute-start.8 = (f32[128,128]{1,0:T(8,128)S(1)}, f32[128,128]{1,0:T(8,128)S(1)}, u32[]{:S(2)}, u32[]{:S(2)}) collective-permute-start(f32[128,128]{1,0:T(8,128)S(1)} %get-tuple-element.27), channel_id=1, source_target_pairs={{0,5},{1,4},{2,7},{3,6},{4,1},{5,0},{6,3},{7,2},{8,13},{9,12},{10,... | collective-permute-start | bytes 196616 | tf_op jit(solution)/shard_map/ppermute | solution.py:178
  16.1 1.4 %collective-permute-start.9 = (f32[128,128]{1,0:T(8,128)S(1)}, f32[128,128]{1,0:T(8,128)S(1)}, u32[]{:S(2)}, u32[]{:S(2)}) collective-permute-start(f32[128,128]{1,0:T(8,128)S(1)} %get-tuple-element.27), channel_id=1, source_target_pairs={{0,6},{1,7},{2,4},{3,5},{4,2},{5,3},{6,0},{7,1},{8,14},{9,15},{10,... | collective-permute-start | bytes 196616 | tf_op jit(solution)/shard_map/ppermute | solution.py:178
  17.5 0.9 %shard_map.57 = (f32[128,1024]{1,0:T(8,128)S(1)}, f32[8,128]{1,0:T(8,128)S(1)}) custom-call(bf16[128,1024]{1,0:T(8,128)(2,1)S(1)} %get-tuple-element.17.refs_0_, bf16[128,1024]{1,0:T(8,128)(2,1)S(1)} %get-tuple-element.18.refs_1_, f32[128,256]{1,0:T(8,128)S(1)} %collective-permute-done.kc_ref.refs_2_, f32[128,256]{1,0:T(8,128)S(1)} %collective-permute-done.1.vc_ref.refs_3_, ...), custom_call_target="tpu_custom_call" | custom-call | flops 1000000 | bytes 100000 | tf_op jit(solution)/shard_map/pallas_call | solution.py:261
  18.5 0.9 %collective-permute-done.8.refs_2_ = f32[128,128]{1,0:T(8,128)S(1)} collective-permute-done((f32[128,128]{1,0:T(8,128)S(1)}, f32[128,128]{1,0:T(8,128)S(1)}, u32[]{:S(2)}, u32[]{:S(2)}) %collective-permute-start.8) | collective-permute-done | bytes 65568 | tf_op jit(solution)/shard_map/ppermute | solution.py:178
  19.3 1.9 %collective-permute-done.9.refs_3_ = f32[128,128]{1,0:T(8,128)S(1)} collective-permute-done((f32[128,128]{1,0:T(8,128)S(1)}, f32[128,128]{1,0:T(8,128)S(1)}, u32[]{:S(2)}, u32[]{:S(2)}) %collective-permute-start.9) | collective-permute-done | bytes 65568 | tf_op jit(solution)/shard_map/ppermute | solution.py:178
  21.3 0.1 collective-permute-start.10
  21.4 1.2 %collective-permute-done.10.other_ref = f32[128,128]{1,0:T(8,128)S(1)} collective-permute-done((f32[128,128]{1,0:T(8,128)S(1)}, f32[128,128]{1,0:T(8,128)S(1)}, u32[]{:S(2)}, u32[]{:S(2)}) %collective-permute-start.10) | collective-permute-done | bytes 65568 | tf_op jit(solution)/shard_map/ppermute | solution.py:178
  22.6 1.3 %shard_map.60 = f32[128,1024]{1,0:T(8,128)} custom-call(f32[128,1024]{1,0:T(8,128)S(1)} %get-tuple-element.21.att_ref, bf16[128,1024]{1,0:T(8,128)(2,1)S(1)} %get-tuple-element.22.sh_ref, bf16[128,1024]{1,0:T(8,128)(2,1)S(1)} %get-tuple-element.23.sl_ref, f32[1,1024]{1,0:T(1,128)S(1)} %get-tuple-element.24.refs_4_.mult_ref, ...), custom_call_target="tpu_custom_call" | custom-call | tf_op jit(solution)/shard_map/pallas_call | solution.py:271
  (11 shorter events, 0.1 us)
Async XLA Ops:
  0.0 1.6 %collective-permute-start = (f32[128,256]{1,0:T(8,128)}, f32[128,256]{1,0:T(8,128)S(1)}, u32[]{:S(2)}, u32[]{:S(2)}) collective-permute-start(f32[128,256]{1,0:T(8,128)} %param.6), channel_id=1, source_target_pairs={{0,1},{1,0},{2,3},{3,2},{4,5},{5,4},{6,7},{7,6},{8,9},{9,8},{10,11... | collective-permute-start | bytes 393224 | tf_op jit(solution)/shard_map/ppermute | solution.py:178
  0.5 1.6 %collective-permute-start.1 = (f32[128,256]{1,0:T(8,128)}, f32[128,256]{1,0:T(8,128)S(1)}, u32[]{:S(2)}, u32[]{:S(2)}) collective-permute-start(f32[128,256]{1,0:T(8,128)} %param.7), channel_id=1, source_target_pairs={{0,1},{1,0},{2,3},{3,2},{4,5},{5,4},{6,7},{7,6},{8,9},{9,8},{10,11... | collective-permute-start | bytes 393224 | tf_op jit(solution)/shard_map/ppermute | solution.py:178
  1.5 7.7 %copy-start = (f32[128,1024]{1,0:T(8,128)S(1)}, f32[128,1024]{1,0:T(8,128)}, u32[]{:S(2)}) copy-start(f32[128,1024]{1,0:T(8,128)} %refs_0_.1) | copy-start | bytes 1572868
  2.3 6.9 %copy-start.1 = (f32[1024]{0:T(1024)S(1)}, f32[1024]{0:T(1024)}, u32[]{:S(2)}) copy-start(f32[1024]{0:T(1024)} %param.9) | copy-start | bytes 12292
  2.3 9.5 %collective-permute-start.2 = (f32[128,512]{1,0:T(8,128)S(1)}, f32[128,512]{1,0:T(8,128)S(1)}, u32[]{:S(2)}, u32[]{:S(2)}) collective-permute-start(f32[128,512]{1,0:T(8,128)S(1)} %get-tuple-element.19.refs_4_), channel_id=1, source_target_pairs={{0,2},{1,3},{2,0},{3,1},{4,6},{5,7},{6,4},{7,5},{8,10},{9,11},{10,... | collective-permute-start | bytes 786440 | tf_op jit(solution)/shard_map/ppermute | solution.py:178
  5.0 7.7 %collective-permute-start.4 = (f32[128,128]{1,0:T(8,128)S(1)}, f32[128,128]{1,0:T(8,128)S(1)}, u32[]{:S(2)}, u32[]{:S(2)}) collective-permute-start(f32[128,128]{1,0:T(8,128)S(1)} %get-tuple-element.25.refs_0_), channel_id=1, source_target_pairs={{0,16},{1,17},{2,18},{3,19},{4,20},{5,21},{6,22},{7,23},{8,24},{9,... | collective-permute-start | bytes 196616 | tf_op jit(solution)/shard_map/ppermute | solution.py:178
  7.6 6.3 %collective-permute-start.5 = (f32[128,128]{1,0:T(8,128)S(1)}, f32[128,128]{1,0:T(8,128)S(1)}, u32[]{:S(2)}, u32[]{:S(2)}) collective-permute-start(f32[128,128]{1,0:T(8,128)S(1)} %get-tuple-element.25.refs_0_), channel_id=1, source_target_pairs={{0,24},{1,25},{2,26},{3,27},{4,28},{5,29},{6,30},{7,31},{8,16},{9,... | collective-permute-start | bytes 196616 | tf_op jit(solution)/shard_map/ppermute | solution.py:178
  9.0 5.3 %collective-permute-start.6 = (f32[128,128]{1,0:T(8,128)S(1)}, f32[128,128]{1,0:T(8,128)S(1)}, u32[]{:S(2)}, u32[]{:S(2)}) collective-permute-start(f32[128,128]{1,0:T(8,128)S(1)} %get-tuple-element.25.refs_0_), channel_id=1, source_target_pairs={{0,8},{1,9},{2,10},{3,11},{4,12},{5,13},{6,14},{7,15},{8,0},{9,1},... | collective-permute-start | bytes 196616 | tf_op jit(solution)/shard_map/ppermute | solution.py:178
  9.2 0.7 %copy-start.2 = (f32[8]{0:T(128)S(1)}, f32[8]{0:T(128)}, u32[]{:S(2)}) copy-start(f32[8]{0:T(128)} %param.8) | copy-start | bytes 100
  11.8 5.7 %collective-permute-start.3 = (f32[128,512]{1,0:T(8,128)S(1)}, f32[128,512]{1,0:T(8,128)S(1)}, u32[]{:S(2)}, u32[]{:S(2)}) collective-permute-start(f32[128,512]{1,0:T(8,128)S(1)} %collective-permute-done.2.refs_5_), channel_id=1, source_target_pairs={{0,1},{1,0},{2,3},{3,2},{4,5},{5,4},{6,7},{7,6},{8,9},{9,8},{10,11... | collective-permute-start | bytes 786440 | tf_op jit(solution)/shard_map/ppermute | solution.py:178
  14.3 4.2 %collective-permute-start.7 = (f32[128,128]{1,0:T(8,128)S(1)}, f32[128,128]{1,0:T(8,128)S(1)}, u32[]{:S(2)}, u32[]{:S(2)}) collective-permute-start(f32[128,128]{1,0:T(8,128)S(1)} %get-tuple-element.26.refs_4_), channel_id=1, source_target_pairs={{0,3},{1,2},{2,1},{3,0},{4,7},{5,6},{6,5},{7,4},{8,11},{9,10},{10,... | collective-permute-start | bytes 196616 | tf_op jit(solution)/shard_map/ppermute | solution.py:178
  14.3 5.0 %collective-permute-start.8 = (f32[128,128]{1,0:T(8,128)S(1)}, f32[128,128]{1,0:T(8,128)S(1)}, u32[]{:S(2)}, u32[]{:S(2)}) collective-permute-start(f32[128,128]{1,0:T(8,128)S(1)} %get-tuple-element.27), channel_id=1, source_target_pairs={{0,5},{1,4},{2,7},{3,6},{4,1},{5,0},{6,3},{7,2},{8,13},{9,12},{10,... | collective-permute-start | bytes 196616 | tf_op jit(solution)/shard_map/ppermute | solution.py:178
  16.1 5.2 %collective-permute-start.9 = (f32[128,128]{1,0:T(8,128)S(1)}, f32[128,128]{1,0:T(8,128)S(1)}, u32[]{:S(2)}, u32[]{:S(2)}) collective-permute-start(f32[128,128]{1,0:T(8,128)S(1)} %get-tuple-element.27), channel_id=1, source_target_pairs={{0,6},{1,7},{2,4},{3,5},{4,2},{5,3},{6,0},{7,1},{8,14},{9,15},{10,... | collective-permute-start | bytes 196616 | tf_op jit(solution)/shard_map/ppermute | solution.py:178
  21.3 1.3 %collective-permute-start.10 = (f32[128,128]{1,0:T(8,128)S(1)}, f32[128,128]{1,0:T(8,128)S(1)}, u32[]{:S(2)}, u32[]{:S(2)}) collective-permute-start(f32[128,128]{1,0:T(8,128)S(1)} %shard_map.59.mine_ref), channel_id=1, source_target_pairs={{0,1},{1,0},{2,3},{3,2},{4,5},{5,4},{6,7},{7,6},{8,9},{9,8},{10,11... | collective-permute-start | bytes 196616 | tf_op jit(solution)/shard_map/ppermute | solution.py:178

commit v5 on v4

--- a/solution.py
+++ b/solution.py
@@ -188,7 +188,7 @@
             flip = int(number == len(groups) - 1)
             step = (1 << bit, flip) if axis == "seg" else (0, (1 << bit) ^ flip)
             found += [(s ^ step[0], b ^ step[1]) for s, b in found]
-        return [found[i] for i in ((2, 3, 1) if number == 0 and len(found) > 3 else range(1, len(found)))]
+        return [found[i] for i in ((2, 3, 1) if number == 0 and len(found) > 3 else (3, 2, 1) if len(found) == 4 else range(1, len(found)))]
 
     def on_device(queries, keys, values, gate_logit, memory_gain):
         rows, width = queries.shape

time: 24 us -> 23.1 us (0.963)
  waiting for transfers between devices: 8.53 us -> 7.13 us
  starting transfers between devices: 10.8 us -> 11.3 us
    ppermute x11, waiting for transfers between devices: 8.53 us -> 7.13 us  [swap(): return lax.ppermute(x, both, pairs)]
    ppermute x11, starting transfers between devices: 10.8 us -> 11.3 us  [swap(): return lax.ppermute(x, both, pairs)]
  transfers between devices with their start and end apart: 11 -> 11, of which waited for: 9 -> 9; matrix products, arithmetic and copies ran while one was open for 4% -> 4% of each run, Pallas kernels for 5% -> 6%
where the time goes in v5:
time: 23.1 us; the launch traced here: 23 us
  starting transfers between devices  11.3 us (49%)
  waiting for transfers between devices  7.13 us (31%)
  Pallas kernels  2.85 us (12%)
  other arithmetic  0.99 us (4%)
  local copies, waits for them, and re-layouts  0.66 us (3%)
    ppermute x11, starting transfers between devices, swap(): return lax.ppermute(x, both, pairs)  11.3 us
    ppermute x11, waiting for transfers between devices, swap(): return lax.ppermute(x, both, pairs)  7.13 us
    pallas_call x1, Pallas kernels, on_device(): pl.pallas_call(functools.partial(final_kernel, group, lines), out_shape=j...  1.26 us
    concatenate x1, other arithmetic, on_device(): own = jnp.concatenate([keys, values], 1)  0.99 us
    pallas_call x1, Pallas kernels, on_device(): pl.pallas_call(functools.partial(attention_kernel, group, n_blk), out_sha...  0.9 us
    unnamed x6, local copies, waits for them, and re-layouts  0.66 us
  transfers between devices with their start and end apart: 11, of which 9 were waited for; matrix products, arithmetic and copies ran while one was open for 4% of the time, Pallas kernels for 6%

profile of v5, /device:TPU:0, one launch (start us, length us, event | category | flops | bytes accessed | tf_op | source)
XLA Modules:
  0.0 23.0 jit_solution(12146402313710565370)
XLA Ops:
  0.0 0.5 %collective-permute-start = (f32[128,256]{1,0:T(8,128)}, f32[128,256]{1,0:T(8,128)S(1)}, u32[]{:S(2)}, u32[]{:S(2)}) collective-permute-start(f32[128,256]{1,0:T(8,128)} %param.6), channel_id=1, source_target_pairs={{0,1},{1,0},{2,3},{3,2},{4,5},{5,4},{6,7},{7,6},{8,9},{9,8},{10,11... | collective-permute-start | bytes 393224 | tf_op jit(solution)/shard_map/ppermute | solution.py:178
  0.5 0.1 collective-permute-start.1
  0.5 1.0 %pad_maximum_fusion.kv_ref = f32[128,512]{1,0:T(8,128)S(1)} fusion(f32[128,256]{1,0:T(8,128)} %param.7, f32[128,256]{1,0:T(8,128)} %param.6), kind=kLoop, calls=%fused_computation | loop fusion | flops 65536 | bytes 524288 | tf_op jit(solution)/shard_map/concatenate | solution.py:215
  1.5 0.1 collective-permute-done.kc_ref.refs_2_
  1.7 0.4 %collective-permute-done.1.vc_ref.refs_3_ = f32[128,256]{1,0:T(8,128)S(1)} collective-permute-done((f32[128,256]{1,0:T(8,128)}, f32[128,256]{1,0:T(8,128)S(1)}, u32[]{:S(2)}, u32[]{:S(2)}) %collective-permute-start.1) | collective-permute-done | bytes 131104 | tf_op jit(solution)/shard_map/ppermute | solution.py:178
  2.0 0.3 %shard_map.56 = (f32[128,128]{1,0:T(8,128)S(1)}, f32[128,512]{1,0:T(8,128)S(1)}) custom-call(f32[128,256]{1,0:T(8,128)S(1)} %collective-permute-done.kc_ref.refs_2_, f32[128,256]{1,0:T(8,128)S(1)} %collective-permute-done.1.vc_ref.refs_3_, f32[128,512]{1,0:T(8,128)S(1)} %pad_maximum_fusion.kv_ref), custom_call_target="tpu_custom_call", output_to_operand_aliasing={{1}: (2, {})} | custom-call | flops 500000000 | bytes 500000 | tf_op jit(solution)/shard_map/pallas_call | solution.py:201
  2.3 2.7 %collective-permute-start.2 = (f32[128,512]{1,0:T(8,128)S(1)}, f32[128,512]{1,0:T(8,128)S(1)}, u32[]{:S(2)}, u32[]{:S(2)}) collective-permute-start(f32[128,512]{1,0:T(8,128)S(1)} %get-tuple-element.19.refs_4_), channel_id=1, source_target_pairs={{0,2},{1,3},{2,0},{3,1},{4,6},{5,7},{6,4},{7,5},{8,10},{9,11},{10,... | collective-permute-start | bytes 786440 | tf_op jit(solution)/shard_map/ppermute | solution.py:178
  5.0 2.6 %collective-permute-start.4 = (f32[128,128]{1,0:T(8,128)S(1)}, f32[128,128]{1,0:T(8,128)S(1)}, u32[]{:S(2)}, u32[]{:S(2)}) collective-permute-start(f32[128,128]{1,0:T(8,128)S(1)} %get-tuple-element.25.refs_0_), channel_id=1, source_target_pairs={{0,16},{1,17},{2,18},{3,19},{4,20},{5,21},{6,22},{7,23},{8,24},{9,... | collective-permute-start | bytes 196616 | tf_op jit(solution)/shard_map/ppermute | solution.py:178
  7.6 1.3 %collective-permute-start.5 = (f32[128,128]{1,0:T(8,128)S(1)}, f32[128,128]{1,0:T(8,128)S(1)}, u32[]{:S(2)}, u32[]{:S(2)}) collective-permute-start(f32[128,128]{1,0:T(8,128)S(1)} %get-tuple-element.25.refs_0_), channel_id=1, source_target_pairs={{0,24},{1,25},{2,26},{3,27},{4,28},{5,29},{6,30},{7,31},{8,16},{9,... | collective-permute-start | bytes 196616 | tf_op jit(solution)/shard_map/ppermute | solution.py:178
  9.0 0.2 %collective-permute-start.6 = (f32[128,128]{1,0:T(8,128)S(1)}, f32[128,128]{1,0:T(8,128)S(1)}, u32[]{:S(2)}, u32[]{:S(2)}) collective-permute-start(f32[128,128]{1,0:T(8,128)S(1)} %get-tuple-element.25.refs_0_), channel_id=1, source_target_pairs={{0,8},{1,9},{2,10},{3,11},{4,12},{5,13},{6,14},{7,15},{8,0},{9,1},... | collective-permute-start | bytes 196616 | tf_op jit(solution)/shard_map/ppermute | solution.py:178
  9.2 0.6 %copy-done.2 = f32[8]{0:T(128)S(1)} copy-done((f32[8]{0:T(128)S(1)}, f32[8]{0:T(128)}, u32[]{:S(2)}) %copy-start.2) | copy-done | bytes 56
  9.9 0.4 %shard_map.55 = (bf16[128,1024]{1,0:T(8,128)(2,1)S(1)}, bf16[128,1024]{1,0:T(8,128)(2,1)S(1)}, bf16[128,1024]{1,0:T(8,128)(2,1)S(1)}, bf16[128,1024]{1,0:T(8,128...) custom-call(f32[128,1024]{1,0:T(8,128)S(1)} %copy-done, f32[1,8]{1,0:T(1,128)S(1)} %bitcast.3, f32[1,1024]{1,0:T(1,128)S(1)} %bitcast.2), custom_call_target="tpu_custom_call" | custom-call | flops 1000000 | bytes 100000 | tf_op jit(solution)/shard_map/pallas_call | solution.py:224
  10.2 1.6 %collective-permute-done.2.refs_5_ = f32[128,512]{1,0:T(8,128)S(1)} collective-permute-done((f32[128,512]{1,0:T(8,128)S(1)}, f32[128,512]{1,0:T(8,128)S(1)}, u32[]{:S(2)}, u32[]{:S(2)}) %collective-permute-start.2) | collective-permute-done | bytes 262176 | tf_op jit(solution)/shard_map/ppermute | solution.py:178
  11.8 0.9 %collective-permute-done.4.refs_1_ = f32[128,128]{1,0:T(8,128)S(1)} collective-permute-done((f32[128,128]{1,0:T(8,128)S(1)}, f32[128,128]{1,0:T(8,128)S(1)}, u32[]{:S(2)}, u32[]{:S(2)}) %collective-permute-start.4) | collective-permute-done | bytes 65568 | tf_op jit(solution)/shard_map/ppermute | solution.py:178
  12.7 1.2 %collective-permute-done.5.refs_2_ = f32[128,128]{1,0:T(8,128)S(1)} collective-permute-done((f32[128,128]{1,0:T(8,128)S(1)}, f32[128,128]{1,0:T(8,128)S(1)}, u32[]{:S(2)}, u32[]{:S(2)}) %collective-permute-start.5) | collective-permute-done | bytes 65568 | tf_op jit(solution)/shard_map/ppermute | solution.py:178
  13.9 0.3 %collective-permute-done.6.refs_3_ = f32[128,128]{1,0:T(8,128)S(1)} collective-permute-done((f32[128,128]{1,0:T(8,128)S(1)}, f32[128,128]{1,0:T(8,128)S(1)}, u32[]{:S(2)}, u32[]{:S(2)}) %collective-permute-start.6) | collective-permute-done | bytes 65568 | tf_op jit(solution)/shard_map/ppermute | solution.py:178
  14.3 1.6 %collective-permute-start.7 = (f32[128,128]{1,0:T(8,128)S(1)}, f32[128,128]{1,0:T(8,128)S(1)}, u32[]{:S(2)}, u32[]{:S(2)}) collective-permute-start(f32[128,128]{1,0:T(8,128)S(1)} %get-tuple-element.26), channel_id=1, source_target_pairs={{0,6},{1,7},{2,4},{3,5},{4,2},{5,3},{6,0},{7,1},{8,14},{9,15},{10,... | collective-permute-start | bytes 196616 | tf_op jit(solution)/shard_map/ppermute | solution.py:178
  15.8 1.7 %collective-permute-start.9 = (f32[128,128]{1,0:T(8,128)S(1)}, f32[128,128]{1,0:T(8,128)S(1)}, u32[]{:S(2)}, u32[]{:S(2)}) collective-permute-start(f32[128,128]{1,0:T(8,128)S(1)} %get-tuple-element.27.refs_4_), channel_id=1, source_target_pairs={{0,3},{1,2},{2,1},{3,0},{4,7},{5,6},{6,5},{7,4},{8,11},{9,10},{10,... | collective-permute-start | bytes 196616 | tf_op jit(solution)/shard_map/ppermute | solution.py:178
  17.5 0.9 %shard_map.57 = (f32[128,1024]{1,0:T(8,128)S(1)}, f32[8,128]{1,0:T(8,128)S(1)}) custom-call(bf16[128,1024]{1,0:T(8,128)(2,1)S(1)} %get-tuple-element.17.refs_0_, bf16[128,1024]{1,0:T(8,128)(2,1)S(1)} %get-tuple-element.18.refs_1_, f32[128,256]{1,0:T(8,128)S(1)} %collective-permute-done.kc_ref.refs_2_, f32[128,256]{1,0:T(8,128)S(1)} %collective-permute-done.1.vc_ref.refs_3_, ...), custom_call_target="tpu_custom_call" | custom-call | flops 1000000 | bytes 100000 | tf_op jit(solution)/shard_map/pallas_call | solution.py:261
  18.5 1.1 %collective-permute-done.7.refs_1_ = f32[128,128]{1,0:T(8,128)S(1)} collective-permute-done((f32[128,128]{1,0:T(8,128)S(1)}, f32[128,128]{1,0:T(8,128)S(1)}, u32[]{:S(2)}, u32[]{:S(2)}) %collective-permute-start.7) | collective-permute-done | bytes 65568 | tf_op jit(solution)/shard_map/ppermute | solution.py:178
  19.6 0.6 %collective-permute-done.8.refs_2_ = f32[128,128]{1,0:T(8,128)S(1)} collective-permute-done((f32[128,128]{1,0:T(8,128)S(1)}, f32[128,128]{1,0:T(8,128)S(1)}, u32[]{:S(2)}, u32[]{:S(2)}) %collective-permute-start.8) | collective-permute-done | bytes 65568 | tf_op jit(solution)/shard_map/ppermute | solution.py:178
  20.2 0.6 %collective-permute-start.10 = (f32[128,128]{1,0:T(8,128)S(1)}, f32[128,128]{1,0:T(8,128)S(1)}, u32[]{:S(2)}, u32[]{:S(2)}) collective-permute-start(f32[128,128]{1,0:T(8,128)S(1)} %shard_map.59.mine_ref), channel_id=1, source_target_pairs={{0,1},{1,0},{2,3},{3,2},{4,5},{5,4},{6,7},{7,6},{8,9},{9,8},{10,11... | collective-permute-start | bytes 196616 | tf_op jit(solution)/shard_map/ppermute | solution.py:178
  20.8 0.9 %collective-permute-done.10.other_ref = f32[128,128]{1,0:T(8,128)S(1)} collective-permute-done((f32[128,128]{1,0:T(8,128)S(1)}, f32[128,128]{1,0:T(8,128)S(1)}, u32[]{:S(2)}, u32[]{:S(2)}) %collective-permute-start.10) | collective-permute-done | bytes 65568 | tf_op jit(solution)/shard_map/ppermute | solution.py:178
  21.7 1.3 %shard_map.60 = f32[128,1024]{1,0:T(8,128)} custom-call(f32[128,1024]{1,0:T(8,128)S(1)} %get-tuple-element.21.att_ref, bf16[128,1024]{1,0:T(8,128)(2,1)S(1)} %get-tuple-element.22.sh_ref, bf16[128,1024]{1,0:T(8,128)(2,1)S(1)} %get-tuple-element.23.sl_ref, f32[1,1024]{1,0:T(1,128)S(1)} %get-tuple-element.24.refs_4_.mult_ref, ...), custom_call_target="tpu_custom_call" | custom-call | tf_op jit(solution)/shard_map/pallas_call | solution.py:271
  (11 shorter events, 0.1 us)
Async XLA Ops:
  0.0 1.6 %collective-permute-start = (f32[128,256]{1,0:T(8,128)}, f32[128,256]{1,0:T(8,128)S(1)}, u32[]{:S(2)}, u32[]{:S(2)}) collective-permute-start(f32[128,256]{1,0:T(8,128)} %param.6), channel_id=1, source_target_pairs={{0,1},{1,0},{2,3},{3,2},{4,5},{5,4},{6,7},{7,6},{8,9},{9,8},{10,11... | collective-permute-start | bytes 393224 | tf_op jit(solution)/shard_map/ppermute | solution.py:178
  0.5 1.6 %collective-permute-start.1 = (f32[128,256]{1,0:T(8,128)}, f32[128,256]{1,0:T(8,128)S(1)}, u32[]{:S(2)}, u32[]{:S(2)}) collective-permute-start(f32[128,256]{1,0:T(8,128)} %param.7), channel_id=1, source_target_pairs={{0,1},{1,0},{2,3},{3,2},{4,5},{5,4},{6,7},{7,6},{8,9},{9,8},{10,11... | collective-permute-start | bytes 393224 | tf_op jit(solution)/shard_map/ppermute | solution.py:178
  1.5 7.7 %copy-start = (f32[128,1024]{1,0:T(8,128)S(1)}, f32[128,1024]{1,0:T(8,128)}, u32[]{:S(2)}) copy-start(f32[128,1024]{1,0:T(8,128)} %refs_0_.1) | copy-start | bytes 1572868
  2.3 6.9 %copy-start.1 = (f32[1024]{0:T(1024)S(1)}, f32[1024]{0:T(1024)}, u32[]{:S(2)}) copy-start(f32[1024]{0:T(1024)} %param.9) | copy-start | bytes 12292
  2.3 9.5 %collective-permute-start.2 = (f32[128,512]{1,0:T(8,128)S(1)}, f32[128,512]{1,0:T(8,128)S(1)}, u32[]{:S(2)}, u32[]{:S(2)}) collective-permute-start(f32[128,512]{1,0:T(8,128)S(1)} %get-tuple-element.19.refs_4_), channel_id=1, source_target_pairs={{0,2},{1,3},{2,0},{3,1},{4,6},{5,7},{6,4},{7,5},{8,10},{9,11},{10,... | collective-permute-start | bytes 786440 | tf_op jit(solution)/shard_map/ppermute | solution.py:178
  5.0 7.7 %collective-permute-start.4 = (f32[128,128]{1,0:T(8,128)S(1)}, f32[128,128]{1,0:T(8,128)S(1)}, u32[]{:S(2)}, u32[]{:S(2)}) collective-permute-start(f32[128,128]{1,0:T(8,128)S(1)} %get-tuple-element.25.refs_0_), channel_id=1, source_target_pairs={{0,16},{1,17},{2,18},{3,19},{4,20},{5,21},{6,22},{7,23},{8,24},{9,... | collective-permute-start | bytes 196616 | tf_op jit(solution)/shard_map/ppermute | solution.py:178
  7.6 6.3 %collective-permute-start.5 = (f32[128,128]{1,0:T(8,128)S(1)}, f32[128,128]{1,0:T(8,128)S(1)}, u32[]{:S(2)}, u32[]{:S(2)}) collective-permute-start(f32[128,128]{1,0:T(8,128)S(1)} %get-tuple-element.25.refs_0_), channel_id=1, source_target_pairs={{0,24},{1,25},{2,26},{3,27},{4,28},{5,29},{6,30},{7,31},{8,16},{9,... | collective-permute-start | bytes 196616 | tf_op jit(solution)/shard_map/ppermute | solution.py:178
  9.0 5.3 %collective-permute-start.6 = (f32[128,128]{1,0:T(8,128)S(1)}, f32[128,128]{1,0:T(8,128)S(1)}, u32[]{:S(2)}, u32[]{:S(2)}) collective-permute-start(f32[128,128]{1,0:T(8,128)S(1)} %get-tuple-element.25.refs_0_), channel_id=1, source_target_pairs={{0,8},{1,9},{2,10},{3,11},{4,12},{5,13},{6,14},{7,15},{8,0},{9,1},... | collective-permute-start | bytes 196616 | tf_op jit(solution)/shard_map/ppermute | solution.py:178
  9.2 0.7 %copy-start.2 = (f32[8]{0:T(128)S(1)}, f32[8]{0:T(128)}, u32[]{:S(2)}) copy-start(f32[8]{0:T(128)} %param.8) | copy-start | bytes 100
  11.8 5.7 %collective-permute-start.3 = (f32[128,512]{1,0:T(8,128)S(1)}, f32[128,512]{1,0:T(8,128)S(1)}, u32[]{:S(2)}, u32[]{:S(2)}) collective-permute-start(f32[128,512]{1,0:T(8,128)S(1)} %collective-permute-done.2.refs_5_), channel_id=1, source_target_pairs={{0,1},{1,0},{2,3},{3,2},{4,5},{5,4},{6,7},{7,6},{8,9},{9,8},{10,11... | collective-permute-start | bytes 786440 | tf_op jit(solution)/shard_map/ppermute | solution.py:178
  14.3 5.3 %collective-permute-start.7 = (f32[128,128]{1,0:T(8,128)S(1)}, f32[128,128]{1,0:T(8,128)S(1)}, u32[]{:S(2)}, u32[]{:S(2)}) collective-permute-start(f32[128,128]{1,0:T(8,128)S(1)} %get-tuple-element.26), channel_id=1, source_target_pairs={{0,6},{1,7},{2,4},{3,5},{4,2},{5,3},{6,0},{7,1},{8,14},{9,15},{10,... | collective-permute-start | bytes 196616 | tf_op jit(solution)/shard_map/ppermute | solution.py:178
  15.8 4.4 %collective-permute-start.8 = (f32[128,128]{1,0:T(8,128)S(1)}, f32[128,128]{1,0:T(8,128)S(1)}, u32[]{:S(2)}, u32[]{:S(2)}) collective-permute-start(f32[128,128]{1,0:T(8,128)S(1)} %get-tuple-element.26), channel_id=1, source_target_pairs={{0,5},{1,4},{2,7},{3,6},{4,1},{5,0},{6,3},{7,2},{8,13},{9,12},{10,... | collective-permute-start | bytes 196616 | tf_op jit(solution)/shard_map/ppermute | solution.py:178
  15.8 4.4 %collective-permute-start.9 = (f32[128,128]{1,0:T(8,128)S(1)}, f32[128,128]{1,0:T(8,128)S(1)}, u32[]{:S(2)}, u32[]{:S(2)}) collective-permute-start(f32[128,128]{1,0:T(8,128)S(1)} %get-tuple-element.27.refs_4_), channel_id=1, source_target_pairs={{0,3},{1,2},{2,1},{3,0},{4,7},{5,6},{6,5},{7,4},{8,11},{9,10},{10,... | collective-permute-start | bytes 196616 | tf_op jit(solution)/shard_map/ppermute | solution.py:178
  20.2 1.5 %collective-permute-start.10 = (f32[128,128]{1,0:T(8,128)S(1)}, f32[128,128]{1,0:T(8,128)S(1)}, u32[]{:S(2)}, u32[]{:S(2)}) collective-permute-start(f32[128,128]{1,0:T(8,128)S(1)} %shard_map.59.mine_ref), channel_id=1, source_target_pairs={{0,1},{1,0},{2,3},{3,2},{4,5},{5,4},{6,7},{7,6},{8,9},{9,8},{10,11... | collective-permute-start | bytes 196616 | tf_op jit(solution)/shard_map/ppermute | solution.py:178

commit v6 on v5

--- a/solution.py
+++ b/solution.py
@@ -42,11 +42,12 @@
     return dot(left, right, ((0,), (0,)))
 
 
-def chip_kernel(lines, kc_ref, vc_ref, kv_ref, part_ref, _):
+def chip_kernel(lines, kc_ref, vc_ref, kv_ref, part_ref, kv_out):
     half = kc_ref.shape[1]
     head = carried_head(lines)
     own = add_partial(head, kv_ref.at[:, :half], kv_ref.at[:, half:])
     part_ref[...] = own + add_partial(head, kc_ref, vc_ref)
+    kv_out[...] = kv_ref[...]
 
 
 def combine_kernel(masks, nexts, carries, loose, *refs):

time: 23.1 us -> 23.2 us (level)
  no operation moved by 1% of the time
where the time goes in v6:
time: 23.2 us; the launch traced here: 23 us
  starting transfers between devices  11.3 us (49%)
  waiting for transfers between devices  7.14 us (31%)
  Pallas kernels  2.87 us (12%)
  other arithmetic  0.99 us (4%)
  local copies, waits for them, and re-layouts  0.66 us (3%)
    ppermute x11, starting transfers between devices, swap(): return lax.ppermute(x, both, pairs)  11.3 us
    ppermute x11, waiting for transfers between devices, swap(): return lax.ppermute(x, both, pairs)  7.14 us
    pallas_call x1, Pallas kernels, on_device(): pl.pallas_call(functools.partial(final_kernel, group, lines), out_shape=j...  1.26 us
    concatenate x1, other arithmetic, on_device(): own = jnp.concatenate([keys, values], 1)  0.99 us
    pallas_call x1, Pallas kernels, on_device(): pl.pallas_call(functools.partial(attention_kernel, group, n_blk), out_sha...  0.9 us
    unnamed x6, local copies, waits for them, and re-layouts  0.66 us
  transfers between devices with their start and end apart: 11, of which 9 were waited for; matrix products, arithmetic and copies ran while one was open for 4% of the time, Pallas kernels for 6%

profile of v6, /device:TPU:0, one launch (start us, length us, event | category | flops | bytes accessed | tf_op | source)
XLA Modules:
  0.0 23.0 jit_solution(4550897131036548610)
XLA Ops:
  0.0 0.5 %collective-permute-start = (f32[128,256]{1,0:T(8,128)}, f32[128,256]{1,0:T(8,128)S(1)}, u32[]{:S(2)}, u32[]{:S(2)}) collective-permute-start(f32[128,256]{1,0:T(8,128)} %param.6), channel_id=1, source_target_pairs={{0,1},{1,0},{2,3},{3,2},{4,5},{5,4},{6,7},{7,6},{8,9},{9,8},{10,11... | collective-permute-start | bytes 393224 | tf_op jit(solution)/shard_map/ppermute | solution.py:179
  0.5 0.1 collective-permute-start.1
  0.5 1.0 %pad_maximum_fusion.kv_ref = f32[128,512]{1,0:T(8,128)S(1)} fusion(f32[128,256]{1,0:T(8,128)} %param.7, f32[128,256]{1,0:T(8,128)} %param.6), kind=kLoop, calls=%fused_computation | loop fusion | flops 65536 | bytes 524288 | tf_op jit(solution)/shard_map/concatenate | solution.py:216
  1.5 0.1 collective-permute-done.kc_ref.refs_2_
  1.7 0.4 %collective-permute-done.1.vc_ref.refs_3_ = f32[128,256]{1,0:T(8,128)S(1)} collective-permute-done((f32[128,256]{1,0:T(8,128)}, f32[128,256]{1,0:T(8,128)S(1)}, u32[]{:S(2)}, u32[]{:S(2)}) %collective-permute-start.1) | collective-permute-done | bytes 131104 | tf_op jit(solution)/shard_map/ppermute | solution.py:179
  2.0 0.3 %shard_map.56 = (f32[128,128]{1,0:T(8,128)S(1)}, f32[128,512]{1,0:T(8,128)S(1)}) custom-call(f32[128,256]{1,0:T(8,128)S(1)} %collective-permute-done.kc_ref.refs_2_, f32[128,256]{1,0:T(8,128)S(1)} %collective-permute-done.1.vc_ref.refs_3_, f32[128,512]{1,0:T(8,128)S(1)} %pad_maximum_fusion.kv_ref), custom_call_target="tpu_custom_call", output_to_operand_aliasing={{1}: (2, {})} | custom-call | flops 500000000 | bytes 500000 | tf_op jit(solution)/shard_map/pallas_call | solution.py:202
  2.3 2.7 %collective-permute-start.2 = (f32[128,512]{1,0:T(8,128)S(1)}, f32[128,512]{1,0:T(8,128)S(1)}, u32[]{:S(2)}, u32[]{:S(2)}) collective-permute-start(f32[128,512]{1,0:T(8,128)S(1)} %get-tuple-element.19.refs_4_), channel_id=1, source_target_pairs={{0,2},{1,3},{2,0},{3,1},{4,6},{5,7},{6,4},{7,5},{8,10},{9,11},{10,... | collective-permute-start | bytes 786440 | tf_op jit(solution)/shard_map/ppermute | solution.py:179
  5.0 2.6 %collective-permute-start.4 = (f32[128,128]{1,0:T(8,128)S(1)}, f32[128,128]{1,0:T(8,128)S(1)}, u32[]{:S(2)}, u32[]{:S(2)}) collective-permute-start(f32[128,128]{1,0:T(8,128)S(1)} %get-tuple-element.25.refs_0_), channel_id=1, source_target_pairs={{0,16},{1,17},{2,18},{3,19},{4,20},{5,21},{6,22},{7,23},{8,24},{9,... | collective-permute-start | bytes 196616 | tf_op jit(solution)/shard_map/ppermute | solution.py:179
  7.6 1.3 %collective-permute-start.5 = (f32[128,128]{1,0:T(8,128)S(1)}, f32[128,128]{1,0:T(8,128)S(1)}, u32[]{:S(2)}, u32[]{:S(2)}) collective-permute-start(f32[128,128]{1,0:T(8,128)S(1)} %get-tuple-element.25.refs_0_), channel_id=1, source_target_pairs={{0,24},{1,25},{2,26},{3,27},{4,28},{5,29},{6,30},{7,31},{8,16},{9,... | collective-permute-start | bytes 196616 | tf_op jit(solution)/shard_map/ppermute | solution.py:179
  9.0 0.2 %collective-permute-start.6 = (f32[128,128]{1,0:T(8,128)S(1)}, f32[128,128]{1,0:T(8,128)S(1)}, u32[]{:S(2)}, u32[]{:S(2)}) collective-permute-start(f32[128,128]{1,0:T(8,128)S(1)} %get-tuple-element.25.refs_0_), channel_id=1, source_target_pairs={{0,8},{1,9},{2,10},{3,11},{4,12},{5,13},{6,14},{7,15},{8,0},{9,1},... | collective-permute-start | bytes 196616 | tf_op jit(solution)/shard_map/ppermute | solution.py:179
  9.2 0.6 %copy-done.2 = f32[8]{0:T(128)S(1)} copy-done((f32[8]{0:T(128)S(1)}, f32[8]{0:T(128)}, u32[]{:S(2)}) %copy-start.2) | copy-done | bytes 56
  9.9 0.4 %shard_map.55 = (bf16[128,1024]{1,0:T(8,128)(2,1)S(1)}, bf16[128,1024]{1,0:T(8,128)(2,1)S(1)}, bf16[128,1024]{1,0:T(8,128)(2,1)S(1)}, bf16[128,1024]{1,0:T(8,128...) custom-call(f32[128,1024]{1,0:T(8,128)S(1)} %copy-done, f32[1,8]{1,0:T(1,128)S(1)} %bitcast.3, f32[1,1024]{1,0:T(1,128)S(1)} %bitcast.2), custom_call_target="tpu_custom_call" | custom-call | flops 1000000 | bytes 100000 | tf_op jit(solution)/shard_map/pallas_call | solution.py:225
  10.3 1.6 %collective-permute-done.2.refs_5_ = f32[128,512]{1,0:T(8,128)S(1)} collective-permute-done((f32[128,512]{1,0:T(8,128)S(1)}, f32[128,512]{1,0:T(8,128)S(1)}, u32[]{:S(2)}, u32[]{:S(2)}) %collective-permute-start.2) | collective-permute-done | bytes 262176 | tf_op jit(solution)/shard_map/ppermute | solution.py:179
  11.8 0.9 %collective-permute-done.4.refs_1_ = f32[128,128]{1,0:T(8,128)S(1)} collective-permute-done((f32[128,128]{1,0:T(8,128)S(1)}, f32[128,128]{1,0:T(8,128)S(1)}, u32[]{:S(2)}, u32[]{:S(2)}) %collective-permute-start.4) | collective-permute-done | bytes 65568 | tf_op jit(solution)/shard_map/ppermute | solution.py:179
  12.7 1.2 %collective-permute-done.5.refs_2_ = f32[128,128]{1,0:T(8,128)S(1)} collective-permute-done((f32[128,128]{1,0:T(8,128)S(1)}, f32[128,128]{1,0:T(8,128)S(1)}, u32[]{:S(2)}, u32[]{:S(2)}) %collective-permute-start.5) | collective-permute-done | bytes 65568 | tf_op jit(solution)/shard_map/ppermute | solution.py:179
  14.0 0.3 %collective-permute-done.6.refs_3_ = f32[128,128]{1,0:T(8,128)S(1)} collective-permute-done((f32[128,128]{1,0:T(8,128)S(1)}, f32[128,128]{1,0:T(8,128)S(1)}, u32[]{:S(2)}, u32[]{:S(2)}) %collective-permute-start.6) | collective-permute-done | bytes 65568 | tf_op jit(solution)/shard_map/ppermute | solution.py:179
  14.3 1.6 %collective-permute-start.7 = (f32[128,128]{1,0:T(8,128)S(1)}, f32[128,128]{1,0:T(8,128)S(1)}, u32[]{:S(2)}, u32[]{:S(2)}) collective-permute-start(f32[128,128]{1,0:T(8,128)S(1)} %get-tuple-element.26), channel_id=1, source_target_pairs={{0,6},{1,7},{2,4},{3,5},{4,2},{5,3},{6,0},{7,1},{8,14},{9,15},{10,... | collective-permute-start | bytes 196616 | tf_op jit(solution)/shard_map/ppermute | solution.py:179
  15.9 1.7 %collective-permute-start.9 = (f32[128,128]{1,0:T(8,128)S(1)}, f32[128,128]{1,0:T(8,128)S(1)}, u32[]{:S(2)}, u32[]{:S(2)}) collective-permute-start(f32[128,128]{1,0:T(8,128)S(1)} %get-tuple-element.27.refs_4_), channel_id=1, source_target_pairs={{0,3},{1,2},{2,1},{3,0},{4,7},{5,6},{6,5},{7,4},{8,11},{9,10},{10,... | collective-permute-start | bytes 196616 | tf_op jit(solution)/shard_map/ppermute | solution.py:179
  17.6 0.9 %shard_map.57 = (f32[128,1024]{1,0:T(8,128)S(1)}, f32[8,128]{1,0:T(8,128)S(1)}) custom-call(bf16[128,1024]{1,0:T(8,128)(2,1)S(1)} %get-tuple-element.17.refs_0_, bf16[128,1024]{1,0:T(8,128)(2,1)S(1)} %get-tuple-element.18.refs_1_, f32[128,256]{1,0:T(8,128)S(1)} %collective-permute-done.kc_ref.refs_2_, f32[128,256]{1,0:T(8,128)S(1)} %collective-permute-done.1.vc_ref.refs_3_, ...), custom_call_target="tpu_custom_call" | custom-call | flops 1000000 | bytes 100000 | tf_op jit(solution)/shard_map/pallas_call | solution.py:262
  18.5 1.1 %collective-permute-done.7.refs_1_ = f32[128,128]{1,0:T(8,128)S(1)} collective-permute-done((f32[128,128]{1,0:T(8,128)S(1)}, f32[128,128]{1,0:T(8,128)S(1)}, u32[]{:S(2)}, u32[]{:S(2)}) %collective-permute-start.7) | collective-permute-done | bytes 65568 | tf_op jit(solution)/shard_map/ppermute | solution.py:179
  19.6 0.6 %collective-permute-done.8.refs_2_ = f32[128,128]{1,0:T(8,128)S(1)} collective-permute-done((f32[128,128]{1,0:T(8,128)S(1)}, f32[128,128]{1,0:T(8,128)S(1)}, u32[]{:S(2)}, u32[]{:S(2)}) %collective-permute-start.8) | collective-permute-done | bytes 65568 | tf_op jit(solution)/shard_map/ppermute | solution.py:179
  20.3 0.6 %collective-permute-start.10 = (f32[128,128]{1,0:T(8,128)S(1)}, f32[128,128]{1,0:T(8,128)S(1)}, u32[]{:S(2)}, u32[]{:S(2)}) collective-permute-start(f32[128,128]{1,0:T(8,128)S(1)} %shard_map.59.mine_ref), channel_id=1, source_target_pairs={{0,1},{1,0},{2,3},{3,2},{4,5},{5,4},{6,7},{7,6},{8,9},{9,8},{10,11... | collective-permute-start | bytes 196616 | tf_op jit(solution)/shard_map/ppermute | solution.py:179
  20.9 0.9 %collective-permute-done.10.other_ref = f32[128,128]{1,0:T(8,128)S(1)} collective-permute-done((f32[128,128]{1,0:T(8,128)S(1)}, f32[128,128]{1,0:T(8,128)S(1)}, u32[]{:S(2)}, u32[]{:S(2)}) %collective-permute-start.10) | collective-permute-done | bytes 65568 | tf_op jit(solution)/shard_map/ppermute | solution.py:179
  21.8 1.3 %shard_map.60 = f32[128,1024]{1,0:T(8,128)} custom-call(f32[128,1024]{1,0:T(8,128)S(1)} %get-tuple-element.21.att_ref, bf16[128,1024]{1,0:T(8,128)(2,1)S(1)} %get-tuple-element.22.sh_ref, bf16[128,1024]{1,0:T(8,128)(2,1)S(1)} %get-tuple-element.23.sl_ref, f32[1,1024]{1,0:T(1,128)S(1)} %get-tuple-element.24.refs_4_.mult_ref, ...), custom_call_target="tpu_custom_call" | custom-call | tf_op jit(solution)/shard_map/pallas_call | solution.py:272
  (11 shorter events, 0.1 us)
Async XLA Ops:
  0.0 1.6 %collective-permute-start = (f32[128,256]{1,0:T(8,128)}, f32[128,256]{1,0:T(8,128)S(1)}, u32[]{:S(2)}, u32[]{:S(2)}) collective-permute-start(f32[128,256]{1,0:T(8,128)} %param.6), channel_id=1, source_target_pairs={{0,1},{1,0},{2,3},{3,2},{4,5},{5,4},{6,7},{7,6},{8,9},{9,8},{10,11... | collective-permute-start | bytes 393224 | tf_op jit(solution)/shard_map/ppermute | solution.py:179
  0.5 1.6 %collective-permute-start.1 = (f32[128,256]{1,0:T(8,128)}, f32[128,256]{1,0:T(8,128)S(1)}, u32[]{:S(2)}, u32[]{:S(2)}) collective-permute-start(f32[128,256]{1,0:T(8,128)} %param.7), channel_id=1, source_target_pairs={{0,1},{1,0},{2,3},{3,2},{4,5},{5,4},{6,7},{7,6},{8,9},{9,8},{10,11... | collective-permute-start | bytes 393224 | tf_op jit(solution)/shard_map/ppermute | solution.py:179
  1.5 7.7 %copy-start = (f32[128,1024]{1,0:T(8,128)S(1)}, f32[128,1024]{1,0:T(8,128)}, u32[]{:S(2)}) copy-start(f32[128,1024]{1,0:T(8,128)} %refs_0_.1) | copy-start | bytes 1572868
  2.3 6.9 %copy-start.1 = (f32[1024]{0:T(1024)S(1)}, f32[1024]{0:T(1024)}, u32[]{:S(2)}) copy-start(f32[1024]{0:T(1024)} %param.9) | copy-start | bytes 12292
  2.3 9.5 %collective-permute-start.2 = (f32[128,512]{1,0:T(8,128)S(1)}, f32[128,512]{1,0:T(8,128)S(1)}, u32[]{:S(2)}, u32[]{:S(2)}) collective-permute-start(f32[128,512]{1,0:T(8,128)S(1)} %get-tuple-element.19.refs_4_), channel_id=1, source_target_pairs={{0,2},{1,3},{2,0},{3,1},{4,6},{5,7},{6,4},{7,5},{8,10},{9,11},{10,... | collective-permute-start | bytes 786440 | tf_op jit(solution)/shard_map/ppermute | solution.py:179
  5.0 7.7 %collective-permute-start.4 = (f32[128,128]{1,0:T(8,128)S(1)}, f32[128,128]{1,0:T(8,128)S(1)}, u32[]{:S(2)}, u32[]{:S(2)}) collective-permute-start(f32[128,128]{1,0:T(8,128)S(1)} %get-tuple-element.25.refs_0_), channel_id=1, source_target_pairs={{0,16},{1,17},{2,18},{3,19},{4,20},{5,21},{6,22},{7,23},{8,24},{9,... | collective-permute-start | bytes 196616 | tf_op jit(solution)/shard_map/ppermute | solution.py:179
  7.6 6.3 %collective-permute-start.5 = (f32[128,128]{1,0:T(8,128)S(1)}, f32[128,128]{1,0:T(8,128)S(1)}, u32[]{:S(2)}, u32[]{:S(2)}) collective-permute-start(f32[128,128]{1,0:T(8,128)S(1)} %get-tuple-element.25.refs_0_), channel_id=1, source_target_pairs={{0,24},{1,25},{2,26},{3,27},{4,28},{5,29},{6,30},{7,31},{8,16},{9,... | collective-permute-start | bytes 196616 | tf_op jit(solution)/shard_map/ppermute | solution.py:179
  9.0 5.3 %collective-permute-start.6 = (f32[128,128]{1,0:T(8,128)S(1)}, f32[128,128]{1,0:T(8,128)S(1)}, u32[]{:S(2)}, u32[]{:S(2)}) collective-permute-start(f32[128,128]{1,0:T(8,128)S(1)} %get-tuple-element.25.refs_0_), channel_id=1, source_target_pairs={{0,8},{1,9},{2,10},{3,11},{4,12},{5,13},{6,14},{7,15},{8,0},{9,1},... | collective-permute-start | bytes 196616 | tf_op jit(solution)/shard_map/ppermute | solution.py:179
  9.2 0.7 %copy-start.2 = (f32[8]{0:T(128)S(1)}, f32[8]{0:T(128)}, u32[]{:S(2)}) copy-start(f32[8]{0:T(128)} %param.8) | copy-start | bytes 100
  11.8 5.7 %collective-permute-start.3 = (f32[128,512]{1,0:T(8,128)S(1)}, f32[128,512]{1,0:T(8,128)S(1)}, u32[]{:S(2)}, u32[]{:S(2)}) collective-permute-start(f32[128,512]{1,0:T(8,128)S(1)} %collective-permute-done.2.refs_5_), channel_id=1, source_target_pairs={{0,1},{1,0},{2,3},{3,2},{4,5},{5,4},{6,7},{7,6},{8,9},{9,8},{10,11... | collective-permute-start | bytes 786440 | tf_op jit(solution)/shard_map/ppermute | solution.py:179
  14.3 5.3 %collective-permute-start.7 = (f32[128,128]{1,0:T(8,128)S(1)}, f32[128,128]{1,0:T(8,128)S(1)}, u32[]{:S(2)}, u32[]{:S(2)}) collective-permute-start(f32[128,128]{1,0:T(8,128)S(1)} %get-tuple-element.26), channel_id=1, source_target_pairs={{0,6},{1,7},{2,4},{3,5},{4,2},{5,3},{6,0},{7,1},{8,14},{9,15},{10,... | collective-permute-start | bytes 196616 | tf_op jit(solution)/shard_map/ppermute | solution.py:179
  15.8 4.4 %collective-permute-start.8 = (f32[128,128]{1,0:T(8,128)S(1)}, f32[128,128]{1,0:T(8,128)S(1)}, u32[]{:S(2)}, u32[]{:S(2)}) collective-permute-start(f32[128,128]{1,0:T(8,128)S(1)} %get-tuple-element.26), channel_id=1, source_target_pairs={{0,5},{1,4},{2,7},{3,6},{4,1},{5,0},{6,3},{7,2},{8,13},{9,12},{10,... | collective-permute-start | bytes 196616 | tf_op jit(solution)/shard_map/ppermute | solution.py:179
  15.9 4.4 %collective-permute-start.9 = (f32[128,128]{1,0:T(8,128)S(1)}, f32[128,128]{1,0:T(8,128)S(1)}, u32[]{:S(2)}, u32[]{:S(2)}) collective-permute-start(f32[128,128]{1,0:T(8,128)S(1)} %get-tuple-element.27.refs_4_), channel_id=1, source_target_pairs={{0,3},{1,2},{2,1},{3,0},{4,7},{5,6},{6,5},{7,4},{8,11},{9,10},{10,... | collective-permute-start | bytes 196616 | tf_op jit(solution)/shard_map/ppermute | solution.py:179
  20.3 1.5 %collective-permute-start.10 = (f32[128,128]{1,0:T(8,128)S(1)}, f32[128,128]{1,0:T(8,128)S(1)}, u32[]{:S(2)}, u32[]{:S(2)}) collective-permute-start(f32[128,128]{1,0:T(8,128)S(1)} %shard_map.59.mine_ref), channel_id=1, source_target_pairs={{0,1},{1,0},{2,3},{3,2},{4,5},{5,4},{6,7},{7,6},{8,9},{9,8},{10,11... | collective-permute-start | bytes 196616 | tf_op jit(solution)/shard_map/ppermute | solution.py:179

commit v7 on v6

--- a/solution.py
+++ b/solution.py
@@ -145,25 +145,40 @@
     done_ref[...] = jnp.zeros_like(done_ref)
 
 
-def final_kernel(group, lines, att_ref, sh_ref, sl_ref, mult_ref, mine_ref, other_ref, out_ref):
+def mix_head(group, first, att_ref, sh_ref, sl_ref, mult_ref, memory_ref):
     rows = att_ref.shape[0]
-    kv_heads = att_ref.shape[1] // (group * HD)
+    m_hi, m_lo = split(memory_ref[...])
+    spans = [pl.ds(pl.multiple_of((first + g) * HD, HD), HD) for g in range(group)]
+    f_hi = jnp.concatenate([sh_ref[:, s] for s in spans], 0)
+    f_lo = jnp.concatenate([sl_ref[:, s] for s in spans], 0)
+    r = dot(jnp.concatenate([f_hi, f_lo], 1), jnp.concatenate([m_hi, m_hi], 0), ((1,), (0,)))
+    r = r + dot(f_hi, m_lo, ((1,), (0,)))
+    r = r * lax.rsqrt(jnp.mean(r * r, axis=1, keepdims=True) + EPS)
+    return [
+        (s, att_ref[:, s] + r[g * rows : (g + 1) * rows] * mult_ref[:, s])
+        for g, s in enumerate(spans)
+    ]
+
+
+def own_mix_kernel(group, lines, *refs):
+    for g, (_, mixed) in enumerate(mix_head(group, carried_head(lines) * group, *refs[:5])):
+        refs[5][g] = mixed
+
+
+def final_kernel(group, lines, *refs):
+    ready_ref, out_ref, tile_ref, sems = refs[5:]
     own = carried_head(lines)
-    for head in range(kv_heads):
-        memory = jnp.where(own == head, mine_ref[...], other_ref[...])
-        m_hi, m_lo = split(memory)
-        right = jnp.concatenate([m_hi, m_hi], 0)
-        spans = [
-            slice((head * group + g) * HD, (head * group + g + 1) * HD) for g in range(group)
-        ]
-        f_hi = jnp.concatenate([sh_ref[:, s] for s in spans], 0)
-        f_lo = jnp.concatenate([sl_ref[:, s] for s in spans], 0)
-        r = dot(jnp.concatenate([f_hi, f_lo], 1), right, ((1,), (0,)))
-        r = r + dot(f_hi, m_lo, ((1,), (0,)))
-        inv = lax.rsqrt(jnp.mean(r * r, axis=1, keepdims=True) + EPS)
-        r = r * inv
-        for g, s in enumerate(spans):
-            out_ref[:, s] = att_ref[:, s] + r[g * rows : (g + 1) * rows] * mult_ref[:, s]
+    copies = []
+    for g in range(group):
+        s = pl.ds(pl.multiple_of((own * group + g) * HD, HD), HD)
+        copies.append(pltpu.make_async_copy(ready_ref.at[g], out_ref.at[:, s], sems.at[g]))
+        copies[-1].start()
+    for g, (s, mixed) in enumerate(mix_head(group, (1 - own) * group, *refs[:5])):
+        tile_ref[g] = mixed
+        copies.append(pltpu.make_async_copy(tile_ref.at[g], out_ref.at[:, s], sems.at[group + g]))
+        copies[-1].start()
+    for copy in copies:
+        copy.wait()
 
 
 def solution(mesh):
@@ -269,11 +284,26 @@
                 )(q_hi, q_lo, k_core, v_core, own, *held[2:], keep)
         other = swap(carried, 0, 1)
 
+        tiles = (group, rows, HD)
+        small = pltpu.CompilerParams(vmem_limit_bytes=16 * 1024 * 1024)
+        ready = pl.pallas_call(
+            functools.partial(own_mix_kernel, group, lines),
+            out_shape=jax.ShapeDtypeStruct(tiles, jnp.float32),
+            compiler_params=small,
+            cost_estimate=pl.CostEstimate(
+                flops=1_000_000_000, bytes_accessed=500_000, transcendentals=0
+            ),
+        )(att, f_hi, f_lo, mult, carried)
         return pl.pallas_call(
             functools.partial(final_kernel, group, lines),
-            out_shape=jax.ShapeDtypeStruct((rows, width), jnp.float32),
-            compiler_params=pltpu.CompilerParams(vmem_limit_bytes=16 * 1024 * 1024),
-        )(att, f_hi, f_lo, mult, carried, other)
+            out_specs=pl.BlockSpec(memory_space=pl.ANY),
+            out_shape=wide,
+            scratch_shapes=[
+                pltpu.VMEM(tiles, jnp.float32),
+                pltpu.SemaphoreType.DMA((2 * group,)),
+            ],
+            compiler_params=small,
+        )(att, f_hi, f_lo, mult, other, ready)
 
     return jax.shard_map(
         on_device,

time: 23.2 us -> 23 us (level)
  waiting for transfers between devices: 7.14 us -> 6.8 us
    ppermute x11, waiting for transfers between devices: 7.14 us -> 6.8 us  [swap(): return lax.ppermute(x, both, pairs)]
    pallas_call x1 -> x2, Pallas kernels: 1.26 us -> 1.45 us  [the longest x1 1.11 us: on_device(): pl.pallas_call(functools.partial(final_kernel, group, lines), out_specs=p...]
  transfers between devices with their start and end apart: 11 -> 11, of which waited for: 9 -> 9; matrix products, arithmetic and copies ran while one was open for 4% -> 4% of each run, Pallas kernels for 6% -> 7%
where the time goes in v7:
time: 23 us; the launch traced here: 22.9 us
  starting transfers between devices  11.3 us (49%)
  waiting for transfers between devices  6.8 us (30%)
  Pallas kernels  3.05 us (13%)
  other arithmetic  0.99 us (4%)
  local copies, waits for them, and re-layouts  0.66 us (3%)
    ppermute x11, starting transfers between devices, swap(): return lax.ppermute(x, both, pairs)  11.3 us
    ppermute x11, waiting for transfers between devices, swap(): return lax.ppermute(x, both, pairs)  6.8 us
    pallas_call x1, Pallas kernels, on_device(): pl.pallas_call(functools.partial(final_kernel, group, lines), out_specs=p...  1.11 us
    concatenate x1, other arithmetic, on_device(): own = jnp.concatenate([keys, values], 1)  0.99 us
    pallas_call x1, Pallas kernels, on_device(): pl.pallas_call(functools.partial(attention_kernel, group, n_blk), out_sha...  0.9 us
    unnamed x6, local copies, waits for them, and re-layouts  0.66 us
  transfers between devices with their start and end apart: 11, of which 9 were waited for; matrix products, arithmetic and copies ran while one was open for 4% of the time, Pallas kernels for 7%

profile of v7, /device:TPU:0, one launch (start us, length us, event | category | flops | bytes accessed | tf_op | source)
XLA Modules:
  0.0 22.9 jit_solution(3174324050959029006)
XLA Ops:
  0.0 0.5 %collective-permute-start = (f32[128,256]{1,0:T(8,128)}, f32[128,256]{1,0:T(8,128)S(1)}, u32[]{:S(2)}, u32[]{:S(2)}) collective-permute-start(f32[128,256]{1,0:T(8,128)} %param.6), channel_id=1, source_target_pairs={{0,1},{1,0},{2,3},{3,2},{4,5},{5,4},{6,7},{7,6},{8,9},{9,8},{10,11... | collective-permute-start | bytes 393224 | tf_op jit(solution)/shard_map/ppermute | solution.py:194
  0.5 1.0 %pad_maximum_fusion.kv_ref = f32[128,512]{1,0:T(8,128)S(1)} fusion(f32[128,256]{1,0:T(8,128)} %param.7, f32[128,256]{1,0:T(8,128)} %param.6), kind=kLoop, calls=%fused_computation | loop fusion | flops 65536 | bytes 524288 | tf_op jit(solution)/shard_map/concatenate | solution.py:231
  1.5 0.1 collective-permute-done.kc_ref.refs_2_
  1.7 0.4 %collective-permute-done.1.vc_ref.refs_3_ = f32[128,256]{1,0:T(8,128)S(1)} collective-permute-done((f32[128,256]{1,0:T(8,128)}, f32[128,256]{1,0:T(8,128)S(1)}, u32[]{:S(2)}, u32[]{:S(2)}) %collective-permute-start.1) | collective-permute-done | bytes 131104 | tf_op jit(solution)/shard_map/ppermute | solution.py:194
  2.0 0.3 %shard_map.56 = (f32[128,128]{1,0:T(8,128)S(1)}, f32[128,512]{1,0:T(8,128)S(1)}) custom-call(f32[128,256]{1,0:T(8,128)S(1)} %collective-permute-done.kc_ref.refs_2_, f32[128,256]{1,0:T(8,128)S(1)} %collective-permute-done.1.vc_ref.refs_3_, f32[128,512]{1,0:T(8,128)S(1)} %pad_maximum_fusion.kv_ref), custom_call_target="tpu_custom_call", output_to_operand_aliasing={{1}: (2, {})} | custom-call | flops 500000000 | bytes 500000 | tf_op jit(solution)/shard_map/pallas_call | solution.py:217
  2.3 2.7 %collective-permute-start.2 = (f32[128,512]{1,0:T(8,128)S(1)}, f32[128,512]{1,0:T(8,128)S(1)}, u32[]{:S(2)}, u32[]{:S(2)}) collective-permute-start(f32[128,512]{1,0:T(8,128)S(1)} %get-tuple-element.19.refs_4_), channel_id=1, source_target_pairs={{0,2},{1,3},{2,0},{3,1},{4,6},{5,7},{6,4},{7,5},{8,10},{9,11},{10,... | collective-permute-start | bytes 786440 | tf_op jit(solution)/shard_map/ppermute | solution.py:194
  5.0 2.6 %collective-permute-start.4 = (f32[128,128]{1,0:T(8,128)S(1)}, f32[128,128]{1,0:T(8,128)S(1)}, u32[]{:S(2)}, u32[]{:S(2)}) collective-permute-start(f32[128,128]{1,0:T(8,128)S(1)} %get-tuple-element.25.refs_0_), channel_id=1, source_target_pairs={{0,16},{1,17},{2,18},{3,19},{4,20},{5,21},{6,22},{7,23},{8,24},{9,... | collective-permute-start | bytes 196616 | tf_op jit(solution)/shard_map/ppermute | solution.py:194
  7.6 1.3 %collective-permute-start.5 = (f32[128,128]{1,0:T(8,128)S(1)}, f32[128,128]{1,0:T(8,128)S(1)}, u32[]{:S(2)}, u32[]{:S(2)}) collective-permute-start(f32[128,128]{1,0:T(8,128)S(1)} %get-tuple-element.25.refs_0_), channel_id=1, source_target_pairs={{0,24},{1,25},{2,26},{3,27},{4,28},{5,29},{6,30},{7,31},{8,16},{9,... | collective-permute-start | bytes 196616 | tf_op jit(solution)/shard_map/ppermute | solution.py:194
  9.0 0.2 %collective-permute-start.6 = (f32[128,128]{1,0:T(8,128)S(1)}, f32[128,128]{1,0:T(8,128)S(1)}, u32[]{:S(2)}, u32[]{:S(2)}) collective-permute-start(f32[128,128]{1,0:T(8,128)S(1)} %get-tuple-element.25.refs_0_), channel_id=1, source_target_pairs={{0,8},{1,9},{2,10},{3,11},{4,12},{5,13},{6,14},{7,15},{8,0},{9,1},... | collective-permute-start | bytes 196616 | tf_op jit(solution)/shard_map/ppermute | solution.py:194
  9.2 0.6 %copy-done.2 = f32[8]{0:T(128)S(1)} copy-done((f32[8]{0:T(128)S(1)}, f32[8]{0:T(128)}, u32[]{:S(2)}) %copy-start.2) | copy-done | bytes 56
  9.9 0.4 %shard_map.55 = (bf16[128,1024]{1,0:T(8,128)(2,1)S(1)}, bf16[128,1024]{1,0:T(8,128)(2,1)S(1)}, bf16[128,1024]{1,0:T(8,128)(2,1)S(1)}, bf16[128,1024]{1,0:T(8,128...) custom-call(f32[128,1024]{1,0:T(8,128)S(1)} %copy-done, f32[1,8]{1,0:T(1,128)S(1)} %bitcast.3, f32[1,1024]{1,0:T(1,128)S(1)} %bitcast.2), custom_call_target="tpu_custom_call" | custom-call | flops 1000000 | bytes 100000 | tf_op jit(solution)/shard_map/pallas_call | solution.py:240
  10.3 1.6 %collective-permute-done.2.refs_5_ = f32[128,512]{1,0:T(8,128)S(1)} collective-permute-done((f32[128,512]{1,0:T(8,128)S(1)}, f32[128,512]{1,0:T(8,128)S(1)}, u32[]{:S(2)}, u32[]{:S(2)}) %collective-permute-start.2) | collective-permute-done | bytes 262176 | tf_op jit(solution)/shard_map/ppermute | solution.py:194
  11.8 0.9 %collective-permute-done.4.refs_1_ = f32[128,128]{1,0:T(8,128)S(1)} collective-permute-done((f32[128,128]{1,0:T(8,128)S(1)}, f32[128,128]{1,0:T(8,128)S(1)}, u32[]{:S(2)}, u32[]{:S(2)}) %collective-permute-start.4) | collective-permute-done | bytes 65568 | tf_op jit(solution)/shard_map/ppermute | solution.py:194
  12.7 1.2 %collective-permute-done.5.refs_2_ = f32[128,128]{1,0:T(8,128)S(1)} collective-permute-done((f32[128,128]{1,0:T(8,128)S(1)}, f32[128,128]{1,0:T(8,128)S(1)}, u32[]{:S(2)}, u32[]{:S(2)}) %collective-permute-start.5) | collective-permute-done | bytes 65568 | tf_op jit(solution)/shard_map/ppermute | solution.py:194
  14.0 0.3 %collective-permute-done.6.refs_3_ = f32[128,128]{1,0:T(8,128)S(1)} collective-permute-done((f32[128,128]{1,0:T(8,128)S(1)}, f32[128,128]{1,0:T(8,128)S(1)}, u32[]{:S(2)}, u32[]{:S(2)}) %collective-permute-start.6) | collective-permute-done | bytes 65568 | tf_op jit(solution)/shard_map/ppermute | solution.py:194
  14.3 1.6 %collective-permute-start.7 = (f32[128,128]{1,0:T(8,128)S(1)}, f32[128,128]{1,0:T(8,128)S(1)}, u32[]{:S(2)}, u32[]{:S(2)}) collective-permute-start(f32[128,128]{1,0:T(8,128)S(1)} %get-tuple-element.26), channel_id=1, source_target_pairs={{0,6},{1,7},{2,4},{3,5},{4,2},{5,3},{6,0},{7,1},{8,14},{9,15},{10,... | collective-permute-start | bytes 196616 | tf_op jit(solution)/shard_map/ppermute | solution.py:194
  15.9 1.7 %collective-permute-start.9 = (f32[128,128]{1,0:T(8,128)S(1)}, f32[128,128]{1,0:T(8,128)S(1)}, u32[]{:S(2)}, u32[]{:S(2)}) collective-permute-start(f32[128,128]{1,0:T(8,128)S(1)} %get-tuple-element.27.refs_4_), channel_id=1, source_target_pairs={{0,3},{1,2},{2,1},{3,0},{4,7},{5,6},{6,5},{7,4},{8,11},{9,10},{10,... | collective-permute-start | bytes 196616 | tf_op jit(solution)/shard_map/ppermute | solution.py:194
  17.6 0.9 %shard_map.57 = (f32[128,1024]{1,0:T(8,128)S(1)}, f32[8,128]{1,0:T(8,128)S(1)}) custom-call(bf16[128,1024]{1,0:T(8,128)(2,1)S(1)} %get-tuple-element.17.refs_0_, bf16[128,1024]{1,0:T(8,128)(2,1)S(1)} %get-tuple-element.18.refs_1_, f32[128,256]{1,0:T(8,128)S(1)} %collective-permute-done.kc_ref.refs_2_, f32[128,256]{1,0:T(8,128)S(1)} %collective-permute-done.1.vc_ref.refs_3_, ...), custom_call_target="tpu_custom_call" | custom-call | flops 1000000 | bytes 100000 | tf_op jit(solution)/shard_map/pallas_call | solution.py:277
  18.5 1.1 %collective-permute-done.7.refs_1_ = f32[128,128]{1,0:T(8,128)S(1)} collective-permute-done((f32[128,128]{1,0:T(8,128)S(1)}, f32[128,128]{1,0:T(8,128)S(1)}, u32[]{:S(2)}, u32[]{:S(2)}) %collective-permute-start.7) | collective-permute-done | bytes 65568 | tf_op jit(solution)/shard_map/ppermute | solution.py:194
  19.6 0.6 %collective-permute-done.8.refs_2_ = f32[128,128]{1,0:T(8,128)S(1)} collective-permute-done((f32[128,128]{1,0:T(8,128)S(1)}, f32[128,128]{1,0:T(8,128)S(1)}, u32[]{:S(2)}, u32[]{:S(2)}) %collective-permute-start.8) | collective-permute-done | bytes 65568 | tf_op jit(solution)/shard_map/ppermute | solution.py:194
  20.3 0.6 %collective-permute-start.10 = (f32[128,128]{1,0:T(8,128)S(1)}, f32[128,128]{1,0:T(8,128)S(1)}, u32[]{:S(2)}, u32[]{:S(2)}) collective-permute-start(f32[128,128]{1,0:T(8,128)S(1)} %shard_map.59.refs_4_), channel_id=1, source_target_pairs={{0,1},{1,0},{2,3},{3,2},{4,5},{5,4},{6,7},{7,6},{8,9},{9,8},{10,11... | collective-permute-start | bytes 196616 | tf_op jit(solution)/shard_map/ppermute | solution.py:194
  20.9 0.3 %shard_map.60.refs_5_ = f32[4,128,128]{2,1,0:T(8,128)S(1)} custom-call(f32[128,1024]{1,0:T(8,128)S(1)} %get-tuple-element.21.refs_0_, bf16[128,1024]{1,0:T(8,128)(2,1)S(1)} %get-tuple-element.22.refs_1_, bf16[128,1024]{1,0:T(8,128)(2,1)S(1)} %get-tuple-element.23.refs_2_, f32[1,1024]{1,0:T(1,128)S(1)} %get-tuple-element.24.refs_4_.refs_3_, ...), custom_call_target="tpu_custom_call" | custom-call | flops 1000000000 | bytes 500000 | tf_op jit(solution)/shard_map/pallas_call | solution.py:289
  21.2 0.6 %collective-permute-done.10.refs_4_ = f32[128,128]{1,0:T(8,128)S(1)} collective-permute-done((f32[128,128]{1,0:T(8,128)S(1)}, f32[128,128]{1,0:T(8,128)S(1)}, u32[]{:S(2)}, u32[]{:S(2)}) %collective-permute-start.10) | collective-permute-done | bytes 65568 | tf_op jit(solution)/shard_map/ppermute | solution.py:194
  21.8 1.1 %shard_map.61 = f32[128,1024]{1,0:T(8,128)} custom-call(f32[128,1024]{1,0:T(8,128)S(1)} %get-tuple-element.21.refs_0_, bf16[128,1024]{1,0:T(8,128)(2,1)S(1)} %get-tuple-element.22.refs_1_, bf16[128,1024]{1,0:T(8,128)(2,1)S(1)} %get-tuple-element.23.refs_2_, f32[1,1024]{1,0:T(1,128)S(1)} %get-tuple-element.24.refs_4_.refs_3_, ...), custom_call_target="tpu_custom_call" | custom-call | tf_op jit(solution)/shard_map/pallas_call | solution.py:297
  (12 shorter events, 0.1 us)
Async XLA Ops:
  0.0 1.6 %collective-permute-start = (f32[128,256]{1,0:T(8,128)}, f32[128,256]{1,0:T(8,128)S(1)}, u32[]{:S(2)}, u32[]{:S(2)}) collective-permute-start(f32[128,256]{1,0:T(8,128)} %param.6), channel_id=1, source_target_pairs={{0,1},{1,0},{2,3},{3,2},{4,5},{5,4},{6,7},{7,6},{8,9},{9,8},{10,11... | collective-permute-start | bytes 393224 | tf_op jit(solution)/shard_map/ppermute | solution.py:194
  0.5 1.6 %collective-permute-start.1 = (f32[128,256]{1,0:T(8,128)}, f32[128,256]{1,0:T(8,128)S(1)}, u32[]{:S(2)}, u32[]{:S(2)}) collective-permute-start(f32[128,256]{1,0:T(8,128)} %param.7), channel_id=1, source_target_pairs={{0,1},{1,0},{2,3},{3,2},{4,5},{5,4},{6,7},{7,6},{8,9},{9,8},{10,11... | collective-permute-start | bytes 393224 | tf_op jit(solution)/shard_map/ppermute | solution.py:194
  1.5 7.7 %copy-start = (f32[128,1024]{1,0:T(8,128)S(1)}, f32[128,1024]{1,0:T(8,128)}, u32[]{:S(2)}) copy-start(f32[128,1024]{1,0:T(8,128)} %refs_0_.1) | copy-start | bytes 1572868
  2.3 6.9 %copy-start.1 = (f32[1024]{0:T(1024)S(1)}, f32[1024]{0:T(1024)}, u32[]{:S(2)}) copy-start(f32[1024]{0:T(1024)} %param.9) | copy-start | bytes 12292
  2.3 9.5 %collective-permute-start.2 = (f32[128,512]{1,0:T(8,128)S(1)}, f32[128,512]{1,0:T(8,128)S(1)}, u32[]{:S(2)}, u32[]{:S(2)}) collective-permute-start(f32[128,512]{1,0:T(8,128)S(1)} %get-tuple-element.19.refs_4_), channel_id=1, source_target_pairs={{0,2},{1,3},{2,0},{3,1},{4,6},{5,7},{6,4},{7,5},{8,10},{9,11},{10,... | collective-permute-start | bytes 786440 | tf_op jit(solution)/shard_map/ppermute | solution.py:194
  5.0 7.7 %collective-permute-start.4 = (f32[128,128]{1,0:T(8,128)S(1)}, f32[128,128]{1,0:T(8,128)S(1)}, u32[]{:S(2)}, u32[]{:S(2)}) collective-permute-start(f32[128,128]{1,0:T(8,128)S(1)} %get-tuple-element.25.refs_0_), channel_id=1, source_target_pairs={{0,16},{1,17},{2,18},{3,19},{4,20},{5,21},{6,22},{7,23},{8,24},{9,... | collective-permute-start | bytes 196616 | tf_op jit(solution)/shard_map/ppermute | solution.py:194
  7.6 6.3 %collective-permute-start.5 = (f32[128,128]{1,0:T(8,128)S(1)}, f32[128,128]{1,0:T(8,128)S(1)}, u32[]{:S(2)}, u32[]{:S(2)}) collective-permute-start(f32[128,128]{1,0:T(8,128)S(1)} %get-tuple-element.25.refs_0_), channel_id=1, source_target_pairs={{0,24},{1,25},{2,26},{3,27},{4,28},{5,29},{6,30},{7,31},{8,16},{9,... | collective-permute-start | bytes 196616 | tf_op jit(solution)/shard_map/ppermute | solution.py:194
  9.0 5.3 %collective-permute-start.6 = (f32[128,128]{1,0:T(8,128)S(1)}, f32[128,128]{1,0:T(8,128)S(1)}, u32[]{:S(2)}, u32[]{:S(2)}) collective-permute-start(f32[128,128]{1,0:T(8,128)S(1)} %get-tuple-element.25.refs_0_), channel_id=1, source_target_pairs={{0,8},{1,9},{2,10},{3,11},{4,12},{5,13},{6,14},{7,15},{8,0},{9,1},... | collective-permute-start | bytes 196616 | tf_op jit(solution)/shard_map/ppermute | solution.py:194
  9.2 0.7 %copy-start.2 = (f32[8]{0:T(128)S(1)}, f32[8]{0:T(128)}, u32[]{:S(2)}) copy-start(f32[8]{0:T(128)} %param.8) | copy-start | bytes 100
  11.8 5.7 %collective-permute-start.3 = (f32[128,512]{1,0:T(8,128)S(1)}, f32[128,512]{1,0:T(8,128)S(1)}, u32[]{:S(2)}, u32[]{:S(2)}) collective-permute-start(f32[128,512]{1,0:T(8,128)S(1)} %collective-permute-done.2.refs_5_), channel_id=1, source_target_pairs={{0,1},{1,0},{2,3},{3,2},{4,5},{5,4},{6,7},{7,6},{8,9},{9,8},{10,11... | collective-permute-start | bytes 786440 | tf_op jit(solution)/shard_map/ppermute | solution.py:194
  14.3 5.3 %collective-permute-start.7 = (f32[128,128]{1,0:T(8,128)S(1)}, f32[128,128]{1,0:T(8,128)S(1)}, u32[]{:S(2)}, u32[]{:S(2)}) collective-permute-start(f32[128,128]{1,0:T(8,128)S(1)} %get-tuple-element.26), channel_id=1, source_target_pairs={{0,6},{1,7},{2,4},{3,5},{4,2},{5,3},{6,0},{7,1},{8,14},{9,15},{10,... | collective-permute-start | bytes 196616 | tf_op jit(solution)/shard_map/ppermute | solution.py:194
  15.8 4.4 %collective-permute-start.8 = (f32[128,128]{1,0:T(8,128)S(1)}, f32[128,128]{1,0:T(8,128)S(1)}, u32[]{:S(2)}, u32[]{:S(2)}) collective-permute-start(f32[128,128]{1,0:T(8,128)S(1)} %get-tuple-element.26), channel_id=1, source_target_pairs={{0,5},{1,4},{2,7},{3,6},{4,1},{5,0},{6,3},{7,2},{8,13},{9,12},{10,... | collective-permute-start | bytes 196616 | tf_op jit(solution)/shard_map/ppermute | solution.py:194
  15.9 4.4 %collective-permute-start.9 = (f32[128,128]{1,0:T(8,128)S(1)}, f32[128,128]{1,0:T(8,128)S(1)}, u32[]{:S(2)}, u32[]{:S(2)}) collective-permute-start(f32[128,128]{1,0:T(8,128)S(1)} %get-tuple-element.27.refs_4_), channel_id=1, source_target_pairs={{0,3},{1,2},{2,1},{3,0},{4,7},{5,6},{6,5},{7,4},{8,11},{9,10},{10,... | collective-permute-start | bytes 196616 | tf_op jit(solution)/shard_map/ppermute | solution.py:194
  20.3 1.5 %collective-permute-start.10 = (f32[128,128]{1,0:T(8,128)S(1)}, f32[128,128]{1,0:T(8,128)S(1)}, u32[]{:S(2)}, u32[]{:S(2)}) collective-permute-start(f32[128,128]{1,0:T(8,128)S(1)} %shard_map.59.refs_4_), channel_id=1, source_target_pairs={{0,1},{1,0},{2,3},{3,2},{4,5},{5,4},{6,7},{7,6},{8,9},{9,8},{10,11... | collective-permute-start | bytes 196616 | tf_op jit(solution)/shard_map/ppermute | solution.py:194

commit v8 on v7

--- a/solution.py
+++ b/solution.py
@@ -196,12 +196,14 @@
     bits = [("seg", i) for i in reversed(range(n_seg.bit_length() - 1))]
     bits += [("blk", i) for i in reversed(range(1, n_blk.bit_length() - 1))]
     groups = [bits[i : i + 2] for i in range(0, len(bits), 2)]
-    lines = groups[-1]
+    flips = dict(zip(groups[0], (0, 0), strict=False))
+    flips.update(zip(groups[-1], (0, 1), strict=False))
+    lines = [line for line in bits if flips.get(line)]
 
     def masks_of(number):
         found = [(0, 0)]
         for axis, bit in reversed(groups[number]):
-            flip = int(number == len(groups) - 1)
+            flip = flips.get((axis, bit), 0)
             step = (1 << bit, flip) if axis == "seg" else (0, (1 << bit) ^ flip)
             found += [(s ^ step[0], b ^ step[1]) for s, b in found]
         return [found[i] for i in ((2, 3, 1) if number == 0 and len(found) > 3 else (3, 2, 1) if len(found) == 4 else range(1, len(found)))]
@@ -247,7 +249,7 @@
         )(queries, gate, gain)
 
         held = [own, None]
-        fresh = [swap(own, 0, 2)] if n_blk > 2 else []
+        fresh = [swap(own, 0, 3)] if n_blk > 2 else []
 
         carried = None
         sends = {s: part for s, _ in masks_of(0)}
@@ -272,7 +274,8 @@
                 while step < n_blk:
                     news = fresh if step == 2 else [swap(held[m], 0, step) for m in range(0, step, 2)]
                     for new in news:
-                        held += [new, swap(new, 0, 1)]
+                        near = swap(new, 0, 1)
+                        held += [near, new] if step == 2 else [new, near]
                     step *= 2
                 att, done = pl.pallas_call(
                     functools.partial(attention_kernel, group, n_blk),

time: 23 us -> 22.8 us (level)
  starting transfers between devices: 11.3 us -> 10.9 us
    ppermute x11, starting transfers between devices: 11.3 us -> 10.9 us  [swap(): return lax.ppermute(x, both, pairs)]
where the time goes in v8:
time: 22.8 us; the launch traced here: 22.7 us
  starting transfers between devices  10.9 us (48%)
  waiting for transfers between devices  7.02 us (31%)
  Pallas kernels  3.06 us (13%)
  other arithmetic  0.99 us (4%)
  local copies, waits for them, and re-layouts  0.66 us (3%)
    ppermute x11, starting transfers between devices, swap(): return lax.ppermute(x, both, pairs)  10.9 us
    ppermute x11, waiting for transfers between devices, swap(): return lax.ppermute(x, both, pairs)  7.02 us
    pallas_call x1, Pallas kernels, on_device(): pl.pallas_call(functools.partial(final_kernel, group, lines), out_specs=p...  1.11 us
    concatenate x1, other arithmetic, on_device(): own = jnp.concatenate([keys, values], 1)  0.99 us
    pallas_call x1, Pallas kernels, on_device(): pl.pallas_call(functools.partial(attention_kernel, group, n_blk), out_sha...  0.9 us
    unnamed x6, local copies, waits for them, and re-layouts  0.66 us
  transfers between devices with their start and end apart: 11, of which 9 were waited for; matrix products, arithmetic and copies ran while one was open for 4% of the time, Pallas kernels for 7%

profile of v8, /device:TPU:0, one launch (start us, length us, event | category | flops | bytes accessed | tf_op | source)
XLA Modules:
  0.0 22.7 jit_solution(9962350532493553660)
XLA Ops:
  0.0 0.5 %collective-permute-start = (f32[128,256]{1,0:T(8,128)}, f32[128,256]{1,0:T(8,128)S(1)}, u32[]{:S(2)}, u32[]{:S(2)}) collective-permute-start(f32[128,256]{1,0:T(8,128)} %param.6), channel_id=1, source_target_pairs={{0,1},{1,0},{2,3},{3,2},{4,5},{5,4},{6,7},{7,6},{8,9},{9,8},{10,11... | collective-permute-start | bytes 393224 | tf_op jit(solution)/shard_map/ppermute | solution.py:194
  0.5 1.0 %pad_maximum_fusion.kv_ref = f32[128,512]{1,0:T(8,128)S(1)} fusion(f32[128,256]{1,0:T(8,128)} %param.7, f32[128,256]{1,0:T(8,128)} %param.6), kind=kLoop, calls=%fused_computation | loop fusion | flops 65536 | bytes 524288 | tf_op jit(solution)/shard_map/concatenate | solution.py:233
  1.5 0.1 collective-permute-done.kc_ref.refs_2_
  1.7 0.4 %collective-permute-done.1.vc_ref.refs_3_ = f32[128,256]{1,0:T(8,128)S(1)} collective-permute-done((f32[128,256]{1,0:T(8,128)}, f32[128,256]{1,0:T(8,128)S(1)}, u32[]{:S(2)}, u32[]{:S(2)}) %collective-permute-start.1) | collective-permute-done | bytes 131104 | tf_op jit(solution)/shard_map/ppermute | solution.py:194
  2.0 0.3 %shard_map.56 = (f32[128,128]{1,0:T(8,128)S(1)}, f32[128,512]{1,0:T(8,128)S(1)}) custom-call(f32[128,256]{1,0:T(8,128)S(1)} %collective-permute-done.kc_ref.refs_2_, f32[128,256]{1,0:T(8,128)S(1)} %collective-permute-done.1.vc_ref.refs_3_, f32[128,512]{1,0:T(8,128)S(1)} %pad_maximum_fusion.kv_ref), custom_call_target="tpu_custom_call", output_to_operand_aliasing={{1}: (2, {})} | custom-call | flops 500000000 | bytes 500000 | tf_op jit(solution)/shard_map/pallas_call | solution.py:219
  2.3 2.7 %collective-permute-start.2 = (f32[128,512]{1,0:T(8,128)S(1)}, f32[128,512]{1,0:T(8,128)S(1)}, u32[]{:S(2)}, u32[]{:S(2)}) collective-permute-start(f32[128,512]{1,0:T(8,128)S(1)} %get-tuple-element.19.refs_4_), channel_id=1, source_target_pairs={{0,3},{1,2},{2,1},{3,0},{4,7},{5,6},{6,5},{7,4},{8,11},{9,10},{10,... | collective-permute-start | bytes 786440 | tf_op jit(solution)/shard_map/ppermute | solution.py:194
  5.0 2.6 %collective-permute-start.4 = (f32[128,128]{1,0:T(8,128)S(1)}, f32[128,128]{1,0:T(8,128)S(1)}, u32[]{:S(2)}, u32[]{:S(2)}) collective-permute-start(f32[128,128]{1,0:T(8,128)S(1)} %get-tuple-element.25.refs_0_), channel_id=1, source_target_pairs={{0,16},{1,17},{2,18},{3,19},{4,20},{5,21},{6,22},{7,23},{8,24},{9,... | collective-permute-start | bytes 196616 | tf_op jit(solution)/shard_map/ppermute | solution.py:194
  7.6 1.3 %collective-permute-start.5 = (f32[128,128]{1,0:T(8,128)S(1)}, f32[128,128]{1,0:T(8,128)S(1)}, u32[]{:S(2)}, u32[]{:S(2)}) collective-permute-start(f32[128,128]{1,0:T(8,128)S(1)} %get-tuple-element.25.refs_0_), channel_id=1, source_target_pairs={{0,24},{1,25},{2,26},{3,27},{4,28},{5,29},{6,30},{7,31},{8,16},{9,... | collective-permute-start | bytes 196616 | tf_op jit(solution)/shard_map/ppermute | solution.py:194
  8.9 0.2 %collective-permute-start.6 = (f32[128,128]{1,0:T(8,128)S(1)}, f32[128,128]{1,0:T(8,128)S(1)}, u32[]{:S(2)}, u32[]{:S(2)}) collective-permute-start(f32[128,128]{1,0:T(8,128)S(1)} %get-tuple-element.25.refs_0_), channel_id=1, source_target_pairs={{0,8},{1,9},{2,10},{3,11},{4,12},{5,13},{6,14},{7,15},{8,0},{9,1},... | collective-permute-start | bytes 196616 | tf_op jit(solution)/shard_map/ppermute | solution.py:194
  9.2 0.6 %copy-done.2 = f32[8]{0:T(128)S(1)} copy-done((f32[8]{0:T(128)S(1)}, f32[8]{0:T(128)}, u32[]{:S(2)}) %copy-start.2) | copy-done | bytes 56
  9.8 0.4 %shard_map.55 = (bf16[128,1024]{1,0:T(8,128)(2,1)S(1)}, bf16[128,1024]{1,0:T(8,128)(2,1)S(1)}, bf16[128,1024]{1,0:T(8,128)(2,1)S(1)}, bf16[128,1024]{1,0:T(8,128...) custom-call(f32[128,1024]{1,0:T(8,128)S(1)} %copy-done, f32[1,8]{1,0:T(1,128)S(1)} %bitcast.3, f32[1,1024]{1,0:T(1,128)S(1)} %bitcast.2), custom_call_target="tpu_custom_call" | custom-call | flops 1000000 | bytes 100000 | tf_op jit(solution)/shard_map/pallas_call | solution.py:242
  10.2 1.4 %collective-permute-done.2.refs_6_ = f32[128,512]{1,0:T(8,128)S(1)} collective-permute-done((f32[128,512]{1,0:T(8,128)S(1)}, f32[128,512]{1,0:T(8,128)S(1)}, u32[]{:S(2)}, u32[]{:S(2)}) %collective-permute-start.2) | collective-permute-done | bytes 262176 | tf_op jit(solution)/shard_map/ppermute | solution.py:194
  11.6 0.4 %collective-permute-start.3 = (f32[128,512]{1,0:T(8,128)S(1)}, f32[128,512]{1,0:T(8,128)S(1)}, u32[]{:S(2)}, u32[]{:S(2)}) collective-permute-start(f32[128,512]{1,0:T(8,128)S(1)} %collective-permute-done.2.refs_6_), channel_id=1, source_target_pairs={{0,1},{1,0},{2,3},{3,2},{4,5},{5,4},{6,7},{7,6},{8,9},{9,8},{10,11... | collective-permute-start | bytes 786440 | tf_op jit(solution)/shard_map/ppermute | solution.py:194
  12.0 2.0 %collective-permute-done.5.refs_2_ = f32[128,128]{1,0:T(8,128)S(1)} collective-permute-done((f32[128,128]{1,0:T(8,128)S(1)}, f32[128,128]{1,0:T(8,128)S(1)}, u32[]{:S(2)}, u32[]{:S(2)}) %collective-permute-start.5) | collective-permute-done | bytes 65568 | tf_op jit(solution)/shard_map/ppermute | solution.py:194
  14.0 0.3 %collective-permute-done.6.refs_3_ = f32[128,128]{1,0:T(8,128)S(1)} collective-permute-done((f32[128,128]{1,0:T(8,128)S(1)}, f32[128,128]{1,0:T(8,128)S(1)}, u32[]{:S(2)}, u32[]{:S(2)}) %collective-permute-start.6) | collective-permute-done | bytes 65568 | tf_op jit(solution)/shard_map/ppermute | solution.py:194
  14.5 1.6 %collective-permute-start.8 = (f32[128,128]{1,0:T(8,128)S(1)}, f32[128,128]{1,0:T(8,128)S(1)}, u32[]{:S(2)}, u32[]{:S(2)}) collective-permute-start(f32[128,128]{1,0:T(8,128)S(1)} %get-tuple-element.26), channel_id=1, source_target_pairs={{0,4},{1,5},{2,6},{3,7},{4,0},{5,1},{6,2},{7,3},{8,12},{9,13},{10,... | collective-permute-start | bytes 196616 | tf_op jit(solution)/shard_map/ppermute | solution.py:194
  16.0 1.3 %collective-permute-start.9 = (f32[128,128]{1,0:T(8,128)S(1)}, f32[128,128]{1,0:T(8,128)S(1)}, u32[]{:S(2)}, u32[]{:S(2)}) collective-permute-start(f32[128,128]{1,0:T(8,128)S(1)} %get-tuple-element.27.refs_4_), channel_id=1, source_target_pairs={{0,3},{1,2},{2,1},{3,0},{4,7},{5,6},{6,5},{7,4},{8,11},{9,10},{10,... | collective-permute-start | bytes 196616 | tf_op jit(solution)/shard_map/ppermute | solution.py:194
  17.3 0.9 %shard_map.57 = (f32[128,1024]{1,0:T(8,128)S(1)}, f32[8,128]{1,0:T(8,128)S(1)}) custom-call(bf16[128,1024]{1,0:T(8,128)(2,1)S(1)} %get-tuple-element.17.refs_0_, bf16[128,1024]{1,0:T(8,128)(2,1)S(1)} %get-tuple-element.18.refs_1_, f32[128,256]{1,0:T(8,128)S(1)} %collective-permute-done.kc_ref.refs_2_, f32[128,256]{1,0:T(8,128)S(1)} %collective-permute-done.1.vc_ref.refs_3_, ...), custom_call_target="tpu_custom_call" | custom-call | flops 1000000 | bytes 100000 | tf_op jit(solution)/shard_map/pallas_call | solution.py:280
  18.3 0.8 %collective-permute-done.7.refs_1_ = f32[128,128]{1,0:T(8,128)S(1)} collective-permute-done((f32[128,128]{1,0:T(8,128)S(1)}, f32[128,128]{1,0:T(8,128)S(1)}, u32[]{:S(2)}, u32[]{:S(2)}) %collective-permute-start.7) | collective-permute-done | bytes 65568 | tf_op jit(solution)/shard_map/ppermute | solution.py:194
  19.1 1.1 %collective-permute-done.8.refs_2_ = f32[128,128]{1,0:T(8,128)S(1)} collective-permute-done((f32[128,128]{1,0:T(8,128)S(1)}, f32[128,128]{1,0:T(8,128)S(1)}, u32[]{:S(2)}, u32[]{:S(2)}) %collective-permute-start.8) | collective-permute-done | bytes 65568 | tf_op jit(solution)/shard_map/ppermute | solution.py:194
  20.3 0.2 collective-permute-start.10
  20.5 0.3 %shard_map.60.refs_5_ = f32[4,128,128]{2,1,0:T(8,128)S(1)} custom-call(f32[128,1024]{1,0:T(8,128)S(1)} %get-tuple-element.21.refs_0_, bf16[128,1024]{1,0:T(8,128)(2,1)S(1)} %get-tuple-element.22.refs_1_, bf16[128,1024]{1,0:T(8,128)(2,1)S(1)} %get-tuple-element.23.refs_2_, f32[1,1024]{1,0:T(1,128)S(1)} %get-tuple-element.24.refs_4_.refs_3_, ...), custom_call_target="tpu_custom_call" | custom-call | flops 1000000000 | bytes 500000 | tf_op jit(solution)/shard_map/pallas_call | solution.py:292
  20.8 0.8 %collective-permute-done.10.refs_4_ = f32[128,128]{1,0:T(8,128)S(1)} collective-permute-done((f32[128,128]{1,0:T(8,128)S(1)}, f32[128,128]{1,0:T(8,128)S(1)}, u32[]{:S(2)}, u32[]{:S(2)}) %collective-permute-start.10) | collective-permute-done | bytes 65568 | tf_op jit(solution)/shard_map/ppermute | solution.py:194
  21.6 1.1 %shard_map.61 = f32[128,1024]{1,0:T(8,128)} custom-call(f32[128,1024]{1,0:T(8,128)S(1)} %get-tuple-element.21.refs_0_, bf16[128,1024]{1,0:T(8,128)(2,1)S(1)} %get-tuple-element.22.refs_1_, bf16[128,1024]{1,0:T(8,128)(2,1)S(1)} %get-tuple-element.23.refs_2_, f32[1,1024]{1,0:T(1,128)S(1)} %get-tuple-element.24.refs_4_.refs_3_, ...), custom_call_target="tpu_custom_call" | custom-call | tf_op jit(solution)/shard_map/pallas_call | solution.py:300
  (12 shorter events, 0.4 us)
Async XLA Ops:
  0.0 1.6 %collective-permute-start = (f32[128,256]{1,0:T(8,128)}, f32[128,256]{1,0:T(8,128)S(1)}, u32[]{:S(2)}, u32[]{:S(2)}) collective-permute-start(f32[128,256]{1,0:T(8,128)} %param.6), channel_id=1, source_target_pairs={{0,1},{1,0},{2,3},{3,2},{4,5},{5,4},{6,7},{7,6},{8,9},{9,8},{10,11... | collective-permute-start | bytes 393224 | tf_op jit(solution)/shard_map/ppermute | solution.py:194
  0.5 1.6 %collective-permute-start.1 = (f32[128,256]{1,0:T(8,128)}, f32[128,256]{1,0:T(8,128)S(1)}, u32[]{:S(2)}, u32[]{:S(2)}) collective-permute-start(f32[128,256]{1,0:T(8,128)} %param.7), channel_id=1, source_target_pairs={{0,1},{1,0},{2,3},{3,2},{4,5},{5,4},{6,7},{7,6},{8,9},{9,8},{10,11... | collective-permute-start | bytes 393224 | tf_op jit(solution)/shard_map/ppermute | solution.py:194
  1.5 7.6 %copy-start = (f32[128,1024]{1,0:T(8,128)S(1)}, f32[128,1024]{1,0:T(8,128)}, u32[]{:S(2)}) copy-start(f32[128,1024]{1,0:T(8,128)} %refs_0_.1) | copy-start | bytes 1572868
  2.3 6.9 %copy-start.1 = (f32[1024]{0:T(1024)S(1)}, f32[1024]{0:T(1024)}, u32[]{:S(2)}) copy-start(f32[1024]{0:T(1024)} %param.9) | copy-start | bytes 12292
  2.3 9.3 %collective-permute-start.2 = (f32[128,512]{1,0:T(8,128)S(1)}, f32[128,512]{1,0:T(8,128)S(1)}, u32[]{:S(2)}, u32[]{:S(2)}) collective-permute-start(f32[128,512]{1,0:T(8,128)S(1)} %get-tuple-element.19.refs_4_), channel_id=1, source_target_pairs={{0,3},{1,2},{2,1},{3,0},{4,7},{5,6},{6,5},{7,4},{8,11},{9,10},{10,... | collective-permute-start | bytes 786440 | tf_op jit(solution)/shard_map/ppermute | solution.py:194
  5.0 7.0 %collective-permute-start.4 = (f32[128,128]{1,0:T(8,128)S(1)}, f32[128,128]{1,0:T(8,128)S(1)}, u32[]{:S(2)}, u32[]{:S(2)}) collective-permute-start(f32[128,128]{1,0:T(8,128)S(1)} %get-tuple-element.25.refs_0_), channel_id=1, source_target_pairs={{0,16},{1,17},{2,18},{3,19},{4,20},{5,21},{6,22},{7,23},{8,24},{9,... | collective-permute-start | bytes 196616 | tf_op jit(solution)/shard_map/ppermute | solution.py:194
  7.6 6.4 %collective-permute-start.5 = (f32[128,128]{1,0:T(8,128)S(1)}, f32[128,128]{1,0:T(8,128)S(1)}, u32[]{:S(2)}, u32[]{:S(2)}) collective-permute-start(f32[128,128]{1,0:T(8,128)S(1)} %get-tuple-element.25.refs_0_), channel_id=1, source_target_pairs={{0,24},{1,25},{2,26},{3,27},{4,28},{5,29},{6,30},{7,31},{8,16},{9,... | collective-permute-start | bytes 196616 | tf_op jit(solution)/shard_map/ppermute | solution.py:194
  8.9 5.4 %collective-permute-start.6 = (f32[128,128]{1,0:T(8,128)S(1)}, f32[128,128]{1,0:T(8,128)S(1)}, u32[]{:S(2)}, u32[]{:S(2)}) collective-permute-start(f32[128,128]{1,0:T(8,128)S(1)} %get-tuple-element.25.refs_0_), channel_id=1, source_target_pairs={{0,8},{1,9},{2,10},{3,11},{4,12},{5,13},{6,14},{7,15},{8,0},{9,1},... | collective-permute-start | bytes 196616 | tf_op jit(solution)/shard_map/ppermute | solution.py:194
  9.1 0.7 %copy-start.2 = (f32[8]{0:T(128)S(1)}, f32[8]{0:T(128)}, u32[]{:S(2)}) copy-start(f32[8]{0:T(128)} %param.8) | copy-start | bytes 100
  11.6 5.8 %collective-permute-start.3 = (f32[128,512]{1,0:T(8,128)S(1)}, f32[128,512]{1,0:T(8,128)S(1)}, u32[]{:S(2)}, u32[]{:S(2)}) collective-permute-start(f32[128,512]{1,0:T(8,128)S(1)} %collective-permute-done.2.refs_6_), channel_id=1, source_target_pairs={{0,1},{1,0},{2,3},{3,2},{4,5},{5,4},{6,7},{7,6},{8,9},{9,8},{10,11... | collective-permute-start | bytes 786440 | tf_op jit(solution)/shard_map/ppermute | solution.py:194
  14.3 4.7 %collective-permute-start.7 = (f32[128,128]{1,0:T(8,128)S(1)}, f32[128,128]{1,0:T(8,128)S(1)}, u32[]{:S(2)}, u32[]{:S(2)}) collective-permute-start(f32[128,128]{1,0:T(8,128)S(1)} %get-tuple-element.26), channel_id=1, source_target_pairs={{0,7},{1,6},{2,5},{3,4},{4,3},{5,2},{6,1},{7,0},{8,15},{9,14},{10,... | collective-permute-start | bytes 196616 | tf_op jit(solution)/shard_map/ppermute | solution.py:194
  14.5 5.7 %collective-permute-start.8 = (f32[128,128]{1,0:T(8,128)S(1)}, f32[128,128]{1,0:T(8,128)S(1)}, u32[]{:S(2)}, u32[]{:S(2)}) collective-permute-start(f32[128,128]{1,0:T(8,128)S(1)} %get-tuple-element.26), channel_id=1, source_target_pairs={{0,4},{1,5},{2,6},{3,7},{4,0},{5,1},{6,2},{7,3},{8,12},{9,13},{10,... | collective-permute-start | bytes 196616 | tf_op jit(solution)/shard_map/ppermute | solution.py:194
  16.0 4.2 %collective-permute-start.9 = (f32[128,128]{1,0:T(8,128)S(1)}, f32[128,128]{1,0:T(8,128)S(1)}, u32[]{:S(2)}, u32[]{:S(2)}) collective-permute-start(f32[128,128]{1,0:T(8,128)S(1)} %get-tuple-element.27.refs_4_), channel_id=1, source_target_pairs={{0,3},{1,2},{2,1},{3,0},{4,7},{5,6},{6,5},{7,4},{8,11},{9,10},{10,... | collective-permute-start | bytes 196616 | tf_op jit(solution)/shard_map/ppermute | solution.py:194
  20.3 1.3 %collective-permute-start.10 = (f32[128,128]{1,0:T(8,128)S(1)}, f32[128,128]{1,0:T(8,128)S(1)}, u32[]{:S(2)}, u32[]{:S(2)}) collective-permute-start(f32[128,128]{1,0:T(8,128)S(1)} %shard_map.59.refs_4_), channel_id=1, source_target_pairs={{0,1},{1,0},{2,3},{3,2},{4,5},{5,4},{6,7},{7,6},{8,9},{9,8},{10,11... | collective-permute-start | bytes 196616 | tf_op jit(solution)/shard_map/ppermute | solution.py:194

commit v9 on v8

--- a/solution.py
+++ b/solution.py
@@ -206,7 +206,7 @@
             flip = flips.get((axis, bit), 0)
             step = (1 << bit, flip) if axis == "seg" else (0, (1 << bit) ^ flip)
             found += [(s ^ step[0], b ^ step[1]) for s, b in found]
-        return [found[i] for i in ((2, 3, 1) if number == 0 and len(found) > 3 else (3, 2, 1) if len(found) == 4 else range(1, len(found)))]
+        return [found[i] for i in ((3, 1, 2) if number == 0 and len(found) > 3 else (3, 2, 1) if len(found) == 4 else range(1, len(found)))]
 
     def on_device(queries, keys, values, gate_logit, memory_gain):
         rows, width = queries.shape

time: 22.8 us -> 22.8 us (level)
  transfers between devices with their start and end apart: 11 -> 11, of which waited for: 9 -> 8; matrix products, arithmetic and copies ran while one was open for 4% -> 4% of each run, Pallas kernels for 7% -> 7%
where the time goes in v9:
time: 22.8 us; the launch traced here: 22.7 us
  starting transfers between devices  11 us (48%)
  waiting for transfers between devices  6.87 us (30%)
  Pallas kernels  3.05 us (13%)
  other arithmetic  0.99 us (4%)
  local copies, waits for them, and re-layouts  0.66 us (3%)
    ppermute x11, starting transfers between devices, swap(): return lax.ppermute(x, both, pairs)  11 us
    ppermute x11, waiting for transfers between devices, swap(): return lax.ppermute(x, both, pairs)  6.87 us
    pallas_call x1, Pallas kernels, on_device(): pl.pallas_call(functools.partial(final_kernel, group, lines), out_specs=p...  1.11 us
    concatenate x1, other arithmetic, on_device(): own = jnp.concatenate([keys, values], 1)  0.99 us
    pallas_call x1, Pallas kernels, on_device(): pl.pallas_call(functools.partial(attention_kernel, group, n_blk), out_sha...  0.9 us
    unnamed x6, local copies, waits for them, and re-layouts  0.66 us
  transfers between devices with their start and end apart: 11, of which 8 were waited for; matrix products, arithmetic and copies ran while one was open for 4% of the time, Pallas kernels for 7%

profile of v9, /device:TPU:0, one launch (start us, length us, event | category | flops | bytes accessed | tf_op | source)
XLA Modules:
  0.0 22.7 jit_solution(2809662449777215096)
XLA Ops:
  0.0 0.5 %collective-permute-start = (f32[128,256]{1,0:T(8,128)}, f32[128,256]{1,0:T(8,128)S(1)}, u32[]{:S(2)}, u32[]{:S(2)}) collective-permute-start(f32[128,256]{1,0:T(8,128)} %param.6), channel_id=1, source_target_pairs={{0,1},{1,0},{2,3},{3,2},{4,5},{5,4},{6,7},{7,6},{8,9},{9,8},{10,11... | collective-permute-start | bytes 393224 | tf_op jit(solution)/shard_map/ppermute | solution.py:194
  0.5 1.0 %pad_maximum_fusion.kv_ref = f32[128,512]{1,0:T(8,128)S(1)} fusion(f32[128,256]{1,0:T(8,128)} %param.7, f32[128,256]{1,0:T(8,128)} %param.6), kind=kLoop, calls=%fused_computation | loop fusion | flops 65536 | bytes 524288 | tf_op jit(solution)/shard_map/concatenate | solution.py:233
  1.5 0.1 collective-permute-done.kc_ref.refs_2_
  1.7 0.4 %collective-permute-done.1.vc_ref.refs_3_ = f32[128,256]{1,0:T(8,128)S(1)} collective-permute-done((f32[128,256]{1,0:T(8,128)}, f32[128,256]{1,0:T(8,128)S(1)}, u32[]{:S(2)}, u32[]{:S(2)}) %collective-permute-start.1) | collective-permute-done | bytes 131104 | tf_op jit(solution)/shard_map/ppermute | solution.py:194
  2.0 0.3 %shard_map.56 = (f32[128,128]{1,0:T(8,128)S(1)}, f32[128,512]{1,0:T(8,128)S(1)}) custom-call(f32[128,256]{1,0:T(8,128)S(1)} %collective-permute-done.kc_ref.refs_2_, f32[128,256]{1,0:T(8,128)S(1)} %collective-permute-done.1.vc_ref.refs_3_, f32[128,512]{1,0:T(8,128)S(1)} %pad_maximum_fusion.kv_ref), custom_call_target="tpu_custom_call", output_to_operand_aliasing={{1}: (2, {})} | custom-call | flops 500000000 | bytes 500000 | tf_op jit(solution)/shard_map/pallas_call | solution.py:219
  2.3 2.7 %collective-permute-start.2 = (f32[128,512]{1,0:T(8,128)S(1)}, f32[128,512]{1,0:T(8,128)S(1)}, u32[]{:S(2)}, u32[]{:S(2)}) collective-permute-start(f32[128,512]{1,0:T(8,128)S(1)} %get-tuple-element.19.refs_4_), channel_id=1, source_target_pairs={{0,3},{1,2},{2,1},{3,0},{4,7},{5,6},{6,5},{7,4},{8,11},{9,10},{10,... | collective-permute-start | bytes 786440 | tf_op jit(solution)/shard_map/ppermute | solution.py:194
  5.0 3.6 %collective-permute-start.4 = (f32[128,128]{1,0:T(8,128)S(1)}, f32[128,128]{1,0:T(8,128)S(1)}, u32[]{:S(2)}, u32[]{:S(2)}) collective-permute-start(f32[128,128]{1,0:T(8,128)S(1)} %get-tuple-element.25.refs_0_), channel_id=1, source_target_pairs={{0,24},{1,25},{2,26},{3,27},{4,28},{5,29},{6,30},{7,31},{8,16},{9,... | collective-permute-start | bytes 196616 | tf_op jit(solution)/shard_map/ppermute | solution.py:194
  8.6 0.8 %collective-permute-start.6 = (f32[128,128]{1,0:T(8,128)S(1)}, f32[128,128]{1,0:T(8,128)S(1)}, u32[]{:S(2)}, u32[]{:S(2)}) collective-permute-start(f32[128,128]{1,0:T(8,128)S(1)} %get-tuple-element.25.refs_0_), channel_id=1, source_target_pairs={{0,16},{1,17},{2,18},{3,19},{4,20},{5,21},{6,22},{7,23},{8,24},{9,... | collective-permute-start | bytes 196616 | tf_op jit(solution)/shard_map/ppermute | solution.py:194
  9.4 0.6 %copy-done.2 = f32[8]{0:T(128)S(1)} copy-done((f32[8]{0:T(128)S(1)}, f32[8]{0:T(128)}, u32[]{:S(2)}) %copy-start.2) | copy-done | bytes 56
  10.0 0.4 %shard_map.55 = (bf16[128,1024]{1,0:T(8,128)(2,1)S(1)}, bf16[128,1024]{1,0:T(8,128)(2,1)S(1)}, bf16[128,1024]{1,0:T(8,128)(2,1)S(1)}, bf16[128,1024]{1,0:T(8,128...) custom-call(f32[128,1024]{1,0:T(8,128)S(1)} %copy-done, f32[1,8]{1,0:T(1,128)S(1)} %bitcast.3, f32[1,1024]{1,0:T(1,128)S(1)} %bitcast.2), custom_call_target="tpu_custom_call" | custom-call | flops 1000000 | bytes 100000 | tf_op jit(solution)/shard_map/pallas_call | solution.py:242
  10.4 1.2 %collective-permute-done.2.refs_6_ = f32[128,512]{1,0:T(8,128)S(1)} collective-permute-done((f32[128,512]{1,0:T(8,128)S(1)}, f32[128,512]{1,0:T(8,128)S(1)}, u32[]{:S(2)}, u32[]{:S(2)}) %collective-permute-start.2) | collective-permute-done | bytes 262176 | tf_op jit(solution)/shard_map/ppermute | solution.py:194
  11.6 0.2 %collective-permute-start.3 = (f32[128,512]{1,0:T(8,128)S(1)}, f32[128,512]{1,0:T(8,128)S(1)}, u32[]{:S(2)}, u32[]{:S(2)}) collective-permute-start(f32[128,512]{1,0:T(8,128)S(1)} %collective-permute-done.2.refs_6_), channel_id=1, source_target_pairs={{0,1},{1,0},{2,3},{3,2},{4,5},{5,4},{6,7},{7,6},{8,9},{9,8},{10,11... | collective-permute-start | bytes 786440 | tf_op jit(solution)/shard_map/ppermute | solution.py:194
  11.8 1.9 %collective-permute-done.5.refs_2_ = f32[128,128]{1,0:T(8,128)S(1)} collective-permute-done((f32[128,128]{1,0:T(8,128)S(1)}, f32[128,128]{1,0:T(8,128)S(1)}, u32[]{:S(2)}, u32[]{:S(2)}) %collective-permute-start.5) | collective-permute-done | bytes 65568 | tf_op jit(solution)/shard_map/ppermute | solution.py:194
  13.7 0.7 %collective-permute-done.6.refs_3_ = f32[128,128]{1,0:T(8,128)S(1)} collective-permute-done((f32[128,128]{1,0:T(8,128)S(1)}, f32[128,128]{1,0:T(8,128)S(1)}, u32[]{:S(2)}, u32[]{:S(2)}) %collective-permute-start.6) | collective-permute-done | bytes 65568 | tf_op jit(solution)/shard_map/ppermute | solution.py:194
  14.5 0.1 collective-permute-start.7
  14.6 1.6 %collective-permute-start.8 = (f32[128,128]{1,0:T(8,128)S(1)}, f32[128,128]{1,0:T(8,128)S(1)}, u32[]{:S(2)}, u32[]{:S(2)}) collective-permute-start(f32[128,128]{1,0:T(8,128)S(1)} %get-tuple-element.26), channel_id=1, source_target_pairs={{0,4},{1,5},{2,6},{3,7},{4,0},{5,1},{6,2},{7,3},{8,12},{9,13},{10,... | collective-permute-start | bytes 196616 | tf_op jit(solution)/shard_map/ppermute | solution.py:194
  16.1 1.3 %collective-permute-start.9 = (f32[128,128]{1,0:T(8,128)S(1)}, f32[128,128]{1,0:T(8,128)S(1)}, u32[]{:S(2)}, u32[]{:S(2)}) collective-permute-start(f32[128,128]{1,0:T(8,128)S(1)} %get-tuple-element.27.refs_4_), channel_id=1, source_target_pairs={{0,3},{1,2},{2,1},{3,0},{4,7},{5,6},{6,5},{7,4},{8,11},{9,10},{10,... | collective-permute-start | bytes 196616 | tf_op jit(solution)/shard_map/ppermute | solution.py:194
  17.5 0.9 %shard_map.57 = (f32[128,1024]{1,0:T(8,128)S(1)}, f32[8,128]{1,0:T(8,128)S(1)}) custom-call(bf16[128,1024]{1,0:T(8,128)(2,1)S(1)} %get-tuple-element.17.refs_0_, bf16[128,1024]{1,0:T(8,128)(2,1)S(1)} %get-tuple-element.18.refs_1_, f32[128,256]{1,0:T(8,128)S(1)} %collective-permute-done.kc_ref.refs_2_, f32[128,256]{1,0:T(8,128)S(1)} %collective-permute-done.1.vc_ref.refs_3_, ...), custom_call_target="tpu_custom_call" | custom-call | flops 1000000 | bytes 100000 | tf_op jit(solution)/shard_map/pallas_call | solution.py:280
  18.4 0.8 %collective-permute-done.7.refs_1_ = f32[128,128]{1,0:T(8,128)S(1)} collective-permute-done((f32[128,128]{1,0:T(8,128)S(1)}, f32[128,128]{1,0:T(8,128)S(1)}, u32[]{:S(2)}, u32[]{:S(2)}) %collective-permute-start.7) | collective-permute-done | bytes 65568 | tf_op jit(solution)/shard_map/ppermute | solution.py:194
  19.2 1.0 %collective-permute-done.8.refs_2_ = f32[128,128]{1,0:T(8,128)S(1)} collective-permute-done((f32[128,128]{1,0:T(8,128)S(1)}, f32[128,128]{1,0:T(8,128)S(1)}, u32[]{:S(2)}, u32[]{:S(2)}) %collective-permute-start.8) | collective-permute-done | bytes 65568 | tf_op jit(solution)/shard_map/ppermute | solution.py:194
  20.3 0.2 %collective-permute-start.10 = (f32[128,128]{1,0:T(8,128)S(1)}, f32[128,128]{1,0:T(8,128)S(1)}, u32[]{:S(2)}, u32[]{:S(2)}) collective-permute-start(f32[128,128]{1,0:T(8,128)S(1)} %shard_map.59.refs_4_), channel_id=1, source_target_pairs={{0,1},{1,0},{2,3},{3,2},{4,5},{5,4},{6,7},{7,6},{8,9},{9,8},{10,11... | collective-permute-start | bytes 196616 | tf_op jit(solution)/shard_map/ppermute | solution.py:194
  20.5 0.3 %shard_map.60.refs_5_ = f32[4,128,128]{2,1,0:T(8,128)S(1)} custom-call(f32[128,1024]{1,0:T(8,128)S(1)} %get-tuple-element.21.refs_0_, bf16[128,1024]{1,0:T(8,128)(2,1)S(1)} %get-tuple-element.22.refs_1_, bf16[128,1024]{1,0:T(8,128)(2,1)S(1)} %get-tuple-element.23.refs_2_, f32[1,1024]{1,0:T(1,128)S(1)} %get-tuple-element.24.refs_4_.refs_3_, ...), custom_call_target="tpu_custom_call" | custom-call | flops 1000000000 | bytes 500000 | tf_op jit(solution)/shard_map/pallas_call | solution.py:292
  20.9 0.7 %collective-permute-done.10.refs_4_ = f32[128,128]{1,0:T(8,128)S(1)} collective-permute-done((f32[128,128]{1,0:T(8,128)S(1)}, f32[128,128]{1,0:T(8,128)S(1)}, u32[]{:S(2)}, u32[]{:S(2)}) %collective-permute-start.10) | collective-permute-done | bytes 65568 | tf_op jit(solution)/shard_map/ppermute | solution.py:194
  21.6 1.1 %shard_map.61 = f32[128,1024]{1,0:T(8,128)} custom-call(f32[128,1024]{1,0:T(8,128)S(1)} %get-tuple-element.21.refs_0_, bf16[128,1024]{1,0:T(8,128)(2,1)S(1)} %get-tuple-element.22.refs_1_, bf16[128,1024]{1,0:T(8,128)(2,1)S(1)} %get-tuple-element.23.refs_2_, f32[1,1024]{1,0:T(1,128)S(1)} %get-tuple-element.24.refs_4_.refs_3_, ...), custom_call_target="tpu_custom_call" | custom-call | tf_op jit(solution)/shard_map/pallas_call | solution.py:300
  (12 shorter events, 0.2 us)
Async XLA Ops:
  0.0 1.6 %collective-permute-start = (f32[128,256]{1,0:T(8,128)}, f32[128,256]{1,0:T(8,128)S(1)}, u32[]{:S(2)}, u32[]{:S(2)}) collective-permute-start(f32[128,256]{1,0:T(8,128)} %param.6), channel_id=1, source_target_pairs={{0,1},{1,0},{2,3},{3,2},{4,5},{5,4},{6,7},{7,6},{8,9},{9,8},{10,11... | collective-permute-start | bytes 393224 | tf_op jit(solution)/shard_map/ppermute | solution.py:194
  0.5 1.6 %collective-permute-start.1 = (f32[128,256]{1,0:T(8,128)}, f32[128,256]{1,0:T(8,128)S(1)}, u32[]{:S(2)}, u32[]{:S(2)}) collective-permute-start(f32[128,256]{1,0:T(8,128)} %param.7), channel_id=1, source_target_pairs={{0,1},{1,0},{2,3},{3,2},{4,5},{5,4},{6,7},{7,6},{8,9},{9,8},{10,11... | collective-permute-start | bytes 393224 | tf_op jit(solution)/shard_map/ppermute | solution.py:194
  1.5 7.9 %copy-start = (f32[128,1024]{1,0:T(8,128)S(1)}, f32[128,1024]{1,0:T(8,128)}, u32[]{:S(2)}) copy-start(f32[128,1024]{1,0:T(8,128)} %refs_0_.1) | copy-start | bytes 1572868
  2.3 7.1 %copy-start.1 = (f32[1024]{0:T(1024)S(1)}, f32[1024]{0:T(1024)}, u32[]{:S(2)}) copy-start(f32[1024]{0:T(1024)} %param.9) | copy-start | bytes 12292
  2.3 9.3 %collective-permute-start.2 = (f32[128,512]{1,0:T(8,128)S(1)}, f32[128,512]{1,0:T(8,128)S(1)}, u32[]{:S(2)}, u32[]{:S(2)}) collective-permute-start(f32[128,512]{1,0:T(8,128)S(1)} %get-tuple-element.19.refs_4_), channel_id=1, source_target_pairs={{0,3},{1,2},{2,1},{3,0},{4,7},{5,6},{6,5},{7,4},{8,11},{9,10},{10,... | collective-permute-start | bytes 786440 | tf_op jit(solution)/shard_map/ppermute | solution.py:194
  5.0 6.8 %collective-permute-start.4 = (f32[128,128]{1,0:T(8,128)S(1)}, f32[128,128]{1,0:T(8,128)S(1)}, u32[]{:S(2)}, u32[]{:S(2)}) collective-permute-start(f32[128,128]{1,0:T(8,128)S(1)} %get-tuple-element.25.refs_0_), channel_id=1, source_target_pairs={{0,24},{1,25},{2,26},{3,27},{4,28},{5,29},{6,30},{7,31},{8,16},{9,... | collective-permute-start | bytes 196616 | tf_op jit(solution)/shard_map/ppermute | solution.py:194
  8.6 5.1 %collective-permute-start.5 = (f32[128,128]{1,0:T(8,128)S(1)}, f32[128,128]{1,0:T(8,128)S(1)}, u32[]{:S(2)}, u32[]{:S(2)}) collective-permute-start(f32[128,128]{1,0:T(8,128)S(1)} %get-tuple-element.25.refs_0_), channel_id=1, source_target_pairs={{0,8},{1,9},{2,10},{3,11},{4,12},{5,13},{6,14},{7,15},{8,0},{9,1},... | collective-permute-start | bytes 196616 | tf_op jit(solution)/shard_map/ppermute | solution.py:194
  8.6 5.9 %collective-permute-start.6 = (f32[128,128]{1,0:T(8,128)S(1)}, f32[128,128]{1,0:T(8,128)S(1)}, u32[]{:S(2)}, u32[]{:S(2)}) collective-permute-start(f32[128,128]{1,0:T(8,128)S(1)} %get-tuple-element.25.refs_0_), channel_id=1, source_target_pairs={{0,16},{1,17},{2,18},{3,19},{4,20},{5,21},{6,22},{7,23},{8,24},{9,... | collective-permute-start | bytes 196616 | tf_op jit(solution)/shard_map/ppermute | solution.py:194
  9.4 0.7 %copy-start.2 = (f32[8]{0:T(128)S(1)}, f32[8]{0:T(128)}, u32[]{:S(2)}) copy-start(f32[8]{0:T(128)} %param.8) | copy-start | bytes 100
  11.6 5.9 %collective-permute-start.3 = (f32[128,512]{1,0:T(8,128)S(1)}, f32[128,512]{1,0:T(8,128)S(1)}, u32[]{:S(2)}, u32[]{:S(2)}) collective-permute-start(f32[128,512]{1,0:T(8,128)S(1)} %collective-permute-done.2.refs_6_), channel_id=1, source_target_pairs={{0,1},{1,0},{2,3},{3,2},{4,5},{5,4},{6,7},{7,6},{8,9},{9,8},{10,11... | collective-permute-start | bytes 786440 | tf_op jit(solution)/shard_map/ppermute | solution.py:194
  14.5 4.7 %collective-permute-start.7 = (f32[128,128]{1,0:T(8,128)S(1)}, f32[128,128]{1,0:T(8,128)S(1)}, u32[]{:S(2)}, u32[]{:S(2)}) collective-permute-start(f32[128,128]{1,0:T(8,128)S(1)} %get-tuple-element.26), channel_id=1, source_target_pairs={{0,7},{1,6},{2,5},{3,4},{4,3},{5,2},{6,1},{7,0},{8,15},{9,14},{10,... | collective-permute-start | bytes 196616 | tf_op jit(solution)/shard_map/ppermute | solution.py:194
  14.6 5.6 %collective-permute-start.8 = (f32[128,128]{1,0:T(8,128)S(1)}, f32[128,128]{1,0:T(8,128)S(1)}, u32[]{:S(2)}, u32[]{:S(2)}) collective-permute-start(f32[128,128]{1,0:T(8,128)S(1)} %get-tuple-element.26), channel_id=1, source_target_pairs={{0,4},{1,5},{2,6},{3,7},{4,0},{5,1},{6,2},{7,3},{8,12},{9,13},{10,... | collective-permute-start | bytes 196616 | tf_op jit(solution)/shard_map/ppermute | solution.py:194
  16.1 4.1 %collective-permute-start.9 = (f32[128,128]{1,0:T(8,128)S(1)}, f32[128,128]{1,0:T(8,128)S(1)}, u32[]{:S(2)}, u32[]{:S(2)}) collective-permute-start(f32[128,128]{1,0:T(8,128)S(1)} %get-tuple-element.27.refs_4_), channel_id=1, source_target_pairs={{0,3},{1,2},{2,1},{3,0},{4,7},{5,6},{6,5},{7,4},{8,11},{9,10},{10,... | collective-permute-start | bytes 196616 | tf_op jit(solution)/shard_map/ppermute | solution.py:194
  20.3 1.3 %collective-permute-start.10 = (f32[128,128]{1,0:T(8,128)S(1)}, f32[128,128]{1,0:T(8,128)S(1)}, u32[]{:S(2)}, u32[]{:S(2)}) collective-permute-start(f32[128,128]{1,0:T(8,128)S(1)} %shard_map.59.refs_4_), channel_id=1, source_target_pairs={{0,1},{1,0},{2,3},{3,2},{4,5},{5,4},{6,7},{7,6},{8,9},{9,8},{10,11... | collective-permute-start | bytes 196616 | tf_op jit(solution)/shard_map/ppermute | solution.py:194
